TPU v7x, 512 devices: a whole 4x8x8 slice. The times are simulated.
512 devices in a mesh: dp: 16 (over x_hi, z), tensor: 32 (over x_lo, y, core).
Axes of the slice: x: 4 (x_hi: 2, x_lo: 2; x = x_hi * 2 + x_lo), y: 8, z: 8, core: 2. Of those that a mesh axis runs over, the one named last changes fastest.
Arguments:
- tokens: bfloat16 [8192, 8192], P('dp', 'tensor'), may hold values from -6 to 6
- query_weight: bfloat16 [8192, 8192], P(None, 'tensor'), may hold values from -0.0625 to 0.0625
- adapter_down_weight: bfloat16 [64, 64, 8192], P('dp', None, 'tensor'), may hold values from -0.0625 to 0.0625
- adapter_up_weight: bfloat16 [64, 64, 8192], P('dp', None, 'tensor'), may hold values from -0.75 to 0.75
- segment_request: int32 [64], P('dp'), may hold values from 0 to 31, as said below
- request_adapter_ids: int32 [32], P('dp'), may hold values from 0 to 63
- adapter_stored_row: int32 [64], replicated, may hold values from 0 to 63, each once
Outputs:
- query: bfloat16 [8192, 8192], P('dp', 'tensor')
Inputs may be any that keep to these rules, and one draw needn't show every extreme that they name: `segment_request`: segments of one request are consecutive; every request has one or more segments; the segments of dp index g name requests g * 2 to (g + 1) * 2 - 1.
All inputs are finite; a program needn't handle non-finite values.
Results may differ from a plain program's by a relative error of at most 0.0046.
Values may be sent and summed in bfloat16 or wider, within the bound.
No kernel may reach another device: no remote copies, remote signals or barrier semaphores. Data moves between devices by JAX's collectives and lax.ppermute only.
A program may use at most 64 MiB of HBM per device.

v0:
```python
import jax
import jax.numpy as jnp
from jax import lax
from jax.sharding import PartitionSpec as P

adapter_scale = 2.0


def body(
    tokens,
    query_weight,
    adapter_down_weight,
    adapter_up_weight,
    segment_request,
    request_adapter_ids,
    adapter_stored_row,
):
    segment_row_count, feat_width = tokens.shape
    base_output = jnp.dot(
        lax.all_gather(tokens, "tensor", axis=1, tiled=True),
        query_weight,
        preferred_element_type=jnp.float32,
    )
    group_index = lax.axis_index("dp")
    request_count = request_adapter_ids.shape[0]
    table_size = adapter_stored_row.shape[0]
    local_request = segment_request - group_index * request_count
    slot_hits = (
        request_adapter_ids[:, None] == jnp.arange(table_size, dtype=jnp.int32)[None, :]
    ).astype(jnp.int32)
    request_rows = jnp.sum(slot_hits * adapter_stored_row[None, :], axis=1)
    every_shrink, every_expand = (
        lax.all_gather(adapter_down_weight, "dp", axis=0, tiled=True),
        lax.all_gather(adapter_up_weight, "dp", axis=0, tiled=True),
    )
    storage_rows = request_rows[local_request]
    shrink_mats = every_shrink[storage_rows]
    expand_mats = every_expand[storage_rows]
    segment_count = segment_request.shape[0]
    segment_rows = tokens.reshape(segment_count, segment_row_count // segment_count, feat_width)
    partial_value = jnp.einsum(
        "ksd,krd->ksr", segment_rows, shrink_mats, preferred_element_type=jnp.float32
    )
    partial_value = partial_value.reshape(segment_row_count, -1)
    lowrank = lax.psum(partial_value, "tensor").astype(jnp.bfloat16)
    lowrank = lowrank.reshape(segment_count, segment_row_count // segment_count, -1)
    adapter_output = jnp.einsum(
        "ksr,krc->ksc", lowrank, expand_mats, preferred_element_type=jnp.float32
    )
    return (base_output + adapter_scale * adapter_output.reshape(segment_row_count, -1)).astype(
        jnp.bfloat16
    )


def solution(mesh):
    in_specs = (
        P("dp", "tensor"),
        P(None, "tensor"),
        P("dp", None, "tensor"),
        P("dp", None, "tensor"),
        P("dp"),
        P("dp"),
        P(),
    )
    out_specs = P("dp", "tensor")
    return jax.shard_map(body, mesh=mesh, in_specs=in_specs, out_specs=out_specs, check_vma=False)
```

profile of v0, /device:TPU:1, one launch (start us, length us, event | category | flops | bytes accessed | tf_op | source)
XLA Modules:
  0.0 317.7 jit_solution(7768300726051326789)
XLA Ops:
  6.5 0.0 all-gather.6.cloned.1.call-start
  6.5 0.7 all-gather.6.cloned.1.call-update
  7.3 0.0 all-gather.8.cloned.1.call-start
  7.3 0.7 all-gather.8.cloned.1.call-update
  8.0 0.0 all-gather.4.cloned.1.call-start
  8.1 0.7 all-gather.4.cloned.1.call-update
  8.7 0.7 compare_select_fusion.1
  9.4 0.9 fusion.3
  10.3 0.6 gather_fusion
  10.9 93.3 %all-gather.6.cloned.1.call-done = bf16[64,64,256]{2,1,0:T(8,128)(2,1)} async-done(((bf16[4,64,256]{2,1,0:T(8,128)(2,1)}), bf16[64,64,256]{2,1,0:T(8,128)(2,1)}) %all-gather.6.cloned.1.call-update) | async-done | bytes 2097168 | tf_op jit(solution)/shard_map/all_gather | solution.py:33
  104.2 2.1 gather_fusion.1
  106.4 1.2 convolution_bitcast_fusion
  107.5 87.9 %all-gather.8.cloned.1.call-done = bf16[64,64,256]{2,1,0:T(8,128)(2,1)} async-done(((bf16[4,64,256]{2,1,0:T(8,128)(2,1)}), bf16[64,64,256]{2,1,0:T(8,128)(2,1)}) %all-gather.8.cloned.1.call-update) | async-done | bytes 2097168 | tf_op jit(solution)/shard_map/all_gather | solution.py:34
  195.4 2.1 gather_fusion.2
  197.6 105.6 %all-reduce.1 = bf16[512,64]{0,1:T(8,128)(2,1)S(1)} all-reduce(f32[512,64]{0,1:T(8,128)S(1)} %bitcast.28), channel_id=1, replica_groups=mesh['dp'=16,'tensor'=32] {'tensor'}, use_global_device_ids=true, to_apply=%region_1.0 | all-reduce | flops 32768 | bytes 196608 | tf_op jit(solution)/shard_map/psum | solution.py:45
  303.2 0.3 convolution_multiply_fusion
  303.5 0.0 all-gather.4.cloned.1.call-done
  303.5 7.6 %fusion = bf16[512,256]{1,0:T(8,128)(2,1)} fusion(f32[512,256]{1,0:T(8,128)S(1)} %bitcast.27, bf16[512,8192]{1,0:T(8,128)(2,1)} %all-gather.4.cloned.1.call-done, bf16[8192,256]{1,0:T(8,128)(2,1)} %param.8), kind=kOutput, calls=%fused_computation.5 | convolution fusion | flops 2147745792 | bytes 13369344 | tf_op jit(solution)/shard_map/dot_general | solution.py:19
  (4 shorter events, 0.0 us)
Async XLA Ops:
  6.5 97.7 %all-gather.6.cloned.1.call-start = ((), (), s32[]{:S(2)}) async-start(), calls=%async_computation.1 | async-start | bytes 2228224 | tf_op jit(solution)/shard_map/all_gather | solution.py:33
  7.3 188.2 %all-gather.8.cloned.1.call-start = ((), (), s32[]{:S(2)}) async-start(), calls=%async_computation.2 | async-start | bytes 2228224 | tf_op jit(solution)/shard_map/all_gather | solution.py:34
  8.0 295.5 %all-gather.4.cloned.1.call-start = ((), (), s32[]{:S(2)}) async-start(), calls=%async_computation | async-start | bytes 8650752 | tf_op jit(solution)/shard_map/all_gather | solution.py:20
Sparse Core Ops, SparseCore 0:
  10.5 93.6 all-gather.5
  107.4 88.0 all-gather.7
  197.5 93.8 all-gather.3
where the time goes:
time: 320 us; the launch traced here: 318 us
  waiting for transfers between devices  183 us (57%)
  blocking collectives  106 us (33%)
  between operations  13.2 us (4%)
  matrix products  9.03 us (3%)
  local copies, waits for them, and re-layouts  4.94 us (2%)
    psum x1, blocking collectives, body(): lowrank = lax.psum(partial_value, 'tensor').astype(jnp.bfloat16)  106 us
    all_gather x1, waiting for transfers between devices, body(): lax.all_gather(adapter_down_weight, 'dp', axis=0, tiled=True)  93.3 us
    all_gather x1, waiting for transfers between devices, body(): lax.all_gather(adapter_up_weight, 'dp', axis=0, tiled=True)  87.9 us
    dot_general x1, matrix products, body(): jnp.dot(lax.all_gather(tokens, 'tensor', axis=1, tiled=True), query_weigh...  7.61 us
  transfers between devices with their start and end apart: 3, of which 2 were waited for; matrix products, arithmetic and copies ran while one was open for 2% of the time, Pallas kernels for 0%

commit v1 on v0

v1 whole, which is shorter than its diff:
```python
import jax
import jax.numpy as jnp
from jax import lax
from jax.experimental import pallas as pl
from jax.experimental.pallas import tpu as pltpu
from jax.sharding import Mesh, PartitionSpec as P

SWAP = [(0, 1), (1, 0)]
DP = ("xh", "z")
TENSOR = ("xl", "y", "c")
ROWS = 512
SEG = 128
RANK = 64
WIDTH = 256
OWNED = 4


def select_kernel(rows_ref, me_ref, mats_ref, out_ref):
    first = me_ref[0] * OWNED

    def step(i, carry):
        slot = jnp.clip(rows_ref[i] - first, 0, OWNED - 1)
        out_ref[i] = mats_ref[slot]
        return carry

    lax.fori_loop(0, out_ref.shape[0], step, 0)


def select(rows, me, mats):
    count = rows.shape[0]
    return pl.pallas_call(
        select_kernel,
        out_shape=jax.ShapeDtypeStruct((count,) + mats.shape[1:], mats.dtype),
        in_specs=[
            pl.BlockSpec(memory_space=pltpu.SMEM),
            pl.BlockSpec(memory_space=pltpu.SMEM),
            pl.BlockSpec(memory_space=pltpu.VMEM),
        ],
        out_specs=pl.BlockSpec(memory_space=pltpu.VMEM),
        cost_estimate=pl.CostEstimate(flops=0, bytes_accessed=2 << 20, transcendentals=0),
    )(rows, me, mats)


def down_kernel(pick_ref, tokens_ref, mats_ref, out_ref):
    for k in range(4):
        mat = mats_ref[pick_ref[k]]
        part = lax.dot_general(
            tokens_ref[k * SEG : (k + 1) * SEG, :],
            mat,
            (((1,), (1,)), ((), ())),
            preferred_element_type=jnp.float32,
        )
        row, col = (k % 2) * SEG, (k // 2) * RANK
        out_ref[row : row + SEG, col : col + RANK] = part


def down_product(pick, tokens, mats):
    return pl.pallas_call(
        down_kernel,
        out_shape=jax.ShapeDtypeStruct((256, 128), jnp.float32),
        in_specs=[
            pl.BlockSpec(memory_space=pltpu.SMEM),
            pl.BlockSpec(memory_space=pltpu.VMEM),
            pl.BlockSpec(memory_space=pltpu.VMEM),
        ],
        out_specs=pl.BlockSpec(memory_space=pltpu.VMEM),
        cost_estimate=pl.CostEstimate(flops=1 << 24, bytes_accessed=1 << 20, transcendentals=0),
    )(pick, tokens, mats)


def main_kernel(pick_ref, low_ref, mats_ref, t_ref, w_ref, out_ref, acc_ref):
    step = pl.program_id(0)
    part = jnp.dot(t_ref[...], w_ref[...], preferred_element_type=jnp.float32)

    @pl.when(step == 0)
    def _():
        for k in range(4):
            row, col = (k % 2) * SEG, (k // 2) * RANK
            low = low_ref[row : row + SEG, col : col + RANK].astype(jnp.bfloat16)
            up = jnp.dot(low, mats_ref[pick_ref[k]], preferred_element_type=jnp.float32)
            acc_ref[k * SEG : (k + 1) * SEG, :] = 2.0 * up
        acc_ref[...] += part

    @pl.when(step > 0)
    def _():
        acc_ref[...] += part

    @pl.when(step == pl.num_programs(0) - 1)
    def _():
        out_ref[...] = acc_ref[...].astype(jnp.bfloat16)


def main_product(pick, low, mats, gathered, weight, own_half):
    depth = 1024
    per_half = 4096 // depth

    def t_index(i, pick):
        return (i // per_half, i % per_half)

    def w_index(i, pick):
        half = jnp.where(i < per_half, pick[4], 1 - pick[4])
        return (half * per_half + i % per_half, 0)

    grid_spec = pltpu.PrefetchScalarGridSpec(
        num_scalar_prefetch=1,
        grid=(2 * per_half,),
        in_specs=[
            pl.BlockSpec((256, 128), lambda i, pick: (0, 0)),
            pl.BlockSpec(mats.shape, lambda i, pick: (0, 0, 0)),
            pl.BlockSpec((ROWS, depth), t_index),
            pl.BlockSpec((depth, WIDTH), w_index),
        ],
        out_specs=pl.BlockSpec((ROWS, WIDTH), lambda i, pick: (0, 0)),
        scratch_shapes=[pltpu.VMEM((ROWS, WIDTH), jnp.float32)],
    )
    return pl.pallas_call(
        main_kernel,
        out_shape=jax.ShapeDtypeStruct((ROWS, WIDTH), jnp.bfloat16),
        grid_spec=grid_spec,
        compiler_params=pltpu.CompilerParams(vmem_limit_bytes=40 << 20),
        cost_estimate=pl.CostEstimate(
            flops=2 * ROWS * 8192 * WIDTH, bytes_accessed=12 << 20, transcendentals=0
        ),
    )(jnp.concatenate([pick, own_half[None]]), low, mats, gathered, weight)


def body(tokens, weight, down, up, segment_request, request_ids, stored_row):
    dp = lax.axis_index(DP).astype(jnp.int32)
    half = lax.axis_index("xl").astype(jnp.int32)

    other = lax.ppermute(tokens, "xl", SWAP)
    gathered = lax.all_gather(
        jnp.concatenate([tokens, other], axis=0), ("y", "c"), axis=1, tiled=True
    )

    hits = request_ids[:, None] == jnp.arange(stored_row.shape[0], dtype=jnp.int32)[None, :]
    rows = jnp.sum(jnp.where(hits, stored_row[None, :], 0), axis=1).astype(jnp.int32)
    every_row = lax.all_to_all(
        jnp.broadcast_to(rows[None, None, :], (16, 1, 2)), DP, 0, 0
    ).reshape(32)
    request = segment_request - dp * 2
    owner_slot = (rows // OWNED) * 2 + jnp.arange(2, dtype=jnp.int32)
    pick = jnp.where(request == 0, owner_slot[0], owner_slot[1]).astype(jnp.int32)

    me = dp[None]
    sent_down = select(every_row, me, down)
    sent_up = select(every_row, me, up)
    got_down = lax.all_to_all(sent_down.reshape(16, 2, RANK, WIDTH), DP, 0, 0)
    got_up = lax.all_to_all(sent_up.reshape(16, 2, RANK, WIDTH), DP, 0, 0)

    partial = down_product(pick, tokens, got_down.reshape(32, RANK, WIDTH))
    parts = lax.all_to_all(partial.reshape(32, 8, 128), TENSOR, 0, 0)
    total = jnp.sum(parts, axis=0)
    low = lax.all_to_all(jnp.broadcast_to(total[None], (32, 8, 128)), TENSOR, 0, 0)
    return main_product(
        pick, low.reshape(256, 128), got_up.reshape(32, RANK, WIDTH), gathered, weight, half
    )


def solution(mesh):
    fine = Mesh(mesh.devices.reshape(2, 8, 2, 8, 2), ("xh", "z", "xl", "y", "c"))
    in_specs = (
        P(DP, TENSOR),
        P(None, TENSOR),
        P(DP, None, TENSOR),
        P(DP, None, TENSOR),
        P(DP),
        P(DP),
        P(),
    )
    return jax.shard_map(body, mesh=fine, in_specs=in_specs, out_specs=P(DP, TENSOR), check_vma=False)
```

time: 320 us -> 165 us (0.52)
  waiting for transfers between devices: 183 us -> 74.3 us
  blocking collectives: 106 us -> 0 us
  starting transfers between devices: 0.08 us -> 47.7 us
  Pallas kernels: 0 us -> 13 us
  matrix products: 9.03 us -> 0 us
  other arithmetic: 1.54 us -> 6.57 us
  local copies, waits for them, and re-layouts: 4.94 us -> 9.68 us
    all_gather x3 -> x1, waiting for transfers between devices: 181 us -> 0.01 us  [body(): lax.all_gather(jnp.concatenate([tokens, other], axis=0), ('y', 'c'), axis...]
    psum x1 -> x0, blocking collectives: 106 us -> none  [body(): lowrank = lax.psum(partial_value, 'tensor').astype(jnp.bfloat16)]
    all_to_all x0 -> x5, waiting for transfers between devices: none -> 70.3 us  [the longest x1 25.7 us: body(): got_up = lax.all_to_all(sent_up.reshape(16, 2, RANK, WIDTH), DP, 0, 0)]
    all_to_all x0 -> x5, starting transfers between devices: none -> 43.7 us  [the longest x1 14.8 us: body(): lax.all_to_all(jnp.broadcast_to(rows[None, None, :], (16, 1, 2)), DP, 0, 0)]
    pallas_call x0 -> x4, Pallas kernels: none -> 13 us  [the longest x1 6.19 us: main_product(): pl.pallas_call(main_kernel, out_shape=jax.ShapeDtypeStruct((ROWS, WIDTH),...]
    dot_general x3 -> x0, matrix products: 9.03 us -> none  [the longest x1 7.61 us: body(): jnp.dot(lax.all_gather(tokens, 'tensor', axis=1, tiled=True), query_weigh...]
    unnamed x0 -> x6, local copies, waits for them, and re-layouts: none -> 6.62 us
    gather x3 -> x0, local copies, waits for them, and re-layouts: 4.93 us -> none  [the longest x1 2.14 us: body(): shrink_mats = every_shrink[storage_rows]]
  transfers between devices with their start and end apart: 3 -> 7, of which waited for: 2 -> 6; matrix products, arithmetic and copies ran while one was open for 2% -> 5% of each run, Pallas kernels for 0% -> 4%
where the time goes in v1:
time: 165 us
  waiting for transfers between devices  74.3 us (45%)
  starting transfers between devices  47.7 us (29%)
  between operations  13.5 us (8%)
  Pallas kernels  13 us (8%)
  local copies, waits for them, and re-layouts  9.68 us (6%)
  other arithmetic  6.57 us (4%)
    all_to_all x1, waiting for transfers between devices, body(): got_up = lax.all_to_all(sent_up.reshape(16, 2, RANK, WIDTH), DP, 0, 0)  25.7 us
    all_to_all x1, waiting for transfers between devices, body(): got_down = lax.all_to_all(sent_down.reshape(16, 2, RANK, WIDTH), DP, 0, 0)  20.8 us
    all_to_all x1, starting transfers between devices, body(): lax.all_to_all(jnp.broadcast_to(rows[None, None, :], (16, 1, 2)), DP, 0, 0)  14.8 us
    all_to_all x1, starting transfers between devices, body(): parts = lax.all_to_all(partial.reshape(32, 8, 128), TENSOR, 0, 0)  12.8 us
    all_to_all x1, waiting for transfers between devices, body(): lax.all_to_all(jnp.broadcast_to(rows[None, None, :], (16, 1, 2)), DP, 0, 0)  8.73 us
    all_to_all x1, waiting for transfers between devices, body(): lax.all_to_all(jnp.broadcast_to(total[None], (32, 8, 128)), TENSOR, 0, 0)  8.35 us
    all_to_all x1, starting transfers between devices, body(): lax.all_to_all(jnp.broadcast_to(total[None], (32, 8, 128)), TENSOR, 0, 0)  7.48 us
    all_to_all x1, waiting for transfers between devices, body(): parts = lax.all_to_all(partial.reshape(32, 8, 128), TENSOR, 0, 0)  6.79 us
  transfers between devices with their start and end apart: 7, of which 6 were waited for; matrix products, arithmetic and copies ran while one was open for 5% of the time, Pallas kernels for 4%

profile of v1, /device:TPU:1, one launch (start us, length us, event | category | flops | bytes accessed | tf_op | source)
XLA Modules:
  0.0 164.7 jit_solution(5365464343478178346)
XLA Ops:
  6.5 0.0 all-gather.2.cloned.1.call-start
  6.5 3.9 %collective-permute-start = (bf16[512,256]{1,0:T(8,128)(2,1)}, bf16[512,256]{1,0:T(8,128)(2,1)S(1)}, u32[]{:S(2)}, u32[]{:S(2)}) collective-permute-start(bf16[512,256]{1,0:T(8,128)(2,1)} %tokens_ref.1), channel_id=1, source_target_pairs={{0,16},{16,0},{1,17},{17,1},{2,18},{18,2},{3,19},{19,3},{4,20},{20... | collective-permute-start | bytes 786440 | tf_op jit(solution)/shard_map/ppermute | solution.py:131
  10.5 4.0 %collective-permute-done = bf16[512,256]{1,0:T(8,128)(2,1)S(1)} collective-permute-done((bf16[512,256]{1,0:T(8,128)(2,1)}, bf16[512,256]{1,0:T(8,128)(2,1)S(1)}, u32[]{:S(2)}, u32[]{:S(2)}) %collective-permute-start) | collective-permute-done | bytes 262176 | tf_op jit(solution)/shard_map/ppermute | solution.py:131
  14.4 1.8 %pad_maximum_fusion = bf16[1024,256]{1,0:T(8,128)(2,1)} fusion(bf16[512,256]{1,0:T(8,128)(2,1)S(1)} %collective-permute-done, bf16[512,256]{1,0:T(8,128)(2,1)} %tokens_ref.1), kind=kLoop, calls=%fused_computation | loop fusion | flops 1048576 | bytes 1048576 | tf_op jit(solution)/shard_map/concatenate | solution.py:133
  16.2 0.0 all-gather.2.cloned.1.call-update
  16.2 0.9 fusion
  17.1 0.6 broadcast_in_dim.46
  17.7 14.8 %all-to-all-start = ((s32[16,1,2]{2,1,0:T(1,128)}), s32[16,1,2]{2,1,0:T(1,128)S(1)}, u32[]{:S(2)}, u32[]{:S(2)}) async-start(s32[16,1,2]{2,1,0:T(1,128)} %broadcast_in_dim.46), calls=%async_computation | async-start | bytes 16384 | tf_op jit(solution)/shard_map/all_to_all | solution.py:138
  32.5 8.7 %all-to-all-done = s32[16,1,2]{2,1,0:T(1,128)S(1)} async-done(((s32[16,1,2]{2,1,0:T(1,128)}), s32[16,1,2]{2,1,0:T(1,128)S(1)}, u32[]{:S(2)}, u32[]{:S(2)}) %all-to-all-start) | async-done | bytes 160 | tf_op jit(solution)/shard_map/all_to_all | solution.py:138
  41.2 0.5 broadcast.27
  41.8 0.7 reduce.3
  42.4 0.6 reshape.27.rows_ref
  43.1 2.3 %shard_map.73 = bf16[32,64,256]{2,1,0:T(8,128)(2,1)} custom-call(s32[32]{0:T(128)} %reshape.27.rows_ref, s32[1]{0:T(128)} %bitcast.3.me_ref, bf16[4,64,256]{2,1,0:T(8,128)(2,1)} %mats_ref.2), custom_call_target="tpu_custom_call" | custom-call | bytes 2097152 | tf_op jit(solution)/shard_map/pallas_call | solution.py:31
  45.3 3.7 %all-to-all-start.1 = ((bf16[16,2,64,256]{3,2,1,0:T(8,128)(2,1)}), bf16[16,2,64,256]{3,2,1,0:T(8,128)(2,1)S(1)}, u32[]{:S(2)}, u32[]{:S(2)}) async-start(bf16[16,2,64,256]{3,2,1,0:T(8,128)(2,1)} %bitcast.13), calls=%async_computation.1 | async-start | bytes 2097152 | tf_op jit(solution)/shard_map/all_to_all | solution.py:148
  49.0 0.6 fusion.1
  49.7 2.5 %compare_select_fusion.1.pick_ref = s32[4]{0:T(128)} fusion(s32[4]{0:T(128)} %param.11, s32[]{:T(128)} %bitcast.1, s32[]{:T(128)} %bitcast, s32[]{:T(128)S(6)} %mul.10), kind=kLoop, calls=%fused_computation.3 | loop fusion | flops 12 | bytes 44 | tf_op jit(solution)/shard_map/jit(_where)/select_n | solution.py:143
  52.2 20.8 %all-to-all-done.1 = bf16[16,2,64,256]{3,2,1,0:T(8,128)(2,1)S(1)} async-done(((bf16[16,2,64,256]{3,2,1,0:T(8,128)(2,1)}), bf16[16,2,64,256]{3,2,1,0:T(8,128)(2,1)S(1)}, u32[]{:S(2)}, u32[]{:S(2)}) %all-to-all-start.1) | async-done | bytes 1048608 | tf_op jit(solution)/shard_map/all_to_all | solution.py:148
  72.9 0.0 copy-start.2
  72.9 1.1 copy-done.2
  74.0 2.3 %shard_map.74 = f32[256,128]{1,0:T(8,128)} custom-call(s32[4]{0:T(128)} %compare_select_fusion.1.pick_ref, bf16[512,256]{1,0:T(8,128)(2,1)} %tokens_ref.1, bf16[32,64,256]{2,1,0:T(8,128)(2,1)} %bitcast.12), custom_call_target="tpu_custom_call" | custom-call | flops 16777216 | bytes 1048576 | tf_op jit(solution)/shard_map/pallas_call | solution.py:58
  76.3 12.8 %all-to-all-start.2 = ((f32[32,8,128]{2,1,0:T(8,128)}), f32[32,8,128]{2,1,0:T(8,128)S(1)}, u32[]{:S(2)}, u32[]{:S(2)}) async-start(f32[32,8,128]{2,1,0:T(8,128)} %bitcast.15), calls=%async_computation.2 | async-start | bytes 262144 | tf_op jit(solution)/shard_map/all_to_all | solution.py:152
  89.1 2.3 %shard_map.75 = bf16[32,64,256]{2,1,0:T(8,128)(2,1)} custom-call(s32[32]{0:T(128)} %reshape.27.rows_ref, s32[1]{0:T(128)} %bitcast.3.me_ref, bf16[4,64,256]{2,1,0:T(8,128)(2,1)} %mats_ref.3), custom_call_target="tpu_custom_call" | custom-call | bytes 2097152 | tf_op jit(solution)/shard_map/pallas_call | solution.py:31
  91.3 6.8 %all-to-all-done.2 = f32[32,8,128]{2,1,0:T(8,128)S(1)} async-done(((f32[32,8,128]{2,1,0:T(8,128)}), f32[32,8,128]{2,1,0:T(8,128)S(1)}, u32[]{:S(2)}, u32[]{:S(2)}) %all-to-all-start.2) | async-done | bytes 131104 | tf_op jit(solution)/shard_map/all_to_all | solution.py:152
  98.1 5.0 %all-to-all-start.4 = ((bf16[16,2,64,256]{3,2,1,0:T(8,128)(2,1)}), bf16[16,2,64,256]{3,2,1,0:T(8,128)(2,1)S(1)}, u32[]{:S(2)}, u32[]{:S(2)}) async-start(bf16[16,2,64,256]{3,2,1,0:T(8,128)(2,1)} %bitcast.14), calls=%async_computation.4 | async-start | bytes 2097152 | tf_op jit(solution)/shard_map/all_to_all | solution.py:149
  103.2 25.7 %all-to-all-done.4 = bf16[16,2,64,256]{3,2,1,0:T(8,128)(2,1)S(1)} async-done(((bf16[16,2,64,256]{3,2,1,0:T(8,128)(2,1)}), bf16[16,2,64,256]{3,2,1,0:T(8,128)(2,1)S(1)}, u32[]{:S(2)}, u32[]{:S(2)}) %all-to-all-start.4) | async-done | bytes 1048608 | tf_op jit(solution)/shard_map/all_to_all | solution.py:149
  128.9 0.7 broadcast_in_dim.48
  129.6 7.5 %all-to-all-start.3 = ((f32[32,8,128]{2,1,0:T(8,128)}), f32[32,8,128]{2,1,0:T(8,128)S(1)}, u32[]{:S(2)}, u32[]{:S(2)}) async-start(f32[32,8,128]{2,1,0:T(8,128)} %broadcast_in_dim.48), calls=%async_computation.3 | async-start | bytes 262144 | tf_op jit(solution)/shard_map/all_to_all | solution.py:154
  137.1 0.7 pad_add_fusion.pick_ref
  137.8 8.4 %all-to-all-done.3 = f32[32,8,128]{2,1,0:T(8,128)S(1)} async-done(((f32[32,8,128]{2,1,0:T(8,128)}), f32[32,8,128]{2,1,0:T(8,128)S(1)}, u32[]{:S(2)}, u32[]{:S(2)}) %all-to-all-start.3) | async-done | bytes 131104 | tf_op jit(solution)/shard_map/all_to_all | solution.py:154
  146.1 3.4 %copy-done = bf16[1024,4096]{1,0:T(8,128)(2,1)S(1)} copy-done((bf16[1024,4096]{1,0:T(8,128)(2,1)S(1)}, bf16[1024,4096]{1,0:T(8,128)(2,1)}, u32[]{:S(2)}) %copy-start) | copy-done | bytes 8388632
  149.5 2.2 %copy-done.1 = bf16[8192,256]{1,0:T(8,128)(2,1)S(1)} copy-done((bf16[8192,256]{1,0:T(8,128)(2,1)S(1)}, bf16[8192,256]{1,0:T(8,128)(2,1)}, u32[]{:S(2)}) %copy-start.1) | copy-done | bytes 4194328
  151.7 6.2 %shard_map.76 = bf16[512,256]{1,0:T(8,128)(2,1)} custom-call(s32[5]{0:T(128)S(1)} %pad_add_fusion.pick_ref, f32[256,128]{1,0:T(8,128)S(1)} %bitcast.11, bf16[32,64,256]{2,1,0:T(8,128)(2,1)S(1)} %bitcast.10, bf16[1024,4096]{1,0:T(8,128)(2,1)S(1)} %copy-done, bf16[8192,256]{1,0:T(8,128)(2,1)S(1)} %copy-done.1), custom_call_target="tpu_custom_call" | custom-call | flops 2147483648 | bytes 12582912 | tf_op jit(solution)/shard_map/pallas_call | solution.py:116
  (5 shorter events, 0.1 us)
Async XLA Ops:
  6.5 139.6 %all-gather.2.cloned.1.call-start = ((), (), s32[]{:S(2)}) async-start(), calls=%async_computation.5 | async-start | bytes 8912896 | tf_op jit(solution)/shard_map/all_gather | solution.py:132
  6.5 7.9 %collective-permute-start = (bf16[512,256]{1,0:T(8,128)(2,1)}, bf16[512,256]{1,0:T(8,128)(2,1)S(1)}, u32[]{:S(2)}, u32[]{:S(2)}) collective-permute-start(bf16[512,256]{1,0:T(8,128)(2,1)} %tokens_ref.1), channel_id=1, source_target_pairs={{0,16},{16,0},{1,17},{17,1},{2,18},{18,2},{3,19},{19,3},{4,20},{20... | collective-permute-start | bytes 786440 | tf_op jit(solution)/shard_map/ppermute | solution.py:131
  17.7 23.5 %all-to-all-start = ((s32[16,1,2]{2,1,0:T(1,128)}), s32[16,1,2]{2,1,0:T(1,128)S(1)}, u32[]{:S(2)}, u32[]{:S(2)}) async-start(s32[16,1,2]{2,1,0:T(1,128)} %broadcast_in_dim.46), calls=%async_computation | async-start | bytes 16384 | tf_op jit(solution)/shard_map/all_to_all | solution.py:138
  45.3 27.6 %all-to-all-start.1 = ((bf16[16,2,64,256]{3,2,1,0:T(8,128)(2,1)}), bf16[16,2,64,256]{3,2,1,0:T(8,128)(2,1)S(1)}, u32[]{:S(2)}, u32[]{:S(2)}) async-start(bf16[16,2,64,256]{3,2,1,0:T(8,128)(2,1)} %bitcast.13), calls=%async_computation.1 | async-start | bytes 2097152 | tf_op jit(solution)/shard_map/all_to_all | solution.py:148
  72.9 1.1 copy-start.2
  76.3 21.9 %all-to-all-start.2 = ((f32[32,8,128]{2,1,0:T(8,128)}), f32[32,8,128]{2,1,0:T(8,128)S(1)}, u32[]{:S(2)}, u32[]{:S(2)}) async-start(f32[32,8,128]{2,1,0:T(8,128)} %bitcast.15), calls=%async_computation.2 | async-start | bytes 262144 | tf_op jit(solution)/shard_map/all_to_all | solution.py:152
  98.1 30.8 %all-to-all-start.4 = ((bf16[16,2,64,256]{3,2,1,0:T(8,128)(2,1)}), bf16[16,2,64,256]{3,2,1,0:T(8,128)(2,1)S(1)}, u32[]{:S(2)}, u32[]{:S(2)}) async-start(bf16[16,2,64,256]{3,2,1,0:T(8,128)(2,1)} %bitcast.14), calls=%async_computation.4 | async-start | bytes 2097152 | tf_op jit(solution)/shard_map/all_to_all | solution.py:149
  129.6 16.6 %all-to-all-start.3 = ((f32[32,8,128]{2,1,0:T(8,128)}), f32[32,8,128]{2,1,0:T(8,128)S(1)}, u32[]{:S(2)}, u32[]{:S(2)}) async-start(f32[32,8,128]{2,1,0:T(8,128)} %broadcast_in_dim.48), calls=%async_computation.3 | async-start | bytes 262144 | tf_op jit(solution)/shard_map/all_to_all | solution.py:154
  146.1 3.4 %copy-start = (bf16[1024,4096]{1,0:T(8,128)(2,1)S(1)}, bf16[1024,4096]{1,0:T(8,128)(2,1)}, u32[]{:S(2)}) copy-start(bf16[1024,4096]{1,0:T(8,128)(2,1)} %all-gather.2.cloned.1.call-done.t_ref) | copy-start | bytes 25165828
  149.5 2.2 %copy-start.1 = (bf16[8192,256]{1,0:T(8,128)(2,1)S(1)}, bf16[8192,256]{1,0:T(8,128)(2,1)}, u32[]{:S(2)}) copy-start(bf16[8192,256]{1,0:T(8,128)(2,1)} %w_ref.1) | copy-start | bytes 12582916
Sparse Core Ops, SparseCore 0:
  16.4 76.6 all-gather.1

commit v2 on v1

v2 whole, which is shorter than its diff:
```python
import jax
import jax.numpy as jnp
from jax import lax
from jax.experimental import pallas as pl
from jax.experimental.pallas import tpu as pltpu
from jax.sharding import Mesh, PartitionSpec as P

SWAP = [(0, 1), (1, 0)]
DP = ("xh", "z")
X = ("xh", "xl")
TENSOR = ("xl", "y", "c")
ROWS = 512
SEG = 128
RANK = 64
WIDTH = 256
OWNED = 4
ZS = 8
HALF = 4096
DEPTH = 1024

ANY = pl.BlockSpec(memory_space=pl.ANY)
SMEM = pl.BlockSpec(memory_space=pltpu.SMEM)
VMEM = pl.BlockSpec(memory_space=pltpu.VMEM)


def select_kernel(ids_ref, stored_ref, xh_ref, down_ref, up_ref, other_ref, out_ref, sems):
    copies = []
    for z in range(ZS):
        for r in range(2):
            row = stored_ref[ids_ref[z, r]]
            slot = row % OWNED
            mine = row // (OWNED * ZS) == xh_ref[0]
            for part, own in enumerate((down_ref, up_ref)):
                sem = sems.at[z, r, part]
                target = out_ref.at[z, 2 * r + part]

                @pl.when(mine)
                def _():
                    pltpu.make_async_copy(own.at[slot], target, sem).start()

                @pl.when(jnp.logical_not(mine))
                def _():
                    pltpu.make_async_copy(other_ref.at[part, slot], target, sem).start()

                copies.append(pltpu.make_async_copy(own.at[0], target, sem))
    for copy in copies:
        copy.wait()


def select(ids, stored, xh, down, up, other):
    return pl.pallas_call(
        select_kernel,
        out_shape=jax.ShapeDtypeStruct((ZS, 4, RANK, WIDTH), down.dtype),
        in_specs=[SMEM, SMEM, SMEM, ANY, ANY, ANY],
        out_specs=ANY,
        scratch_shapes=[pltpu.SemaphoreType.DMA((ZS, 2, 2))],
        cost_estimate=pl.CostEstimate(flops=0, bytes_accessed=2 << 20, transcendentals=0),
    )(ids, stored, xh, down, up, other)


def fetch(ids_ref, stored_ref, got_ref, mats, sems, part):
    copies = []
    for r in range(2):
        source = stored_ref[ids_ref[r]] // OWNED % ZS
        copy = pltpu.make_async_copy(got_ref.at[source, 2 * r + part], mats.at[r], sems.at[r])
        copy.start()
        copies.append(copy)
    return copies


def down_kernel(ids_ref, stored_ref, seg_ref, dp_ref, tokens_ref, got_ref, out_ref, mats, sems):
    for copy in fetch(ids_ref, stored_ref, got_ref, mats, sems, 0):
        copy.wait()
    for k in range(4):
        part = lax.dot_general(
            tokens_ref[k * SEG : (k + 1) * SEG, :],
            mats[seg_ref[k] - 2 * dp_ref[0]],
            (((1,), (1,)), ((), ())),
            preferred_element_type=jnp.float32,
        )
        row, col = (k % 2) * SEG, (k // 2) * RANK
        out_ref[row : row + SEG, col : col + RANK] = part


def down_product(ids, stored, seg, dp, tokens, got):
    return pl.pallas_call(
        down_kernel,
        out_shape=jax.ShapeDtypeStruct((256, 128), jnp.float32),
        in_specs=[SMEM, SMEM, SMEM, SMEM, VMEM, ANY],
        out_specs=VMEM,
        scratch_shapes=[
            pltpu.VMEM((2, RANK, WIDTH), jnp.bfloat16),
            pltpu.SemaphoreType.DMA((2,)),
        ],
        cost_estimate=pl.CostEstimate(flops=1 << 24, bytes_accessed=1 << 20, transcendentals=0),
    )(ids, stored, seg, dp, tokens, got)


def base_kernel(half_ref, t_ref, wa_ref, wb_ref, w_ref, theirs_ref, ours_ref):
    step = pl.program_id(0)
    t = t_ref[...]

    @pl.when(step == 0)
    def _():
        theirs_ref[...] = jnp.zeros_like(theirs_ref)
        ours_ref[...] = jnp.zeros_like(ours_ref)

    @pl.when(step < 2)
    def _():
        theirs_ref[...] += jnp.dot(t, wa_ref[...], preferred_element_type=jnp.float32)

    @pl.when(step >= 2)
    def _():
        theirs_ref[...] += jnp.dot(t, wb_ref[...], preferred_element_type=jnp.float32)

    ours_ref[...] += jnp.dot(t, w_ref[...], preferred_element_type=jnp.float32)


def base_products(half, gathered, wa, wb, weight):
    steps = HALF // DEPTH
    whole = pl.BlockSpec((ROWS, WIDTH), lambda i, half: (0, 0))
    grid_spec = pltpu.PrefetchScalarGridSpec(
        num_scalar_prefetch=1,
        grid=(steps,),
        in_specs=[
            pl.BlockSpec((ROWS, DEPTH), lambda i, half: (0, i)),
            pl.BlockSpec((DEPTH, WIDTH), lambda i, half: (jnp.minimum(i, 1), 0)),
            pl.BlockSpec((DEPTH, WIDTH), lambda i, half: (jnp.maximum(i - 2, 0), 0)),
            pl.BlockSpec((DEPTH, WIDTH), lambda i, half: (half[0] * steps + i, 0)),
        ],
        out_specs=[whole, whole],
    )
    shape = jax.ShapeDtypeStruct((ROWS, WIDTH), jnp.float32)
    return pl.pallas_call(
        base_kernel,
        out_shape=[shape, shape],
        grid_spec=grid_spec,
        cost_estimate=pl.CostEstimate(
            flops=4 * ROWS * HALF * WIDTH, bytes_accessed=10 << 20, transcendentals=0
        ),
    )(half, gathered, wa, wb, weight)


def last_kernel(
    ids_ref, stored_ref, seg_ref, dp_ref, low_ref, got_ref, ours_ref, recv_ref, out_ref, mats, sems
):
    copies = fetch(ids_ref, stored_ref, got_ref, mats, sems, 1)
    for copy in copies:
        copy.wait()
    for k in range(4):
        row, col = (k % 2) * SEG, (k // 2) * RANK
        low = low_ref[row : row + SEG, col : col + RANK].astype(jnp.bfloat16)
        up = jnp.dot(low, mats[seg_ref[k] - 2 * dp_ref[0]], preferred_element_type=jnp.float32)
        rows = slice(k * SEG, (k + 1) * SEG)
        out_ref[rows, :] = (ours_ref[rows, :] + recv_ref[rows, :] + 2.0 * up).astype(jnp.bfloat16)


def last_product(ids, stored, seg, dp, low, got, ours, recv):
    return pl.pallas_call(
        last_kernel,
        out_shape=jax.ShapeDtypeStruct((ROWS, WIDTH), jnp.bfloat16),
        in_specs=[SMEM, SMEM, SMEM, SMEM, VMEM, ANY, VMEM, VMEM],
        out_specs=VMEM,
        scratch_shapes=[
            pltpu.VMEM((2, RANK, WIDTH), jnp.bfloat16),
            pltpu.SemaphoreType.DMA((2,)),
        ],
        cost_estimate=pl.CostEstimate(flops=1 << 24, bytes_accessed=2 << 20, transcendentals=0),
    )(ids, stored, seg, dp, low, got, ours, recv)


def body(tokens, weight, down, up, segment_request, request_ids, stored_row):
    xh = lax.axis_index("xh").astype(jnp.int32)
    xl = lax.axis_index("xl").astype(jnp.int32)
    dp = lax.axis_index(DP).astype(jnp.int32)[None]

    gathered = lax.all_gather(tokens, ("y", "c"), axis=1, tiled=True)

    every_id = lax.all_to_all(
        jnp.broadcast_to(request_ids[None, :], (ZS, 2)), "z", 0, 0, tiled=True
    )
    other = lax.ppermute(jnp.stack([down, up]), "xh", SWAP)

    quarter = HALF // 2
    start = (1 - xl) * HALF
    wa = lax.ppermute(
        lax.dynamic_slice_in_dim(weight, start, quarter, 0), X, [(i, (i + 1) % 4) for i in range(4)]
    )
    wb = lax.ppermute(
        lax.dynamic_slice_in_dim(weight, start + quarter, quarter, 0),
        X,
        [(i, (i + 3) % 4) for i in range(4)],
    )

    sent = select(every_id, stored_row, xh[None], down, up, other)
    got = lax.all_to_all(sent, "z", 0, 0, tiled=True)

    partial = down_product(request_ids, stored_row, segment_request, dp, tokens, got)
    parts = lax.all_to_all(partial.reshape(32, 8, 128), TENSOR, 0, 0)
    total = jnp.sum(parts, axis=0)
    low = lax.all_to_all(jnp.broadcast_to(total[None], (32, 8, 128)), TENSOR, 0, 0)

    theirs, ours = base_products(xl[None], gathered, wa, wb, weight)
    recv = lax.ppermute(theirs, "xl", SWAP)
    return last_product(
        request_ids, stored_row, segment_request, dp, low.reshape(256, 128), got, ours, recv
    )


def solution(mesh):
    fine = Mesh(mesh.devices.reshape(2, 8, 2, 8, 2), ("xh", "z", "xl", "y", "c"))
    in_specs = (
        P(DP, TENSOR),
        P(None, TENSOR),
        P(DP, None, TENSOR),
        P(DP, None, TENSOR),
        P(DP),
        P(DP),
        P(),
    )
    return jax.shard_map(body, mesh=fine, in_specs=in_specs, out_specs=P(DP, TENSOR), check_vma=False)
```

time: 165 us -> 165 us (level)
  waiting for transfers between devices: 74.3 us -> 27.8 us
  Pallas kernels: 13 us -> 49.7 us
  blocking collectives: 0 us -> 34.4 us
  starting transfers between devices: 47.7 us -> 30.4 us
  other arithmetic: 6.57 us -> 1.03 us
  local copies, waits for them, and re-layouts: 9.68 us -> 6.43 us
    all_to_all x5 -> x2, waiting for transfers between devices: 70.3 us -> 6.46 us  [the longest x1 6.45 us: body(): lax.all_to_all(jnp.broadcast_to(request_ids[None, :], (ZS, 2)), 'z', 0, 0...]
    pallas_call x3, Pallas kernels: 10.7 us -> 47 us  [the longest x1 37 us: select(): pl.pallas_call(select_kernel, out_shape=jax.ShapeDtypeStruct((ZS, 4, RANK...]
    all_to_all x0 -> x2, blocking collectives: none -> 34.4 us  [the longest x1 20.3 us: body(): parts = lax.all_to_all(partial.reshape(32, 8, 128), TENSOR, 0, 0)]
    all_to_all x5 -> x2, starting transfers between devices: 43.7 us -> 16.5 us  [the longest x1 10 us: body(): lax.all_to_all(jnp.broadcast_to(request_ids[None, :], (ZS, 2)), 'z', 0, 0...]
    ppermute x1 -> x4, waiting for transfers between devices: 3.96 us -> 20.7 us  [the longest x1 19.8 us: body(): lax.ppermute(lax.dynamic_slice_in_dim(weight, start, quarter, 0), X, [(i,...]
    ppermute x1 -> x4, starting transfers between devices: 3.94 us -> 13.9 us  [the longest x1 5.48 us: body(): other = lax.ppermute(jnp.stack([down, up]), 'xh', SWAP)]
    unnamed x6 -> x12, local copies, waits for them, and re-layouts: 6.62 us -> 3.49 us
    select_n x1 -> x0, other arithmetic: 2.51 us -> none  [body(): jnp.where(request == 0, owner_slot[0], owner_slot[1]).astype(jnp.int32)]
  transfers between devices with their start and end apart: 7 -> 7, of which waited for: 6 -> 3; matrix products, arithmetic and copies ran while one was open for 5% -> 2% of each run, Pallas kernels for 4% -> 29%
where the time goes in v2:
time: 165 us; the launch traced here: 163 us
  Pallas kernels  49.7 us (30%)
  blocking collectives  34.4 us (21%)
  starting transfers between devices  30.4 us (18%)
  waiting for transfers between devices  27.8 us (17%)
  between operations  13.5 us (8%)
  local copies, waits for them, and re-layouts  6.43 us (4%)
    pallas_call x1, Pallas kernels, select(): pl.pallas_call(select_kernel, out_shape=jax.ShapeDtypeStruct((ZS, 4, RANK...  37 us
    all_to_all x1, blocking collectives, body(): parts = lax.all_to_all(partial.reshape(32, 8, 128), TENSOR, 0, 0)  20.3 us
    ppermute x1, waiting for transfers between devices, body(): lax.ppermute(lax.dynamic_slice_in_dim(weight, start, quarter, 0), X, [(i,...  19.8 us
    all_to_all x1, blocking collectives, body(): lax.all_to_all(jnp.broadcast_to(total[None], (32, 8, 128)), TENSOR, 0, 0)  14.1 us
    all_to_all x1, starting transfers between devices, body(): lax.all_to_all(jnp.broadcast_to(request_ids[None, :], (ZS, 2)), 'z', 0, 0...  10 us
    pallas_call x1, Pallas kernels, base_products(): pl.pallas_call(base_kernel, out_shape=[shape, shape], grid_spec=grid_spec...  7.06 us
    all_to_all x1, starting transfers between devices, body(): got = lax.all_to_all(sent, 'z', 0, 0, tiled=True)  6.46 us
    all_to_all x1, waiting for transfers between devices, body(): lax.all_to_all(jnp.broadcast_to(request_ids[None, :], (ZS, 2)), 'z', 0, 0...  6.45 us
  transfers between devices with their start and end apart: 7, of which 3 were waited for; matrix products, arithmetic and copies ran while one was open for 2% of the time, Pallas kernels for 29%

profile of v2, /device:TPU:1, one launch (start us, length us, event | category | flops | bytes accessed | tf_op | source)
XLA Modules:
  0.0 163.3 jit_solution(2570655136121370926)
XLA Ops:
  6.5 0.0 all-gather.2.cloned.1.call-start
  6.5 0.7 all-gather.2.cloned.1.call-update
  7.3 1.0 pad_maximum_fusion
  8.3 5.5 %collective-permute-start = (bf16[2,4,64,256]{3,2,1,0:T(8,128)(2,1)S(1)}, bf16[2,4,64,256]{3,2,1,0:T(8,128)(2,1)S(1)}, u32[]{:S(2)}, u32[]{:S(2)}) collective-permute-start(bf16[2,4,64,256]{3,2,1,0:T(8,128)(2,1)S(1)} %pad_maximum_fusion), channel_id=1, source_target_pairs={{0,256},{256,0},{1,257},{257,1},{2,258},{258,2},{3,259},{259,3},{4... | collective-permute-start | bytes 786440 | tf_op jit(solution)/shard_map/ppermute | solution.py:182
  13.7 1.3 broadcast_in_dim.22
  15.0 10.0 %all-to-all-start = ((s32[8,1,2]{2,1,0:T(1,128)}), s32[8,1,2]{2,1,0:T(1,128)S(1)}, u32[]{:S(2)}, u32[]{:S(2)}) async-start(s32[8,1,2]{2,1,0:T(1,128)} %broadcast_in_dim.22), calls=%async_computation | async-start | bytes 8192 | tf_op jit(solution)/shard_map/all_to_all | solution.py:179
  25.0 6.5 %all-to-all-done = s32[8,1,2]{2,1,0:T(1,128)S(1)} async-done(((s32[8,1,2]{2,1,0:T(1,128)}), s32[8,1,2]{2,1,0:T(1,128)S(1)}, u32[]{:S(2)}, u32[]{:S(2)}) %all-to-all-start) | async-done | bytes 96 | tf_op jit(solution)/shard_map/all_to_all | solution.py:179
  31.5 0.0 copy-start.5
  31.5 0.0 collective-permute-done.other_ref
  31.5 0.0 copy-start.4
  31.5 0.6 copy-done.5
  32.1 0.1 copy-done.4
  32.2 37.0 %shard_map.73 = bf16[8,4,64,256]{3,2,1,0:T(8,128)(2,1)} custom-call(s32[8,2]{1,0:T(8,128)} %bitcast.12, s32[64]{0:T(128)} %stored_ref.5, s32[1]{0:T(128)} %bitcast.2.xh_ref, bf16[4,64,256]{2,1,0:T(8,128)(2,1)} %down_ref.1, bf16[4,64,256]{2,1,0:T(8,128)(2,1)} %up_ref.1, bf16[2,4,64,256]{3,2,1,0:T(8,128)(2,1)} %copy-done.4), custom_call_target="tpu_custom_call" | custom-call | bytes 2097152 | tf_op jit(solution)/shard_map/pallas_call | solution.py:51
  69.2 6.5 %all-to-all-start.1 = ((bf16[8,4,64,256]{3,2,1,0:T(8,128)(2,1)}), bf16[8,4,64,256]{3,2,1,0:T(8,128)(2,1)S(1)}, u32[]{:S(2)}, u32[]{:S(2)}) async-start(bf16[8,4,64,256]{3,2,1,0:T(8,128)(2,1)} %shard_map.73), calls=%async_computation.1 | async-start | bytes 2097152 | tf_op jit(solution)/shard_map/all_to_all | solution.py:196
  75.6 1.7 %constant_dynamic-slice_fusion = (bf16[2048,256]{1,0:T(8,128)(2,1)S(1)}, bf16[2048,256]{1,0:T(8,128)(2,1)S(1)}) fusion(bf16[8192,256]{1,0:T(8,128)(2,1)} %w_ref.1, s32[]{:T(128)S(6)} %select_n.7, s32[]{:T(128)S(6)} %select_n.6), kind=kLoop, calls=%fused_computation.1 | loop fusion | bytes 4194312 | tf_op jit(solution)/shard_map/dynamic_slice | solution.py:190
  77.3 1.9 %collective-permute-start.1 = (bf16[2048,256]{1,0:T(8,128)(2,1)S(1)}, bf16[2048,256]{1,0:T(8,128)(2,1)S(1)}, u32[]{:S(2)}, u32[]{:S(2)}) collective-permute-start(bf16[2048,256]{1,0:T(8,128)(2,1)S(1)} %get-tuple-element.10), channel_id=1, source_target_pairs={{0,16},{16,256},{256,272},{272,0},{1,17},{17,257},{257,273},{273,1... | collective-permute-start | bytes 3145736 | tf_op jit(solution)/shard_map/ppermute | solution.py:186
  79.2 4.6 %collective-permute-start.2 = (bf16[2048,256]{1,0:T(8,128)(2,1)S(1)}, bf16[2048,256]{1,0:T(8,128)(2,1)S(1)}, u32[]{:S(2)}, u32[]{:S(2)}) collective-permute-start(bf16[2048,256]{1,0:T(8,128)(2,1)S(1)} %get-tuple-element.9), channel_id=1, source_target_pairs={{0,272},{16,0},{256,16},{272,256},{1,273},{17,1},{257,17},{273,257... | collective-permute-start | bytes 3145736 | tf_op jit(solution)/shard_map/ppermute | solution.py:189
  83.8 19.8 %collective-permute-done.1.wa_ref = bf16[2048,256]{1,0:T(8,128)(2,1)S(1)} collective-permute-done((bf16[2048,256]{1,0:T(8,128)(2,1)S(1)}, bf16[2048,256]{1,0:T(8,128)(2,1)S(1)}, u32[]{:S(2)}, u32[]{:S(2)}) %collective-permute-start.1) | collective-permute-done | bytes 1048608 | tf_op jit(solution)/shard_map/ppermute | solution.py:186
  103.6 0.9 collective-permute-done.2.wb_ref
  104.5 0.1 copy-done.1
  104.6 0.9 copy-done.2
  105.5 7.1 %shard_map.75 = (f32[512,256]{1,0:T(8,128)}, f32[512,256]{1,0:T(8,128)}) custom-call(s32[1]{0:T(128)} %bitcast.7.half_ref, bf16[512,4096]{1,0:T(8,128)(2,1)} %all-gather.2.cloned.1.call-done.t_ref, bf16[2048,256]{1,0:T(8,128)(2,1)} %copy-done.1, bf16[2048,256]{1,0:T(8,128)(2,1)} %copy-done.2, bf16[8192,256]{1,0:T(8,128)(2,1)} %w_ref.1), custom_call_target="tpu_custom_call" | custom-call | flops 2147483648 | bytes 10485760 | tf_op jit(solution)/shard_map/pallas_call | solution.py:134
  112.5 1.9 %collective-permute-start.3 = (f32[512,256]{1,0:T(8,128)}, f32[512,256]{1,0:T(8,128)S(1)}, u32[]{:S(2)}, u32[]{:S(2)}) collective-permute-start(f32[512,256]{1,0:T(8,128)} %get-tuple-element.8), channel_id=1, source_target_pairs={{0,16},{16,0},{1,17},{17,1},{2,18},{18,2},{3,19},{19,3},{4,20},{20... | collective-permute-start | bytes 1572872 | tf_op jit(solution)/shard_map/ppermute | solution.py:204
  114.5 0.0 all-to-all-done.1.got_ref
  114.5 0.0 copy-start
  114.5 1.0 copy-done
  115.4 2.7 %shard_map.74 = f32[256,128]{1,0:T(8,128)} custom-call(s32[2]{0:T(128)} %ids_ref.3, s32[64]{0:T(128)} %stored_ref.5, s32[4]{0:T(128)} %seg_ref.3, s32[1]{0:T(128)} %bitcast.dp_ref, bf16[512,256]{1,0:T(8,128)(2,1)} %tokens_ref.1, bf16[8,4,64,256]{3,2,1,0:T(8,128)(2,1)} %copy-done), custom_call_target="tpu_custom_call" | custom-call | flops 16777216 | bytes 1048576 | tf_op jit(solution)/shard_map/pallas_call | solution.py:86
  118.2 20.3 %all_to_all.23 = f32[32,8,128]{2,1,0:T(8,128)S(1)} all-to-all(f32[32,8,128]{2,1,0:T(8,128)} %bitcast.9), channel_id=1, replica_groups=mesh['xh'=2,'z'=8,'xl'=2,'y'=8,'c'=2] {'xl','y','c'}, dimensions={0} | all-to-all | bytes 262144 | tf_op jit(solution)/shard_map/all_to_all | solution.py:199
  138.5 14.1 %all_to_all.24 = f32[32,8,128]{2,1,0:T(8,128)} all-to-all(f32[32,8,128]{2,1,0:T(8,128)S(1)} %broadcast_in_dim.24), channel_id=1, replica_groups=mesh['xh'=2,'z'=8,'xl'=2,'y'=8,'c'=2] {'xl','y','c'}, dimensions={0} | all-to-all | bytes 262144 | tf_op jit(solution)/shard_map/all_to_all | solution.py:201
  152.6 0.0 collective-permute-done.3.recv_ref
  152.6 0.8 copy-done.3
  153.4 3.0 %shard_map.76 = bf16[512,256]{1,0:T(8,128)(2,1)} custom-call(s32[2]{0:T(128)} %ids_ref.3, s32[64]{0:T(128)} %stored_ref.5, s32[4]{0:T(128)} %seg_ref.3, s32[1]{0:T(128)} %bitcast.dp_ref, f32[256,128]{1,0:T(8,128)} %bitcast.8, bf16[8,4,64,256]{3,2,1,0:T(8,128)(2,1)} %copy-done, f32[512,256]{1,0:T(8,128)} %get-tuple-element.7.ours_ref, f32[512,256]{1,0:T(8,128)} %copy-done.3), custom_call_target="tpu_custom_call" | custom-call | flops 16777216 | bytes 2097152 | tf_op jit(solution)/shard_map/pallas_call | solution.py:159
  (6 shorter events, 0.1 us)
Async XLA Ops:
  6.5 97.9 %all-gather.2.cloned.1.call-start = ((), (), s32[]{:S(2)}) async-start(), calls=%async_computation.4 | async-start | bytes 4456448 | tf_op jit(solution)/shard_map/all_gather | solution.py:177
  8.3 23.2 %collective-permute-start = (bf16[2,4,64,256]{3,2,1,0:T(8,128)(2,1)S(1)}, bf16[2,4,64,256]{3,2,1,0:T(8,128)(2,1)S(1)}, u32[]{:S(2)}, u32[]{:S(2)}) collective-permute-start(bf16[2,4,64,256]{3,2,1,0:T(8,128)(2,1)S(1)} %pad_maximum_fusion), channel_id=1, source_target_pairs={{0,256},{256,0},{1,257},{257,1},{2,258},{258,2},{3,259},{259,3},{4... | collective-permute-start | bytes 786440 | tf_op jit(solution)/shard_map/ppermute | solution.py:182
  15.0 16.5 %all-to-all-start = ((s32[8,1,2]{2,1,0:T(1,128)}), s32[8,1,2]{2,1,0:T(1,128)S(1)}, u32[]{:S(2)}, u32[]{:S(2)}) async-start(s32[8,1,2]{2,1,0:T(1,128)} %broadcast_in_dim.22), calls=%async_computation | async-start | bytes 8192 | tf_op jit(solution)/shard_map/all_to_all | solution.py:179
  31.5 0.6 copy-start.5
  31.5 0.7 copy-start.4
  69.2 45.3 %all-to-all-start.1 = ((bf16[8,4,64,256]{3,2,1,0:T(8,128)(2,1)}), bf16[8,4,64,256]{3,2,1,0:T(8,128)(2,1)S(1)}, u32[]{:S(2)}, u32[]{:S(2)}) async-start(bf16[8,4,64,256]{3,2,1,0:T(8,128)(2,1)} %shard_map.73), calls=%async_computation.1 | async-start | bytes 2097152 | tf_op jit(solution)/shard_map/all_to_all | solution.py:196
  77.3 26.3 %collective-permute-start.1 = (bf16[2048,256]{1,0:T(8,128)(2,1)S(1)}, bf16[2048,256]{1,0:T(8,128)(2,1)S(1)}, u32[]{:S(2)}, u32[]{:S(2)}) collective-permute-start(bf16[2048,256]{1,0:T(8,128)(2,1)S(1)} %get-tuple-element.10), channel_id=1, source_target_pairs={{0,16},{16,256},{256,272},{272,0},{1,17},{17,257},{257,273},{273,1... | collective-permute-start | bytes 3145736 | tf_op jit(solution)/shard_map/ppermute | solution.py:186
  79.2 25.2 %collective-permute-start.2 = (bf16[2048,256]{1,0:T(8,128)(2,1)S(1)}, bf16[2048,256]{1,0:T(8,128)(2,1)S(1)}, u32[]{:S(2)}, u32[]{:S(2)}) collective-permute-start(bf16[2048,256]{1,0:T(8,128)(2,1)S(1)} %get-tuple-element.9), channel_id=1, source_target_pairs={{0,272},{16,0},{256,16},{272,256},{1,273},{17,1},{257,17},{273,257... | collective-permute-start | bytes 3145736 | tf_op jit(solution)/shard_map/ppermute | solution.py:189
  103.6 1.0 copy-start.1
  104.5 1.0 copy-start.2
  112.5 40.1 %collective-permute-start.3 = (f32[512,256]{1,0:T(8,128)}, f32[512,256]{1,0:T(8,128)S(1)}, u32[]{:S(2)}, u32[]{:S(2)}) collective-permute-start(f32[512,256]{1,0:T(8,128)} %get-tuple-element.8), channel_id=1, source_target_pairs={{0,16},{16,0},{1,17},{17,1},{2,18},{18,2},{3,19},{19,3},{4,20},{20... | collective-permute-start | bytes 1572872 | tf_op jit(solution)/shard_map/ppermute | solution.py:204
  114.5 1.0 copy-start
  152.6 0.8 copy-start.3
Sparse Core Ops, SparseCore 0:
  9.4 58.3 all-gather.1

commit v3 on v2

--- a/solution.py
+++ b/solution.py
@@ -23,39 +23,36 @@
 VMEM = pl.BlockSpec(memory_space=pltpu.VMEM)
 
 
-def select_kernel(ids_ref, stored_ref, xh_ref, down_ref, up_ref, other_ref, out_ref, sems):
-    copies = []
-    for z in range(ZS):
-        for r in range(2):
-            row = stored_ref[ids_ref[z, r]]
-            slot = row % OWNED
-            mine = row // (OWNED * ZS) == xh_ref[0]
-            for part, own in enumerate((down_ref, up_ref)):
-                sem = sems.at[z, r, part]
-                target = out_ref.at[z, 2 * r + part]
-
-                @pl.when(mine)
-                def _():
-                    pltpu.make_async_copy(own.at[slot], target, sem).start()
-
-                @pl.when(jnp.logical_not(mine))
-                def _():
-                    pltpu.make_async_copy(other_ref.at[part, slot], target, sem).start()
-
-                copies.append(pltpu.make_async_copy(own.at[0], target, sem))
-    for copy in copies:
-        copy.wait()
-
-
-def select(ids, stored, xh, down, up, other):
+def select_kernel(ids_ref, stored_ref, xh_ref, own_ref, other_ref, out_ref):
+    def step(i, carry):
+        z, r = i // 2, i % 2
+        row = stored_ref[ids_ref[z, r]]
+        slot = row % OWNED
+        mine = row // (OWNED * ZS) == xh_ref[0]
+
+        @pl.when(mine)
+        def _():
+            for part in range(2):
+                out_ref[z, 2 * r + part] = own_ref[part, slot]
+
+        @pl.when(jnp.logical_not(mine))
+        def _():
+            for part in range(2):
+                out_ref[z, 2 * r + part] = other_ref[part, slot]
+
+        return carry
+
+    lax.fori_loop(0, 2 * ZS, step, 0)
+
+
+def select(ids, stored, xh, own, other):
     return pl.pallas_call(
         select_kernel,
-        out_shape=jax.ShapeDtypeStruct((ZS, 4, RANK, WIDTH), down.dtype),
-        in_specs=[SMEM, SMEM, SMEM, ANY, ANY, ANY],
-        out_specs=ANY,
-        scratch_shapes=[pltpu.SemaphoreType.DMA((ZS, 2, 2))],
+        out_shape=jax.ShapeDtypeStruct((ZS, 4, RANK, WIDTH), own.dtype),
+        in_specs=[SMEM, SMEM, SMEM, VMEM, VMEM],
+        out_specs=VMEM,
         cost_estimate=pl.CostEstimate(flops=0, bytes_accessed=2 << 20, transcendentals=0),
-    )(ids, stored, xh, down, up, other)
+    )(ids, stored, xh, own, other)
 
 
 def fetch(ids_ref, stored_ref, got_ref, mats, sems, part):
@@ -96,45 +93,50 @@
     )(ids, stored, seg, dp, tokens, got)
 
 
-def base_kernel(half_ref, t_ref, wa_ref, wb_ref, w_ref, theirs_ref, ours_ref):
-    step = pl.program_id(0)
-    t = t_ref[...]
-
-    @pl.when(step == 0)
-    def _():
-        theirs_ref[...] = jnp.zeros_like(theirs_ref)
-        ours_ref[...] = jnp.zeros_like(ours_ref)
-
-    @pl.when(step < 2)
-    def _():
-        theirs_ref[...] += jnp.dot(t, wa_ref[...], preferred_element_type=jnp.float32)
-
-    @pl.when(step >= 2)
-    def _():
-        theirs_ref[...] += jnp.dot(t, wb_ref[...], preferred_element_type=jnp.float32)
-
-    ours_ref[...] += jnp.dot(t, w_ref[...], preferred_element_type=jnp.float32)
+def base_kernel(half_ref, t_ref, wa_ref, wb_ref, w_ref, theirs_ref, ours_ref, t, wt, wo, sems):
+    count = HALF // DEPTH
+    per_quarter = count // 2
+    copies = []
+    for i in range(count):
+        cols = slice(i * DEPTH, (i + 1) * DEPTH)
+        source = wa_ref if i < per_quarter else wb_ref
+        rows = pl.ds((i % per_quarter) * DEPTH, DEPTH)
+        start = pl.multiple_of(half_ref[0] * HALF + i * DEPTH, DEPTH)
+        trio = (
+            pltpu.make_async_copy(t_ref.at[:, cols], t.at[i], sems.at[i, 0]),
+            pltpu.make_async_copy(source.at[rows, :], wt.at[i], sems.at[i, 1]),
+            pltpu.make_async_copy(w_ref.at[pl.ds(start, DEPTH), :], wo.at[i], sems.at[i, 2]),
+        )
+        for copy in trio:
+            copy.start()
+        copies.append(trio)
+    for i in range(count):
+        for copy in copies[i]:
+            copy.wait()
+        theirs = jnp.dot(t[i], wt[i], preferred_element_type=jnp.float32)
+        ours = jnp.dot(t[i], wo[i], preferred_element_type=jnp.float32)
+        if i == 0:
+            theirs_ref[...] = theirs
+            ours_ref[...] = ours
+        else:
+            theirs_ref[...] += theirs
+            ours_ref[...] += ours
 
 
 def base_products(half, gathered, wa, wb, weight):
-    steps = HALF // DEPTH
-    whole = pl.BlockSpec((ROWS, WIDTH), lambda i, half: (0, 0))
-    grid_spec = pltpu.PrefetchScalarGridSpec(
-        num_scalar_prefetch=1,
-        grid=(steps,),
-        in_specs=[
-            pl.BlockSpec((ROWS, DEPTH), lambda i, half: (0, i)),
-            pl.BlockSpec((DEPTH, WIDTH), lambda i, half: (jnp.minimum(i, 1), 0)),
-            pl.BlockSpec((DEPTH, WIDTH), lambda i, half: (jnp.maximum(i - 2, 0), 0)),
-            pl.BlockSpec((DEPTH, WIDTH), lambda i, half: (half[0] * steps + i, 0)),
-        ],
-        out_specs=[whole, whole],
-    )
+    count = HALF // DEPTH
     shape = jax.ShapeDtypeStruct((ROWS, WIDTH), jnp.float32)
     return pl.pallas_call(
         base_kernel,
         out_shape=[shape, shape],
-        grid_spec=grid_spec,
+        in_specs=[SMEM, ANY, ANY, ANY, ANY],
+        out_specs=[VMEM, VMEM],
+        scratch_shapes=[
+            pltpu.VMEM((count, ROWS, DEPTH), jnp.bfloat16),
+            pltpu.VMEM((count, DEPTH, WIDTH), jnp.bfloat16),
+            pltpu.VMEM((count, DEPTH, WIDTH), jnp.bfloat16),
+            pltpu.SemaphoreType.DMA((count, 3)),
+        ],
         cost_estimate=pl.CostEstimate(
             flops=4 * ROWS * HALF * WIDTH, bytes_accessed=10 << 20, transcendentals=0
         ),
@@ -149,7 +151,7 @@
         copy.wait()
     for k in range(4):
         row, col = (k % 2) * SEG, (k // 2) * RANK
-        low = low_ref[row : row + SEG, col : col + RANK].astype(jnp.bfloat16)
+        low = low_ref[row : row + SEG, col : col + RANK]
         up = jnp.dot(low, mats[seg_ref[k] - 2 * dp_ref[0]], preferred_element_type=jnp.float32)
         rows = slice(k * SEG, (k + 1) * SEG)
         out_ref[rows, :] = (ours_ref[rows, :] + recv_ref[rows, :] + 2.0 * up).astype(jnp.bfloat16)
@@ -179,7 +181,8 @@
     every_id = lax.all_to_all(
         jnp.broadcast_to(request_ids[None, :], (ZS, 2)), "z", 0, 0, tiled=True
     )
-    other = lax.ppermute(jnp.stack([down, up]), "xh", SWAP)
+    own = jnp.stack([down, up])
+    other = lax.ppermute(own, "xh", SWAP)
 
     quarter = HALF // 2
     start = (1 - xl) * HALF
@@ -192,14 +195,16 @@
         [(i, (i + 3) % 4) for i in range(4)],
     )
 
-    sent = select(every_id, stored_row, xh[None], down, up, other)
+    sent = select(every_id, stored_row, xh[None], own, other)
     got = lax.all_to_all(sent, "z", 0, 0, tiled=True)
+    got, _, _ = lax.optimization_barrier((got, wa, wb))
 
     partial = down_product(request_ids, stored_row, segment_request, dp, tokens, got)
     parts = lax.all_to_all(partial.reshape(32, 8, 128), TENSOR, 0, 0)
-    total = jnp.sum(parts, axis=0)
+    total = jnp.sum(parts, axis=0).astype(jnp.bfloat16)
     low = lax.all_to_all(jnp.broadcast_to(total[None], (32, 8, 128)), TENSOR, 0, 0)
 
+    weight, _ = lax.optimization_barrier((weight, partial))
     theirs, ours = base_products(xl[None], gathered, wa, wb, weight)
     recv = lax.ppermute(theirs, "xl", SWAP)
     return last_product(

time: 165 us -> 124 us (0.75)
  Pallas kernels: 49.7 us -> 13.6 us
  starting transfers between devices: 30.4 us -> 27.8 us
    pallas_call x1, Pallas kernels: 37 us -> 2.67 us  [select(): pl.pallas_call(select_kernel, out_shape=jax.ShapeDtypeStruct((ZS, 4, RANK...]
    all_to_all x1, starting transfers between devices: 6.46 us -> 3.56 us  [body(): got = lax.all_to_all(sent, 'z', 0, 0, tiled=True)]
    pallas_call x1, Pallas kernels: 7.06 us -> 5.27 us  [base_products(): pl.pallas_call(base_kernel, out_shape=[shape, shape], in_specs=[SMEM, ANY...]
  transfers between devices with their start and end apart: 7 -> 7, of which waited for: 3 -> 3; matrix products, arithmetic and copies ran while one was open for 2% -> 3% of each run, Pallas kernels for 29% -> 4%
where the time goes in v3:
time: 124 us; the launch traced here: 122 us
  blocking collectives  34 us (27%)
  starting transfers between devices  27.8 us (22%)
  waiting for transfers between devices  27 us (22%)
  Pallas kernels  13.6 us (11%)
  between operations  13.5 us (11%)
  local copies, waits for them, and re-layouts  5.49 us (4%)
    all_to_all x1, blocking collectives, body(): parts = lax.all_to_all(partial.reshape(32, 8, 128), TENSOR, 0, 0)  20.9 us
    ppermute x1, waiting for transfers between devices, body(): lax.ppermute(lax.dynamic_slice_in_dim(weight, start, quarter, 0), X, [(i,...  18.9 us
    all_to_all x1, blocking collectives, body(): lax.all_to_all(jnp.broadcast_to(total[None], (32, 8, 128)), TENSOR, 0, 0)  13.1 us
    all_to_all x1, starting transfers between devices, body(): lax.all_to_all(jnp.broadcast_to(request_ids[None, :], (ZS, 2)), 'z', 0, 0...  10 us
    all_to_all x1, waiting for transfers between devices, body(): lax.all_to_all(jnp.broadcast_to(request_ids[None, :], (ZS, 2)), 'z', 0, 0...  6.53 us
    ppermute x1, starting transfers between devices, body(): other = lax.ppermute(own, 'xh', SWAP)  5.48 us
    pallas_call x1, Pallas kernels, base_products(): pl.pallas_call(base_kernel, out_shape=[shape, shape], in_specs=[SMEM, ANY...  5.27 us
    ppermute x1, starting transfers between devices, body(): lax.ppermute(lax.dynamic_slice_in_dim(weight, start + quarter, quarter, 0...  4.27 us
  transfers between devices with their start and end apart: 7, of which 3 were waited for; matrix products, arithmetic and copies ran while one was open for 3% of the time, Pallas kernels for 4%

profile of v3, /device:TPU:1, one launch (start us, length us, event | category | flops | bytes accessed | tf_op | source)
XLA Modules:
  0.0 122.5 jit_solution(7215336864295888258)
XLA Ops:
  6.5 0.0 all-gather.2.cloned.1.call-start
  6.5 0.7 all-gather.2.cloned.1.call-update
  7.3 1.0 pad_maximum_fusion.own_ref
  8.3 0.0 copy-start.1
  8.3 5.5 %collective-permute-start = (bf16[2,4,64,256]{3,2,1,0:T(8,128)(2,1)S(1)}, bf16[2,4,64,256]{3,2,1,0:T(8,128)(2,1)S(1)}, u32[]{:S(2)}, u32[]{:S(2)}) collective-permute-start(bf16[2,4,64,256]{3,2,1,0:T(8,128)(2,1)S(1)} %pad_maximum_fusion.own_ref), channel_id=1, source_target_pairs={{0,256},{256,0},{1,257},{257,1},{2,258},{258,2},{3,259},{259,3},{4... | collective-permute-start | bytes 786440 | tf_op jit(solution)/shard_map/ppermute | solution.py:185
  13.8 1.3 %broadcast_in_dim.22 = s32[8,1,2]{2,1,0:T(1,128)} broadcast(s32[2]{0:T(128)} %ids_ref.3), dimensions={2} | broadcast | bytes 72 | tf_op jit(solution)/shard_map/broadcast_in_dim | solution.py:182
  15.0 10.0 %all-to-all-start = ((s32[8,1,2]{2,1,0:T(1,128)}), s32[8,1,2]{2,1,0:T(1,128)S(1)}, u32[]{:S(2)}, u32[]{:S(2)}) async-start(s32[8,1,2]{2,1,0:T(1,128)} %broadcast_in_dim.22), calls=%async_computation | async-start | bytes 8192 | tf_op jit(solution)/shard_map/all_to_all | solution.py:181
  25.0 6.5 %all-to-all-done = s32[8,1,2]{2,1,0:T(1,128)S(1)} async-done(((s32[8,1,2]{2,1,0:T(1,128)}), s32[8,1,2]{2,1,0:T(1,128)S(1)}, u32[]{:S(2)}, u32[]{:S(2)}) %all-to-all-start) | async-done | bytes 96 | tf_op jit(solution)/shard_map/all_to_all | solution.py:181
  31.6 0.0 collective-permute-done.other_ref
  31.6 0.0 copy-done.1
  31.6 0.6 copy-done.5
  32.2 0.1 copy-done.4
  32.3 2.7 %shard_map.73 = bf16[8,4,64,256]{3,2,1,0:T(8,128)(2,1)} custom-call(s32[8,2]{1,0:T(8,128)} %bitcast.12, s32[64]{0:T(128)} %stored_ref.5, s32[1]{0:T(128)} %bitcast.2.xh_ref, bf16[2,4,64,256]{3,2,1,0:T(8,128)(2,1)} %copy-done.1, bf16[2,4,64,256]{3,2,1,0:T(8,128)(2,1)} %copy-done.4), custom_call_target="tpu_custom_call" | custom-call | bytes 2097152 | tf_op jit(solution)/shard_map/pallas_call | solution.py:49
  35.0 3.6 %all-to-all-start.1 = ((bf16[8,4,64,256]{3,2,1,0:T(8,128)(2,1)}), bf16[8,4,64,256]{3,2,1,0:T(8,128)(2,1)S(1)}, u32[]{:S(2)}, u32[]{:S(2)}) async-start(bf16[8,4,64,256]{3,2,1,0:T(8,128)(2,1)} %shard_map.73), calls=%async_computation.1 | async-start | bytes 2097152 | tf_op jit(solution)/shard_map/all_to_all | solution.py:199
  38.5 1.7 %constant_dynamic-slice_fusion = (bf16[2048,256]{1,0:T(8,128)(2,1)S(1)}, bf16[2048,256]{1,0:T(8,128)(2,1)S(1)}) fusion(bf16[8192,256]{1,0:T(8,128)(2,1)} %w_ref, s32[]{:T(128)S(6)} %select_n.7, s32[]{:T(128)S(6)} %select_n.6), kind=kLoop, calls=%fused_computation.1 | loop fusion | bytes 4194312 | tf_op jit(solution)/shard_map/dynamic_slice | solution.py:193
  40.2 2.2 %collective-permute-start.1 = (bf16[2048,256]{1,0:T(8,128)(2,1)S(1)}, bf16[2048,256]{1,0:T(8,128)(2,1)}, u32[]{:S(2)}, u32[]{:S(2)}) collective-permute-start(bf16[2048,256]{1,0:T(8,128)(2,1)S(1)} %get-tuple-element.14), channel_id=1, source_target_pairs={{0,16},{16,256},{256,272},{272,0},{1,17},{17,257},{257,273},{273,1... | collective-permute-start | bytes 3145736 | tf_op jit(solution)/shard_map/ppermute | solution.py:189
  42.5 4.3 %collective-permute-start.2 = (bf16[2048,256]{1,0:T(8,128)(2,1)S(1)}, bf16[2048,256]{1,0:T(8,128)(2,1)}, u32[]{:S(2)}, u32[]{:S(2)}) collective-permute-start(bf16[2048,256]{1,0:T(8,128)(2,1)S(1)} %get-tuple-element.13), channel_id=1, source_target_pairs={{0,272},{16,0},{256,16},{272,256},{1,273},{17,1},{257,17},{273,257... | collective-permute-start | bytes 3145736 | tf_op jit(solution)/shard_map/ppermute | solution.py:192
  46.8 18.9 %collective-permute-done.1.wa_ref = bf16[2048,256]{1,0:T(8,128)(2,1)} collective-permute-done((bf16[2048,256]{1,0:T(8,128)(2,1)S(1)}, bf16[2048,256]{1,0:T(8,128)(2,1)}, u32[]{:S(2)}, u32[]{:S(2)}) %collective-permute-start.1) | collective-permute-done | bytes 1048608 | tf_op jit(solution)/shard_map/ppermute | solution.py:189
  65.6 0.9 collective-permute-done.2.wb_ref
  66.5 0.0 all-to-all-done.1.got_ref
  66.5 1.0 copy-done
  67.5 2.7 %shard_map.74 = f32[256,128]{1,0:T(8,128)} custom-call(s32[2]{0:T(128)} %ids_ref.3, s32[64]{0:T(128)} %stored_ref.5, s32[4]{0:T(128)} %seg_ref.3, s32[1]{0:T(128)} %bitcast.dp_ref, bf16[512,256]{1,0:T(8,128)(2,1)} %tokens_ref.1, bf16[8,4,64,256]{3,2,1,0:T(8,128)(2,1)} %copy-done), custom_call_target="tpu_custom_call" | custom-call | flops 16777216 | bytes 1048576 | tf_op jit(solution)/shard_map/pallas_call | solution.py:83
  70.2 0.0 all-gather.2.cloned.1.call-done.t_ref
  70.2 0.0 copy-start.3
  70.2 5.3 %shard_map.75 = (f32[512,256]{1,0:T(8,128)}, f32[512,256]{1,0:T(8,128)}) custom-call(s32[1]{0:T(128)} %bitcast.7.half_ref, bf16[512,4096]{1,0:T(8,128)(2,1)} %all-gather.2.cloned.1.call-done.t_ref, bf16[2048,256]{1,0:T(8,128)(2,1)} %collective-permute-done.1.wa_ref, bf16[2048,256]{1,0:T(8,128)(2,1)} %collective-permute-done.2.wb_ref, bf16[8192,256]{1,0:T(8,128)(2,1)} %w_ref), custom_call_target="tpu_custom_call" | custom-call | flops 2147483648 | bytes 10485760 | tf_op jit(solution)/shard_map/pallas_call | solution.py:129
  75.5 2.2 %collective-permute-start.3 = (f32[512,256]{1,0:T(8,128)}, f32[512,256]{1,0:T(8,128)S(1)}, u32[]{:S(2)}, u32[]{:S(2)}) collective-permute-start(f32[512,256]{1,0:T(8,128)} %get-tuple-element.12), channel_id=1, source_target_pairs={{0,16},{16,0},{1,17},{17,1},{2,18},{18,2},{3,19},{19,3},{4,20},{20... | collective-permute-start | bytes 1572872 | tf_op jit(solution)/shard_map/ppermute | solution.py:209
  77.7 0.0 copy-done.3
  77.7 20.9 %all_to_all.23 = f32[32,8,128]{2,1,0:T(8,128)S(1)} all-to-all(f32[32,8,128]{2,1,0:T(8,128)S(1)} %bitcast.8), channel_id=1, replica_groups=mesh['xh'=2,'z'=8,'xl'=2,'y'=8,'c'=2] {'xl','y','c'}, dimensions={0} | all-to-all | bytes 262144 | tf_op jit(solution)/shard_map/all_to_all | solution.py:203
  98.7 13.1 %all_to_all.24 = bf16[32,8,128]{2,1,0:T(8,128)(2,1)} all-to-all(bf16[32,8,128]{2,1,0:T(8,128)(2,1)S(1)} %broadcast_in_dim.24), channel_id=1, replica_groups=mesh['xh'=2,'z'=8,'xl'=2,'y'=8,'c'=2] {'xl','y','c'}, dimensions={0} | all-to-all | bytes 131072 | tf_op jit(solution)/shard_map/all_to_all | solution.py:205
  111.8 0.0 collective-permute-done.3.recv_ref
  111.8 0.8 copy-done.2
  112.6 3.0 %shard_map.76 = bf16[512,256]{1,0:T(8,128)(2,1)} custom-call(s32[2]{0:T(128)} %ids_ref.3, s32[64]{0:T(128)} %stored_ref.5, s32[4]{0:T(128)} %seg_ref.3, s32[1]{0:T(128)} %bitcast.dp_ref, bf16[256,128]{1,0:T(8,128)(2,1)} %bitcast.9, bf16[8,4,64,256]{3,2,1,0:T(8,128)(2,1)} %copy-done, f32[512,256]{1,0:T(8,128)} %get-tuple-element.11.ours_ref, f32[512,256]{1,0:T(8,128)} %copy-done.2), custom_call_target="tpu_custom_call" | custom-call | flops 16777216 | bytes 2097152 | tf_op jit(solution)/shard_map/pallas_call | solution.py:161
  (6 shorter events, 0.1 us)
Async XLA Ops:
  6.5 63.7 %all-gather.2.cloned.1.call-start = ((), (), s32[]{:S(2)}) async-start(), calls=%async_computation.4 | async-start | bytes 4456448 | tf_op jit(solution)/shard_map/all_gather | solution.py:179
  8.3 23.3 %copy-start.1 = (bf16[2,4,64,256]{3,2,1,0:T(8,128)(2,1)}, bf16[2,4,64,256]{3,2,1,0:T(8,128)(2,1)S(1)}, u32[]{:S(2)}) copy-start(bf16[2,4,64,256]{3,2,1,0:T(8,128)(2,1)S(1)} %pad_maximum_fusion.own_ref) | copy-start | bytes 786436
  8.3 23.3 %collective-permute-start = (bf16[2,4,64,256]{3,2,1,0:T(8,128)(2,1)S(1)}, bf16[2,4,64,256]{3,2,1,0:T(8,128)(2,1)S(1)}, u32[]{:S(2)}, u32[]{:S(2)}) collective-permute-start(bf16[2,4,64,256]{3,2,1,0:T(8,128)(2,1)S(1)} %pad_maximum_fusion.own_ref), channel_id=1, source_target_pairs={{0,256},{256,0},{1,257},{257,1},{2,258},{258,2},{3,259},{259,3},{4... | collective-permute-start | bytes 786440 | tf_op jit(solution)/shard_map/ppermute | solution.py:185
  15.0 16.6 %all-to-all-start = ((s32[8,1,2]{2,1,0:T(1,128)}), s32[8,1,2]{2,1,0:T(1,128)S(1)}, u32[]{:S(2)}, u32[]{:S(2)}) async-start(s32[8,1,2]{2,1,0:T(1,128)} %broadcast_in_dim.22), calls=%async_computation | async-start | bytes 8192 | tf_op jit(solution)/shard_map/all_to_all | solution.py:181
  31.6 0.6 copy-start.5
  31.6 0.7 copy-start.4
  35.0 31.5 %all-to-all-start.1 = ((bf16[8,4,64,256]{3,2,1,0:T(8,128)(2,1)}), bf16[8,4,64,256]{3,2,1,0:T(8,128)(2,1)S(1)}, u32[]{:S(2)}, u32[]{:S(2)}) async-start(bf16[8,4,64,256]{3,2,1,0:T(8,128)(2,1)} %shard_map.73), calls=%async_computation.1 | async-start | bytes 2097152 | tf_op jit(solution)/shard_map/all_to_all | solution.py:199
  40.2 25.4 %collective-permute-start.1 = (bf16[2048,256]{1,0:T(8,128)(2,1)S(1)}, bf16[2048,256]{1,0:T(8,128)(2,1)}, u32[]{:S(2)}, u32[]{:S(2)}) collective-permute-start(bf16[2048,256]{1,0:T(8,128)(2,1)S(1)} %get-tuple-element.14), channel_id=1, source_target_pairs={{0,16},{16,256},{256,272},{272,0},{1,17},{17,257},{257,273},{273,1... | collective-permute-start | bytes 3145736 | tf_op jit(solution)/shard_map/ppermute | solution.py:189
  42.5 24.0 %collective-permute-start.2 = (bf16[2048,256]{1,0:T(8,128)(2,1)S(1)}, bf16[2048,256]{1,0:T(8,128)(2,1)}, u32[]{:S(2)}, u32[]{:S(2)}) collective-permute-start(bf16[2048,256]{1,0:T(8,128)(2,1)S(1)} %get-tuple-element.13), channel_id=1, source_target_pairs={{0,272},{16,0},{256,16},{272,256},{1,273},{17,1},{257,17},{273,257... | collective-permute-start | bytes 3145736 | tf_op jit(solution)/shard_map/ppermute | solution.py:192
  66.5 1.0 copy-start
  70.2 7.5 %copy-start.3 = (f32[256,128]{1,0:T(8,128)S(1)}, f32[256,128]{1,0:T(8,128)}, u32[]{:S(2)}) copy-start(f32[256,128]{1,0:T(8,128)} %shard_map.74) | copy-start | bytes 393220
  75.5 36.3 %collective-permute-start.3 = (f32[512,256]{1,0:T(8,128)}, f32[512,256]{1,0:T(8,128)S(1)}, u32[]{:S(2)}, u32[]{:S(2)}) collective-permute-start(f32[512,256]{1,0:T(8,128)} %get-tuple-element.12), channel_id=1, source_target_pairs={{0,16},{16,0},{1,17},{17,1},{2,18},{18,2},{3,19},{19,3},{4,20},{20... | collective-permute-start | bytes 1572872 | tf_op jit(solution)/shard_map/ppermute | solution.py:209
  111.8 0.8 copy-start.2
Sparse Core Ops, SparseCore 0:
  9.4 58.3 all-gather.1

commit v4 on v3

--- a/solution.py
+++ b/solution.py
@@ -6,7 +6,7 @@
 from jax.sharding import Mesh, PartitionSpec as P
 
 SWAP = [(0, 1), (1, 0)]
-DP = ("xh", "z")
+DP = ("xh", "zh", "zl")
 X = ("xh", "xl")
 TENSOR = ("xl", "y", "c")
 ROWS = 512
@@ -15,6 +15,7 @@
 WIDTH = 256
 OWNED = 4
 ZS = 8
+PEERS = 4
 HALF = 4096
 DEPTH = 1024
 
@@ -23,42 +24,48 @@
 VMEM = pl.BlockSpec(memory_space=pltpu.VMEM)
 
 
-def select_kernel(ids_ref, stored_ref, xh_ref, own_ref, other_ref, out_ref):
+def vmem(mib):
+    return pltpu.CompilerParams(vmem_limit_bytes=mib << 20)
+
+
+def select_kernel(ids_ref, stored_ref, place_ref, own_ref, x_ref, z_ref, xz_ref, out_ref):
+    held = (own_ref, x_ref, z_ref, xz_ref)
+
     def step(i, carry):
-        z, r = i // 2, i % 2
-        row = stored_ref[ids_ref[z, r]]
+        zh, r = i // 2, i % 2
+        row = stored_ref[ids_ref[zh, 0, r]]
         slot = row % OWNED
-        mine = row // (OWNED * ZS) == xh_ref[0]
-
-        @pl.when(mine)
-        def _():
-            for part in range(2):
-                out_ref[z, 2 * r + part] = own_ref[part, slot]
-
-        @pl.when(jnp.logical_not(mine))
-        def _():
-            for part in range(2):
-                out_ref[z, 2 * r + part] = other_ref[part, slot]
+        owner = row // OWNED
+        across_x = owner // ZS != place_ref[0]
+        across_z = owner % 2 != place_ref[1]
+        which = across_x.astype(jnp.int32) + 2 * across_z.astype(jnp.int32)
+        for j in range(4):
+
+            @pl.when(which == j)
+            def _():
+                for part in range(2):
+                    out_ref[zh, 2 * r + part] = held[j][part, slot]
 
         return carry
 
-    lax.fori_loop(0, 2 * ZS, step, 0)
-
-
-def select(ids, stored, xh, own, other):
+    lax.fori_loop(0, 2 * PEERS, step, 0)
+
+
+def select(ids, stored, place, own, x, z, xz):
     return pl.pallas_call(
         select_kernel,
-        out_shape=jax.ShapeDtypeStruct((ZS, 4, RANK, WIDTH), own.dtype),
-        in_specs=[SMEM, SMEM, SMEM, VMEM, VMEM],
-        out_specs=VMEM,
+        out_shape=jax.ShapeDtypeStruct((PEERS, 4, RANK, WIDTH), own.dtype),
+        in_specs=[SMEM, SMEM, SMEM, VMEM, VMEM, VMEM, VMEM],
+        out_specs=VMEM,
+        compiler_params=vmem(8),
         cost_estimate=pl.CostEstimate(flops=0, bytes_accessed=2 << 20, transcendentals=0),
-    )(ids, stored, xh, own, other)
+    )(ids, stored, place, own, x, z, xz)
 
 
 def fetch(ids_ref, stored_ref, got_ref, mats, sems, part):
     copies = []
     for r in range(2):
-        source = stored_ref[ids_ref[r]] // OWNED % ZS
+        source = stored_ref[ids_ref[r]] // OWNED % ZS // 2
         copy = pltpu.make_async_copy(got_ref.at[source, 2 * r + part], mats.at[r], sems.at[r])
         copy.start()
         copies.append(copy)
@@ -89,11 +96,28 @@
             pltpu.VMEM((2, RANK, WIDTH), jnp.bfloat16),
             pltpu.SemaphoreType.DMA((2,)),
         ],
+        compiler_params=vmem(4),
         cost_estimate=pl.CostEstimate(flops=1 << 24, bytes_accessed=1 << 20, transcendentals=0),
     )(ids, stored, seg, dp, tokens, got)
 
 
-def base_kernel(half_ref, t_ref, wa_ref, wb_ref, w_ref, theirs_ref, ours_ref, t, wt, wo, sems):
+def sum_kernel(parts_ref, out_ref):
+    total = jnp.sum(parts_ref[...], axis=0).astype(jnp.bfloat16)
+    out_ref[...] = jnp.broadcast_to(total[None], out_ref.shape)
+
+
+def sum_parts(parts):
+    return pl.pallas_call(
+        sum_kernel,
+        out_shape=jax.ShapeDtypeStruct(parts.shape, jnp.bfloat16),
+        in_specs=[VMEM],
+        out_specs=VMEM,
+        compiler_params=vmem(4),
+        cost_estimate=pl.CostEstimate(flops=0, bytes_accessed=128 << 20, transcendentals=0),
+    )(parts)
+
+
+def base_kernel(half_ref, t_ref, wa_ref, wb_ref, w_ref, theirs_ref, ours_ref, t, wt, wo, acc, sems):
     count = HALF // DEPTH
     per_quarter = count // 2
     copies = []
@@ -116,27 +140,32 @@
         theirs = jnp.dot(t[i], wt[i], preferred_element_type=jnp.float32)
         ours = jnp.dot(t[i], wo[i], preferred_element_type=jnp.float32)
         if i == 0:
-            theirs_ref[...] = theirs
+            acc[...] = theirs
             ours_ref[...] = ours
         else:
-            theirs_ref[...] += theirs
+            acc[...] += theirs
             ours_ref[...] += ours
+    theirs_ref[...] = acc[...].astype(jnp.bfloat16)
 
 
 def base_products(half, gathered, wa, wb, weight):
     count = HALF // DEPTH
-    shape = jax.ShapeDtypeStruct((ROWS, WIDTH), jnp.float32)
     return pl.pallas_call(
         base_kernel,
-        out_shape=[shape, shape],
+        out_shape=[
+            jax.ShapeDtypeStruct((ROWS, WIDTH), jnp.bfloat16),
+            jax.ShapeDtypeStruct((ROWS, WIDTH), jnp.float32),
+        ],
         in_specs=[SMEM, ANY, ANY, ANY, ANY],
         out_specs=[VMEM, VMEM],
         scratch_shapes=[
             pltpu.VMEM((count, ROWS, DEPTH), jnp.bfloat16),
             pltpu.VMEM((count, DEPTH, WIDTH), jnp.bfloat16),
             pltpu.VMEM((count, DEPTH, WIDTH), jnp.bfloat16),
+            pltpu.VMEM((ROWS, WIDTH), jnp.float32),
             pltpu.SemaphoreType.DMA((count, 3)),
         ],
+        compiler_params=vmem(56),
         cost_estimate=pl.CostEstimate(
             flops=4 * ROWS * HALF * WIDTH, bytes_accessed=10 << 20, transcendentals=0
         ),
@@ -154,7 +183,7 @@
         low = low_ref[row : row + SEG, col : col + RANK]
         up = jnp.dot(low, mats[seg_ref[k] - 2 * dp_ref[0]], preferred_element_type=jnp.float32)
         rows = slice(k * SEG, (k + 1) * SEG)
-        out_ref[rows, :] = (ours_ref[rows, :] + recv_ref[rows, :] + 2.0 * up).astype(jnp.bfloat16)
+        out_ref[rows, :] = (ours_ref[rows, :] + recv_ref[rows, :].astype(jnp.float32) + 2.0 * up).astype(jnp.bfloat16)
 
 
 def last_product(ids, stored, seg, dp, low, got, ours, recv):
@@ -167,42 +196,43 @@
             pltpu.VMEM((2, RANK, WIDTH), jnp.bfloat16),
             pltpu.SemaphoreType.DMA((2,)),
         ],
+        compiler_params=vmem(8),
         cost_estimate=pl.CostEstimate(flops=1 << 24, bytes_accessed=2 << 20, transcendentals=0),
     )(ids, stored, seg, dp, low, got, ours, recv)
 
 
 def body(tokens, weight, down, up, segment_request, request_ids, stored_row):
-    xh = lax.axis_index("xh").astype(jnp.int32)
     xl = lax.axis_index("xl").astype(jnp.int32)
     dp = lax.axis_index(DP).astype(jnp.int32)[None]
+    place = jnp.stack([lax.axis_index("xh"), lax.axis_index("zl")]).astype(jnp.int32)
 
     gathered = lax.all_gather(tokens, ("y", "c"), axis=1, tiled=True)
 
     every_id = lax.all_to_all(
-        jnp.broadcast_to(request_ids[None, :], (ZS, 2)), "z", 0, 0, tiled=True
+        jnp.broadcast_to(request_ids[None, None, :], (PEERS, 1, 2)), "zh", 0, 0, tiled=True
     )
     own = jnp.stack([down, up])
-    other = lax.ppermute(own, "xh", SWAP)
-
+    pair = ("xh", "zl")
+    far = [lax.ppermute(own, pair, [(i, i ^ flip) for i in range(4)]) for flip in (2, 1, 3)]
+
+    sent = select(every_id, stored_row, place, own, *far)
+    late_weight, _ = lax.optimization_barrier((weight, every_id))
     quarter = HALF // 2
     start = (1 - xl) * HALF
     wa = lax.ppermute(
-        lax.dynamic_slice_in_dim(weight, start, quarter, 0), X, [(i, (i + 1) % 4) for i in range(4)]
+        lax.dynamic_slice_in_dim(late_weight, start, quarter, 0), X, [(i, (i + 1) % 4) for i in range(4)]
     )
     wb = lax.ppermute(
-        lax.dynamic_slice_in_dim(weight, start + quarter, quarter, 0),
+        lax.dynamic_slice_in_dim(late_weight, start + quarter, quarter, 0),
         X,
         [(i, (i + 3) % 4) for i in range(4)],
     )
 
-    sent = select(every_id, stored_row, xh[None], own, other)
-    got = lax.all_to_all(sent, "z", 0, 0, tiled=True)
-    got, _, _ = lax.optimization_barrier((got, wa, wb))
+    got = lax.all_to_all(sent, "zh", 0, 0, tiled=True)
 
     partial = down_product(request_ids, stored_row, segment_request, dp, tokens, got)
     parts = lax.all_to_all(partial.reshape(32, 8, 128), TENSOR, 0, 0)
-    total = jnp.sum(parts, axis=0).astype(jnp.bfloat16)
-    low = lax.all_to_all(jnp.broadcast_to(total[None], (32, 8, 128)), TENSOR, 0, 0)
+    low = lax.all_to_all(sum_parts(parts), TENSOR, 0, 0)
 
     weight, _ = lax.optimization_barrier((weight, partial))
     theirs, ours = base_products(xl[None], gathered, wa, wb, weight)
@@ -213,7 +243,7 @@
 
 
 def solution(mesh):
-    fine = Mesh(mesh.devices.reshape(2, 8, 2, 8, 2), ("xh", "z", "xl", "y", "c"))
+    fine = Mesh(mesh.devices.reshape(2, 4, 2, 2, 8, 2), ("xh", "zh", "zl", "xl", "y", "c"))
     in_specs = (
         P(DP, TENSOR),
         P(None, TENSOR),

time: 124 us -> 110 us (0.89); the launches traced: 122 us -> 110 us
  starting transfers between devices: 27.8 us -> 48 us
  blocking collectives: 34 us -> 14.7 us
  waiting for transfers between devices: 27 us -> 18.2 us
  Pallas kernels: 13.6 us -> 10.2 us
  local copies, waits for them, and re-layouts: 5.49 us -> 3.97 us
    ppermute x3 -> x5, waiting for transfers between devices: 19.7 us -> 0.01 us  [the longest x3 0.01 us: body(): lax.ppermute(own, pair, [(i, i ^ flip) for i in range(4)])]
    all_to_all x2 -> x1, blocking collectives: 34 us -> 14.7 us  [body(): low = lax.all_to_all(sum_parts(parts), TENSOR, 0, 0)]
    all_to_all x2 -> x3, starting transfers between devices: 13.6 us -> 26.8 us  [the longest x1 14 us: body(): parts = lax.all_to_all(partial.reshape(32, 8, 128), TENSOR, 0, 0)]
    all_to_all x2 -> x3, waiting for transfers between devices: 6.54 us -> 17.5 us  [the longest x1 10.3 us: body(): got = lax.all_to_all(sent, 'zh', 0, 0, tiled=True)]
    ppermute x3 -> x5, starting transfers between devices: 12 us -> 17.9 us  [the longest x3 11.4 us: body(): lax.ppermute(own, pair, [(i, i ^ flip) for i in range(4)])]
    unnamed x12 -> x10, local copies, waits for them, and re-layouts: 2.54 us -> 1.06 us
    pallas_call x1, Pallas kernels: 2.96 us -> 1.63 us  [last_product(): pl.pallas_call(last_kernel, out_shape=jax.ShapeDtypeStruct((ROWS, WIDTH),...]
    pallas_call x2 -> x3, Pallas kernels: 7.94 us -> 6.96 us  [the longest x1 5.08 us: base_products(): pl.pallas_call(base_kernel, out_shape=[jax.ShapeDtypeStruct((ROWS, WIDTH)...]
  transfers between devices with their start and end apart: 7 -> 10, of which waited for: 3 -> 3; matrix products, arithmetic and copies ran while one was open for 3% -> 4% of each run, Pallas kernels for 4% -> 8%
where the time goes in v4:
time: 110 us
  starting transfers between devices  48 us (44%)
  waiting for transfers between devices  18.2 us (17%)
  blocking collectives  14.7 us (13%)
  between operations  13.6 us (12%)
  Pallas kernels  10.2 us (9%)
  local copies, waits for them, and re-layouts  3.97 us (4%)
    all_to_all x1, blocking collectives, body(): low = lax.all_to_all(sum_parts(parts), TENSOR, 0, 0)  14.7 us
    all_to_all x1, starting transfers between devices, body(): parts = lax.all_to_all(partial.reshape(32, 8, 128), TENSOR, 0, 0)  14 us
    ppermute x3, starting transfers between devices, body(): lax.ppermute(own, pair, [(i, i ^ flip) for i in range(4)])  11.4 us
    all_to_all x1, waiting for transfers between devices, body(): got = lax.all_to_all(sent, 'zh', 0, 0, tiled=True)  10.3 us
    all_to_all x1, starting transfers between devices, body(): lax.all_to_all(jnp.broadcast_to(request_ids[None, None, :], (PEERS, 1, 2)...  9.32 us
    all_to_all x1, waiting for transfers between devices, body(): lax.all_to_all(jnp.broadcast_to(request_ids[None, None, :], (PEERS, 1, 2)...  6.52 us
    pallas_call x1, Pallas kernels, base_products(): pl.pallas_call(base_kernel, out_shape=[jax.ShapeDtypeStruct((ROWS, WIDTH)...  5.08 us
    all_to_all x1, starting transfers between devices, body(): got = lax.all_to_all(sent, 'zh', 0, 0, tiled=True)  3.47 us
  transfers between devices with their start and end apart: 10, of which 3 were waited for; matrix products, arithmetic and copies ran while one was open for 4% of the time, Pallas kernels for 8%

profile of v4, /device:TPU:1, one launch (start us, length us, event | category | flops | bytes accessed | tf_op | source)
XLA Modules:
  0.0 109.8 jit_solution(3986199299762401825)
XLA Ops:
  6.5 0.0 all-gather.2.cloned.1.call-start
  6.6 0.7 all-gather.2.cloned.1.call-update
  7.3 1.0 pad_maximum_fusion.own_ref
  8.3 5.5 %collective-permute-start = (bf16[2,4,64,256]{3,2,1,0:T(8,128)(2,1)S(1)}, bf16[2,4,64,256]{3,2,1,0:T(8,128)(2,1)S(1)}, u32[]{:S(2)}, u32[]{:S(2)}) collective-permute-start(bf16[2,4,64,256]{3,2,1,0:T(8,128)(2,1)S(1)} %pad_maximum_fusion.own_ref), channel_id=1, source_target_pairs={{0,256},{32,288},{256,0},{288,32},{1,257},{33,289},{257,1},{289,33... | collective-permute-start | bytes 786440 | tf_op jit(solution)/shard_map/ppermute | solution.py:216
  13.8 4.0 %collective-permute-start.1 = (bf16[2,4,64,256]{3,2,1,0:T(8,128)(2,1)S(1)}, bf16[2,4,64,256]{3,2,1,0:T(8,128)(2,1)S(1)}, u32[]{:S(2)}, u32[]{:S(2)}) collective-permute-start(bf16[2,4,64,256]{3,2,1,0:T(8,128)(2,1)S(1)} %pad_maximum_fusion.own_ref), channel_id=1, source_target_pairs={{0,32},{32,0},{256,288},{288,256},{1,33},{33,1},{257,289},{289,257... | collective-permute-start | bytes 786440 | tf_op jit(solution)/shard_map/ppermute | solution.py:216
  17.8 1.9 %collective-permute-start.2 = (bf16[2,4,64,256]{3,2,1,0:T(8,128)(2,1)S(1)}, bf16[2,4,64,256]{3,2,1,0:T(8,128)(2,1)S(1)}, u32[]{:S(2)}, u32[]{:S(2)}) collective-permute-start(bf16[2,4,64,256]{3,2,1,0:T(8,128)(2,1)S(1)} %pad_maximum_fusion.own_ref), channel_id=1, source_target_pairs={{0,288},{32,256},{256,32},{288,0},{1,289},{33,257},{257,33},{289,1... | collective-permute-start | bytes 786440 | tf_op jit(solution)/shard_map/ppermute | solution.py:216
  19.7 1.2 %broadcast_in_dim.13 = s32[4,1,2]{2,1,0:T(1,128)} broadcast(s32[2]{0:T(128)} %ids_ref.3), dimensions={2} | broadcast | bytes 40 | tf_op jit(solution)/shard_map/broadcast_in_dim | solution.py:212
  20.9 9.3 %all-to-all-start = ((s32[4,1,2]{2,1,0:T(1,128)}), s32[4,1,2]{2,1,0:T(1,128)S(1)}, u32[]{:S(2)}, u32[]{:S(2)}) async-start(s32[4,1,2]{2,1,0:T(1,128)} %broadcast_in_dim.13), calls=%async_computation | async-start | bytes 4096 | tf_op jit(solution)/shard_map/all_to_all | solution.py:211
  30.3 6.5 %all-to-all-done.ids_ref = s32[4,1,2]{2,1,0:T(1,128)S(1)} async-done(((s32[4,1,2]{2,1,0:T(1,128)}), s32[4,1,2]{2,1,0:T(1,128)S(1)}, u32[]{:S(2)}, u32[]{:S(2)}) %all-to-all-start) | async-done | bytes 64 | tf_op jit(solution)/shard_map/all_to_all | solution.py:211
  36.8 1.7 %constant_dynamic-slice_fusion = (bf16[2048,256]{1,0:T(8,128)(2,1)S(1)}, bf16[2048,256]{1,0:T(8,128)(2,1)S(1)}) fusion(bf16[8192,256]{1,0:T(8,128)(2,1)} %w_ref, s32[]{:T(128)S(6)} %select_n.7, s32[]{:T(128)S(6)} %select_n.6), kind=kLoop, calls=%fused_computation.2 | loop fusion | bytes 4194312 | tf_op jit(solution)/shard_map/dynamic_slice | solution.py:226
  38.5 3.1 %collective-permute-start.3 = (bf16[2048,256]{1,0:T(8,128)(2,1)S(1)}, bf16[2048,256]{1,0:T(8,128)(2,1)}, u32[]{:S(2)}, u32[]{:S(2)}) collective-permute-start(bf16[2048,256]{1,0:T(8,128)(2,1)S(1)} %get-tuple-element.14), channel_id=1, source_target_pairs={{0,16},{16,256},{256,272},{272,0},{1,17},{17,257},{257,273},{273,1... | collective-permute-start | bytes 3145736 | tf_op jit(solution)/shard_map/ppermute | solution.py:222
  41.6 3.4 %collective-permute-start.4 = (bf16[2048,256]{1,0:T(8,128)(2,1)S(1)}, bf16[2048,256]{1,0:T(8,128)(2,1)}, u32[]{:S(2)}, u32[]{:S(2)}) collective-permute-start(bf16[2048,256]{1,0:T(8,128)(2,1)S(1)} %get-tuple-element.13), channel_id=1, source_target_pairs={{0,272},{16,0},{256,16},{272,256},{1,273},{17,1},{257,17},{273,257... | collective-permute-start | bytes 3145736 | tf_op jit(solution)/shard_map/ppermute | solution.py:225
  45.0 0.1 pad_add_fusion.place_ref
  45.1 0.0 collective-permute-done.x_ref
  45.1 0.0 collective-permute-done.1.z_ref
  45.1 0.0 collective-permute-done.2.xz_ref
  45.1 0.0 copy-done.2
  45.1 1.8 %shard_map.73 = bf16[4,4,64,256]{3,2,1,0:T(8,128)(2,1)} custom-call(s32[4,1,2]{2,1,0:T(1,128)S(1)} %all-to-all-done.ids_ref, s32[64]{0:T(128)S(1)} %copy-done.2, s32[2]{0:T(128)S(1)} %pad_add_fusion.place_ref, bf16[2,4,64,256]{3,2,1,0:T(8,128)(2,1)S(1)} %pad_maximum_fusion.own_ref, bf16[2,4,64,256]{3,2,1,0:T(8,128)(2,1)S(1)} %collective-permute-done.x_ref, ...), custom_call_target="tpu_custom_call" | custom-call | bytes 2097152 | tf_op jit(solution)/shard_map/pallas_call | solution.py:55
  46.9 3.5 %all-to-all-start.1 = ((bf16[4,4,64,256]{3,2,1,0:T(8,128)(2,1)}), bf16[4,4,64,256]{3,2,1,0:T(8,128)(2,1)S(1)}, u32[]{:S(2)}, u32[]{:S(2)}) async-start(bf16[4,4,64,256]{3,2,1,0:T(8,128)(2,1)} %shard_map.73), calls=%async_computation.1 | async-start | bytes 1048576 | tf_op jit(solution)/shard_map/all_to_all | solution.py:231
  50.4 10.3 %all-to-all-done.1.got_ref = bf16[4,4,64,256]{3,2,1,0:T(8,128)(2,1)S(1)} async-done(((bf16[4,4,64,256]{3,2,1,0:T(8,128)(2,1)}), bf16[4,4,64,256]{3,2,1,0:T(8,128)(2,1)S(1)}, u32[]{:S(2)}, u32[]{:S(2)}) %all-to-all-start.1) | async-done | bytes 524320 | tf_op jit(solution)/shard_map/all_to_all | solution.py:231
  60.8 1.6 %shard_map.74 = f32[256,128]{1,0:T(8,128)} custom-call(s32[2]{0:T(128)S(1)} %copy-done.3, s32[64]{0:T(128)S(1)} %copy-done.2, s32[4]{0:T(128)S(1)} %copy-done.4, s32[1]{0:T(128)} %bitcast.dp_ref, bf16[512,256]{1,0:T(8,128)(2,1)S(1)} %copy-done, bf16[4,4,64,256]{3,2,1,0:T(8,128)(2,1)S(1)} %all-to-all-done.1.got_ref), custom_call_target="tpu_custom_call" | custom-call | flops 16777216 | bytes 1048576 | tf_op jit(solution)/shard_map/pallas_call | solution.py:90
  62.4 14.0 %all-to-all-start.2 = ((f32[32,8,128]{2,1,0:T(8,128)}), f32[32,8,128]{2,1,0:T(8,128)S(1)}, u32[]{:S(2)}, u32[]{:S(2)}) async-start(f32[32,8,128]{2,1,0:T(8,128)} %bitcast.5), calls=%async_computation.2 | async-start | bytes 262144 | tf_op jit(solution)/shard_map/all_to_all | solution.py:234
  76.4 0.0 collective-permute-done.3.wa_ref
  76.4 0.0 collective-permute-done.4.wb_ref
  76.5 0.0 all-gather.2.cloned.1.call-done.t_ref
  76.5 5.1 %shard_map.76 = (bf16[512,256]{1,0:T(8,128)(2,1)}, f32[512,256]{1,0:T(8,128)}) custom-call(s32[1]{0:T(128)} %bitcast.7.half_ref, bf16[512,4096]{1,0:T(8,128)(2,1)} %all-gather.2.cloned.1.call-done.t_ref, bf16[2048,256]{1,0:T(8,128)(2,1)} %collective-permute-done.3.wa_ref, bf16[2048,256]{1,0:T(8,128)(2,1)} %collective-permute-done.4.wb_ref, bf16[8192,256]{1,0:T(8,128)(2,1)} %w_ref), custom_call_target="tpu_custom_call" | custom-call | flops 2147483648 | bytes 10485760 | tf_op jit(solution)/shard_map/pallas_call | solution.py:153
  81.6 3.3 %collective-permute-start.5 = (bf16[512,256]{1,0:T(8,128)(2,1)}, bf16[512,256]{1,0:T(8,128)(2,1)S(1)}, u32[]{:S(2)}, u32[]{:S(2)}) collective-permute-start(bf16[512,256]{1,0:T(8,128)(2,1)} %get-tuple-element.12), channel_id=1, source_target_pairs={{0,16},{16,0},{1,17},{17,1},{2,18},{18,2},{3,19},{19,3},{4,20},{20... | collective-permute-start | bytes 786440 | tf_op jit(solution)/shard_map/ppermute | solution.py:239
  84.9 0.6 all-to-all-done.2.parts_ref
  85.5 14.7 %all_to_all.20 = bf16[32,8,128]{2,1,0:T(8,128)(2,1)S(1)} all-to-all(bf16[32,8,128]{2,1,0:T(8,128)(2,1)S(1)} %shard_map.75), channel_id=1, replica_groups=mesh['xh'=2,'zh'=4,'zl'=2,'xl'=2,'y'=8,'c'=2] {'xl','y','c'}, dimensions={0} | all-to-all | bytes 131072 | tf_op jit(solution)/shard_map/all_to_all | solution.py:235
  100.3 0.0 collective-permute-done.5.recv_ref
  100.3 1.0 copy-done.1
  101.3 1.6 %shard_map.77 = bf16[512,256]{1,0:T(8,128)(2,1)} custom-call(s32[2]{0:T(128)S(1)} %copy-done.3, s32[64]{0:T(128)S(1)} %copy-done.2, s32[4]{0:T(128)S(1)} %copy-done.4, s32[1]{0:T(128)} %bitcast.dp_ref, bf16[256,128]{1,0:T(8,128)(2,1)S(1)} %bitcast.8, bf16[4,4,64,256]{3,2,1,0:T(8,128)(2,1)S(1)} %all-to-all-done.1.got_ref, f32[512,256]{1,0:T(8,128)S(1)} %copy-done.1, ...), custom_call_target="tpu_custom_call" | custom-call | flops 16777216 | bytes 2097152 | tf_op jit(solution)/shard_map/pallas_call | solution.py:190
  (9 shorter events, 0.1 us)
Async XLA Ops:
  6.5 54.2 %copy-start = (bf16[512,256]{1,0:T(8,128)(2,1)S(1)}, bf16[512,256]{1,0:T(8,128)(2,1)}, u32[]{:S(2)}) copy-start(bf16[512,256]{1,0:T(8,128)(2,1)} %tokens_ref.1) | copy-start | bytes 786436
  6.5 54.2 %copy-start.3 = (s32[2]{0:T(128)S(1)}, s32[2]{0:T(128)}, u32[]{:S(2)}) copy-start(s32[2]{0:T(128)} %ids_ref.3) | copy-start | bytes 28
  6.5 38.5 %copy-start.2 = (s32[64]{0:T(128)S(1)}, s32[64]{0:T(128)}, u32[]{:S(2)}) copy-start(s32[64]{0:T(128)} %stored_ref.5) | copy-start | bytes 772
  6.5 54.2 %copy-start.4 = (s32[4]{0:T(128)S(1)}, s32[4]{0:T(128)}, u32[]{:S(2)}) copy-start(s32[4]{0:T(128)} %seg_ref.3) | copy-start | bytes 52
  6.5 69.9 %all-gather.2.cloned.1.call-start = ((), (), s32[]{:S(2)}) async-start(), calls=%async_computation.4 | async-start | bytes 4456448 | tf_op jit(solution)/shard_map/all_gather | solution.py:209
  8.3 36.8 %collective-permute-start = (bf16[2,4,64,256]{3,2,1,0:T(8,128)(2,1)S(1)}, bf16[2,4,64,256]{3,2,1,0:T(8,128)(2,1)S(1)}, u32[]{:S(2)}, u32[]{:S(2)}) collective-permute-start(bf16[2,4,64,256]{3,2,1,0:T(8,128)(2,1)S(1)} %pad_maximum_fusion.own_ref), channel_id=1, source_target_pairs={{0,256},{32,288},{256,0},{288,32},{1,257},{33,289},{257,1},{289,33... | collective-permute-start | bytes 786440 | tf_op jit(solution)/shard_map/ppermute | solution.py:216
  13.8 31.3 %collective-permute-start.1 = (bf16[2,4,64,256]{3,2,1,0:T(8,128)(2,1)S(1)}, bf16[2,4,64,256]{3,2,1,0:T(8,128)(2,1)S(1)}, u32[]{:S(2)}, u32[]{:S(2)}) collective-permute-start(bf16[2,4,64,256]{3,2,1,0:T(8,128)(2,1)S(1)} %pad_maximum_fusion.own_ref), channel_id=1, source_target_pairs={{0,32},{32,0},{256,288},{288,256},{1,33},{33,1},{257,289},{289,257... | collective-permute-start | bytes 786440 | tf_op jit(solution)/shard_map/ppermute | solution.py:216
  17.8 27.3 %collective-permute-start.2 = (bf16[2,4,64,256]{3,2,1,0:T(8,128)(2,1)S(1)}, bf16[2,4,64,256]{3,2,1,0:T(8,128)(2,1)S(1)}, u32[]{:S(2)}, u32[]{:S(2)}) collective-permute-start(bf16[2,4,64,256]{3,2,1,0:T(8,128)(2,1)S(1)} %pad_maximum_fusion.own_ref), channel_id=1, source_target_pairs={{0,288},{32,256},{256,32},{288,0},{1,289},{33,257},{257,33},{289,1... | collective-permute-start | bytes 786440 | tf_op jit(solution)/shard_map/ppermute | solution.py:216
  20.9 15.8 %all-to-all-start = ((s32[4,1,2]{2,1,0:T(1,128)}), s32[4,1,2]{2,1,0:T(1,128)S(1)}, u32[]{:S(2)}, u32[]{:S(2)}) async-start(s32[4,1,2]{2,1,0:T(1,128)} %broadcast_in_dim.13), calls=%async_computation | async-start | bytes 4096 | tf_op jit(solution)/shard_map/all_to_all | solution.py:211
  38.5 38.0 %collective-permute-start.3 = (bf16[2048,256]{1,0:T(8,128)(2,1)S(1)}, bf16[2048,256]{1,0:T(8,128)(2,1)}, u32[]{:S(2)}, u32[]{:S(2)}) collective-permute-start(bf16[2048,256]{1,0:T(8,128)(2,1)S(1)} %get-tuple-element.14), channel_id=1, source_target_pairs={{0,16},{16,256},{256,272},{272,0},{1,17},{17,257},{257,273},{273,1... | collective-permute-start | bytes 3145736 | tf_op jit(solution)/shard_map/ppermute | solution.py:222
  41.6 34.9 %collective-permute-start.4 = (bf16[2048,256]{1,0:T(8,128)(2,1)S(1)}, bf16[2048,256]{1,0:T(8,128)(2,1)}, u32[]{:S(2)}, u32[]{:S(2)}) collective-permute-start(bf16[2048,256]{1,0:T(8,128)(2,1)S(1)} %get-tuple-element.13), channel_id=1, source_target_pairs={{0,272},{16,0},{256,16},{272,256},{1,273},{17,1},{257,17},{273,257... | collective-permute-start | bytes 3145736 | tf_op jit(solution)/shard_map/ppermute | solution.py:225
  46.9 13.8 %all-to-all-start.1 = ((bf16[4,4,64,256]{3,2,1,0:T(8,128)(2,1)}), bf16[4,4,64,256]{3,2,1,0:T(8,128)(2,1)S(1)}, u32[]{:S(2)}, u32[]{:S(2)}) async-start(bf16[4,4,64,256]{3,2,1,0:T(8,128)(2,1)} %shard_map.73), calls=%async_computation.1 | async-start | bytes 1048576 | tf_op jit(solution)/shard_map/all_to_all | solution.py:231
  62.4 23.1 %all-to-all-start.2 = ((f32[32,8,128]{2,1,0:T(8,128)}), f32[32,8,128]{2,1,0:T(8,128)S(1)}, u32[]{:S(2)}, u32[]{:S(2)}) async-start(f32[32,8,128]{2,1,0:T(8,128)} %bitcast.5), calls=%async_computation.2 | async-start | bytes 262144 | tf_op jit(solution)/shard_map/all_to_all | solution.py:234
  81.6 18.7 %collective-permute-start.5 = (bf16[512,256]{1,0:T(8,128)(2,1)}, bf16[512,256]{1,0:T(8,128)(2,1)S(1)}, u32[]{:S(2)}, u32[]{:S(2)}) collective-permute-start(bf16[512,256]{1,0:T(8,128)(2,1)} %get-tuple-element.12), channel_id=1, source_target_pairs={{0,16},{16,0},{1,17},{17,1},{2,18},{18,2},{3,19},{19,3},{4,20},{20... | collective-permute-start | bytes 786440 | tf_op jit(solution)/shard_map/ppermute | solution.py:239
  100.3 1.0 copy-start.1
Sparse Core Ops, SparseCore 0:
  9.4 58.5 all-gather.1

commit v5 on v4

--- a/solution.py
+++ b/solution.py
@@ -208,10 +208,9 @@
 
     gathered = lax.all_gather(tokens, ("y", "c"), axis=1, tiled=True)
 
-    every_id = lax.all_to_all(
-        jnp.broadcast_to(request_ids[None, None, :], (PEERS, 1, 2)), "zh", 0, 0, tiled=True
-    )
-    own = jnp.stack([down, up])
+    spread = jnp.broadcast_to(request_ids[None, None, :], (PEERS, 1, 2))
+    every_id = lax.all_to_all(spread, "zh", 0, 0, tiled=True)
+    own, _ = lax.optimization_barrier((jnp.stack([down, up]), spread))
     pair = ("xh", "zl")
     far = [lax.ppermute(own, pair, [(i, i ^ flip) for i in range(4)]) for flip in (2, 1, 3)]
 

time: 110 us -> 110 us (level)
  waiting for transfers between devices: 18.2 us -> 11.3 us
  starting transfers between devices: 48 us -> 54.4 us
    all_to_all x1, waiting for transfers between devices: 6.52 us -> 0.01 us  [body(): every_id = lax.all_to_all(spread, 'zh', 0, 0, tiled=True)]
    all_to_all x1, starting transfers between devices: 14 us -> 17.4 us  [body(): parts = lax.all_to_all(partial.reshape(32, 8, 128), TENSOR, 0, 0)]
    all_to_all x1, starting transfers between devices: 3.47 us -> 6.43 us  [body(): got = lax.all_to_all(sent, 'zh', 0, 0, tiled=True)]
    all_to_all x1, starting transfers between devices: 9.32 us -> 10.8 us  [body(): every_id = lax.all_to_all(spread, 'zh', 0, 0, tiled=True)]
    ppermute x3, starting transfers between devices: 11.4 us -> 9.88 us  [body(): lax.ppermute(own, pair, [(i, i ^ flip) for i in range(4)])]
where the time goes in v5:
time: 110 us; the launch traced here: 109 us
  starting transfers between devices  54.4 us (49%)
  blocking collectives  14.7 us (13%)
  between operations  13.6 us (12%)
  waiting for transfers between devices  11.3 us (10%)
  Pallas kernels  10.2 us (9%)
  local copies, waits for them, and re-layouts  3.97 us (4%)
    all_to_all x1, starting transfers between devices, body(): parts = lax.all_to_all(partial.reshape(32, 8, 128), TENSOR, 0, 0)  17.4 us
    all_to_all x1, blocking collectives, body(): low = lax.all_to_all(sum_parts(parts), TENSOR, 0, 0)  14.7 us
    all_to_all x1, starting transfers between devices, body(): every_id = lax.all_to_all(spread, 'zh', 0, 0, tiled=True)  10.8 us
    ppermute x3, starting transfers between devices, body(): lax.ppermute(own, pair, [(i, i ^ flip) for i in range(4)])  9.88 us
    all_to_all x1, waiting for transfers between devices, body(): got = lax.all_to_all(sent, 'zh', 0, 0, tiled=True)  9.69 us
    all_to_all x1, starting transfers between devices, body(): got = lax.all_to_all(sent, 'zh', 0, 0, tiled=True)  6.43 us
    pallas_call x1, Pallas kernels, base_products(): pl.pallas_call(base_kernel, out_shape=[jax.ShapeDtypeStruct((ROWS, WIDTH)...  5.08 us
    ppermute x1, starting transfers between devices, body(): lax.ppermute(lax.dynamic_slice_in_dim(late_weight, start + quarter, quart...  3.37 us
  transfers between devices with their start and end apart: 10, of which 3 were waited for; matrix products, arithmetic and copies ran while one was open for 4% of the time, Pallas kernels for 8%

profile of v5, /device:TPU:1, one launch (start us, length us, event | category | flops | bytes accessed | tf_op | source)
XLA Modules:
  0.0 109.2 jit_solution(1546044612573878552)
XLA Ops:
  6.5 0.0 all-gather.2.cloned.1.call-start
  6.6 0.7 all-gather.2.cloned.1.call-update
  7.3 1.2 %broadcast_in_dim.13 = s32[4,1,2]{2,1,0:T(1,128)} broadcast(s32[2]{0:T(128)} %ids_ref.3), dimensions={2} | broadcast | bytes 40 | tf_op jit(solution)/shard_map/broadcast_in_dim | solution.py:211
  8.5 10.8 %all-to-all-start = ((s32[4,1,2]{2,1,0:T(1,128)}), s32[4,1,2]{2,1,0:T(1,128)S(1)}, u32[]{:S(2)}, u32[]{:S(2)}) async-start(s32[4,1,2]{2,1,0:T(1,128)} %broadcast_in_dim.13), calls=%async_computation | async-start | bytes 4096 | tf_op jit(solution)/shard_map/all_to_all | solution.py:212
  19.4 1.0 pad_maximum_fusion.own_ref
  20.4 4.7 %collective-permute-start = (bf16[2,4,64,256]{3,2,1,0:T(8,128)(2,1)S(1)}, bf16[2,4,64,256]{3,2,1,0:T(8,128)(2,1)S(1)}, u32[]{:S(2)}, u32[]{:S(2)}) collective-permute-start(bf16[2,4,64,256]{3,2,1,0:T(8,128)(2,1)S(1)} %pad_maximum_fusion.own_ref), channel_id=1, source_target_pairs={{0,256},{32,288},{256,0},{288,32},{1,257},{33,289},{257,1},{289,33... | collective-permute-start | bytes 786440 | tf_op jit(solution)/shard_map/ppermute | solution.py:215
  25.0 3.1 %collective-permute-start.1 = (bf16[2,4,64,256]{3,2,1,0:T(8,128)(2,1)S(1)}, bf16[2,4,64,256]{3,2,1,0:T(8,128)(2,1)S(1)}, u32[]{:S(2)}, u32[]{:S(2)}) collective-permute-start(bf16[2,4,64,256]{3,2,1,0:T(8,128)(2,1)S(1)} %pad_maximum_fusion.own_ref), channel_id=1, source_target_pairs={{0,32},{32,0},{256,288},{288,256},{1,33},{33,1},{257,289},{289,257... | collective-permute-start | bytes 786440 | tf_op jit(solution)/shard_map/ppermute | solution.py:215
  28.1 2.1 %collective-permute-start.2 = (bf16[2,4,64,256]{3,2,1,0:T(8,128)(2,1)S(1)}, bf16[2,4,64,256]{3,2,1,0:T(8,128)(2,1)S(1)}, u32[]{:S(2)}, u32[]{:S(2)}) collective-permute-start(bf16[2,4,64,256]{3,2,1,0:T(8,128)(2,1)S(1)} %pad_maximum_fusion.own_ref), channel_id=1, source_target_pairs={{0,288},{32,256},{256,32},{288,0},{1,289},{33,257},{257,33},{289,1... | collective-permute-start | bytes 786440 | tf_op jit(solution)/shard_map/ppermute | solution.py:215
  30.3 0.0 all-to-all-done.ids_ref
  30.3 1.7 %constant_dynamic-slice_fusion = (bf16[2048,256]{1,0:T(8,128)(2,1)S(1)}, bf16[2048,256]{1,0:T(8,128)(2,1)S(1)}) fusion(bf16[8192,256]{1,0:T(8,128)(2,1)} %w_ref, s32[]{:T(128)S(6)} %select_n.7, s32[]{:T(128)S(6)} %select_n.6), kind=kLoop, calls=%fused_computation.2 | loop fusion | bytes 4194312 | tf_op jit(solution)/shard_map/dynamic_slice | solution.py:225
  32.0 3.1 %collective-permute-start.3 = (bf16[2048,256]{1,0:T(8,128)(2,1)S(1)}, bf16[2048,256]{1,0:T(8,128)(2,1)}, u32[]{:S(2)}, u32[]{:S(2)}) collective-permute-start(bf16[2048,256]{1,0:T(8,128)(2,1)S(1)} %get-tuple-element.16), channel_id=1, source_target_pairs={{0,16},{16,256},{256,272},{272,0},{1,17},{17,257},{257,273},{273,1... | collective-permute-start | bytes 3145736 | tf_op jit(solution)/shard_map/ppermute | solution.py:221
  35.1 3.4 %collective-permute-start.4 = (bf16[2048,256]{1,0:T(8,128)(2,1)S(1)}, bf16[2048,256]{1,0:T(8,128)(2,1)}, u32[]{:S(2)}, u32[]{:S(2)}) collective-permute-start(bf16[2048,256]{1,0:T(8,128)(2,1)S(1)} %get-tuple-element.15), channel_id=1, source_target_pairs={{0,272},{16,0},{256,16},{272,256},{1,273},{17,1},{257,17},{273,257... | collective-permute-start | bytes 3145736 | tf_op jit(solution)/shard_map/ppermute | solution.py:224
  38.5 0.1 pad_add_fusion.place_ref
  38.5 0.0 collective-permute-done.x_ref
  38.6 0.0 collective-permute-done.1.z_ref
  38.6 0.2 collective-permute-done.2.xz_ref
  38.8 1.8 %shard_map.73 = bf16[4,4,64,256]{3,2,1,0:T(8,128)(2,1)} custom-call(s32[4,1,2]{2,1,0:T(1,128)S(1)} %all-to-all-done.ids_ref, s32[64]{0:T(128)S(1)} %copy-done.2, s32[2]{0:T(128)S(1)} %pad_add_fusion.place_ref, bf16[2,4,64,256]{3,2,1,0:T(8,128)(2,1)S(1)} %pad_maximum_fusion.own_ref, bf16[2,4,64,256]{3,2,1,0:T(8,128)(2,1)S(1)} %collective-permute-done.x_ref, ...), custom_call_target="tpu_custom_call" | custom-call | bytes 2097152 | tf_op jit(solution)/shard_map/pallas_call | solution.py:55
  40.6 6.4 %all-to-all-start.1 = ((bf16[4,4,64,256]{3,2,1,0:T(8,128)(2,1)}), bf16[4,4,64,256]{3,2,1,0:T(8,128)(2,1)S(1)}, u32[]{:S(2)}, u32[]{:S(2)}) async-start(bf16[4,4,64,256]{3,2,1,0:T(8,128)(2,1)} %shard_map.73), calls=%async_computation.1 | async-start | bytes 1048576 | tf_op jit(solution)/shard_map/all_to_all | solution.py:230
  47.1 9.7 %all-to-all-done.1.got_ref = bf16[4,4,64,256]{3,2,1,0:T(8,128)(2,1)S(1)} async-done(((bf16[4,4,64,256]{3,2,1,0:T(8,128)(2,1)}), bf16[4,4,64,256]{3,2,1,0:T(8,128)(2,1)S(1)}, u32[]{:S(2)}, u32[]{:S(2)}) %all-to-all-start.1) | async-done | bytes 524320 | tf_op jit(solution)/shard_map/all_to_all | solution.py:230
  56.8 0.0 copy-done.3
  56.8 1.6 %shard_map.74 = f32[256,128]{1,0:T(8,128)} custom-call(s32[2]{0:T(128)S(1)} %copy-done.3, s32[64]{0:T(128)S(1)} %copy-done.2, s32[4]{0:T(128)S(1)} %copy-done.4, s32[1]{0:T(128)} %bitcast.dp_ref, bf16[512,256]{1,0:T(8,128)(2,1)S(1)} %copy-done, bf16[4,4,64,256]{3,2,1,0:T(8,128)(2,1)S(1)} %all-to-all-done.1.got_ref), custom_call_target="tpu_custom_call" | custom-call | flops 16777216 | bytes 1048576 | tf_op jit(solution)/shard_map/pallas_call | solution.py:90
  58.4 17.4 %all-to-all-start.2 = ((f32[32,8,128]{2,1,0:T(8,128)}), f32[32,8,128]{2,1,0:T(8,128)S(1)}, u32[]{:S(2)}, u32[]{:S(2)}) async-start(f32[32,8,128]{2,1,0:T(8,128)} %bitcast.5), calls=%async_computation.2 | async-start | bytes 262144 | tf_op jit(solution)/shard_map/all_to_all | solution.py:233
  75.8 0.0 collective-permute-done.3.wa_ref
  75.9 0.0 collective-permute-done.4.wb_ref
  75.9 0.0 all-gather.2.cloned.1.call-done.t_ref
  75.9 5.1 %shard_map.76 = (bf16[512,256]{1,0:T(8,128)(2,1)}, f32[512,256]{1,0:T(8,128)}) custom-call(s32[1]{0:T(128)} %bitcast.7.half_ref, bf16[512,4096]{1,0:T(8,128)(2,1)} %all-gather.2.cloned.1.call-done.t_ref, bf16[2048,256]{1,0:T(8,128)(2,1)} %collective-permute-done.3.wa_ref, bf16[2048,256]{1,0:T(8,128)(2,1)} %collective-permute-done.4.wb_ref, bf16[8192,256]{1,0:T(8,128)(2,1)} %w_ref), custom_call_target="tpu_custom_call" | custom-call | flops 2147483648 | bytes 10485760 | tf_op jit(solution)/shard_map/pallas_call | solution.py:153
  81.0 3.3 %collective-permute-start.5 = (bf16[512,256]{1,0:T(8,128)(2,1)}, bf16[512,256]{1,0:T(8,128)(2,1)S(1)}, u32[]{:S(2)}, u32[]{:S(2)}) collective-permute-start(bf16[512,256]{1,0:T(8,128)(2,1)} %get-tuple-element.14), channel_id=1, source_target_pairs={{0,16},{16,0},{1,17},{17,1},{2,18},{18,2},{3,19},{19,3},{4,20},{20... | collective-permute-start | bytes 786440 | tf_op jit(solution)/shard_map/ppermute | solution.py:238
  84.3 0.6 all-to-all-done.2.parts_ref
  85.0 14.7 %all_to_all.20 = bf16[32,8,128]{2,1,0:T(8,128)(2,1)S(1)} all-to-all(bf16[32,8,128]{2,1,0:T(8,128)(2,1)S(1)} %shard_map.75), channel_id=1, replica_groups=mesh['xh'=2,'zh'=4,'zl'=2,'xl'=2,'y'=8,'c'=2] {'xl','y','c'}, dimensions={0} | all-to-all | bytes 131072 | tf_op jit(solution)/shard_map/all_to_all | solution.py:234
  99.7 0.0 collective-permute-done.5.recv_ref
  99.7 1.0 copy-done.1
  100.7 1.6 %shard_map.77 = bf16[512,256]{1,0:T(8,128)(2,1)} custom-call(s32[2]{0:T(128)S(1)} %copy-done.3, s32[64]{0:T(128)S(1)} %copy-done.2, s32[4]{0:T(128)S(1)} %copy-done.4, s32[1]{0:T(128)} %bitcast.dp_ref, bf16[256,128]{1,0:T(8,128)(2,1)S(1)} %bitcast.8, bf16[4,4,64,256]{3,2,1,0:T(8,128)(2,1)S(1)} %all-to-all-done.1.got_ref, f32[512,256]{1,0:T(8,128)S(1)} %copy-done.1, ...), custom_call_target="tpu_custom_call" | custom-call | flops 16777216 | bytes 2097152 | tf_op jit(solution)/shard_map/pallas_call | solution.py:190
  (9 shorter events, 0.1 us)
Async XLA Ops:
  6.5 50.2 %copy-start = (bf16[512,256]{1,0:T(8,128)(2,1)S(1)}, bf16[512,256]{1,0:T(8,128)(2,1)}, u32[]{:S(2)}) copy-start(bf16[512,256]{1,0:T(8,128)(2,1)} %tokens_ref.1) | copy-start | bytes 786436
  6.5 50.2 %copy-start.3 = (s32[2]{0:T(128)S(1)}, s32[2]{0:T(128)}, u32[]{:S(2)}) copy-start(s32[2]{0:T(128)} %ids_ref.3) | copy-start | bytes 28
  6.5 32.3 %copy-start.2 = (s32[64]{0:T(128)S(1)}, s32[64]{0:T(128)}, u32[]{:S(2)}) copy-start(s32[64]{0:T(128)} %stored_ref.5) | copy-start | bytes 772
  6.5 50.2 %copy-start.4 = (s32[4]{0:T(128)S(1)}, s32[4]{0:T(128)}, u32[]{:S(2)}) copy-start(s32[4]{0:T(128)} %seg_ref.3) | copy-start | bytes 52
  6.5 69.3 %all-gather.2.cloned.1.call-start = ((), (), s32[]{:S(2)}) async-start(), calls=%async_computation.4 | async-start | bytes 4456448 | tf_op jit(solution)/shard_map/all_gather | solution.py:209
  8.5 21.8 %all-to-all-start = ((s32[4,1,2]{2,1,0:T(1,128)}), s32[4,1,2]{2,1,0:T(1,128)S(1)}, u32[]{:S(2)}, u32[]{:S(2)}) async-start(s32[4,1,2]{2,1,0:T(1,128)} %broadcast_in_dim.13), calls=%async_computation | async-start | bytes 4096 | tf_op jit(solution)/shard_map/all_to_all | solution.py:212
  20.4 18.2 %collective-permute-start = (bf16[2,4,64,256]{3,2,1,0:T(8,128)(2,1)S(1)}, bf16[2,4,64,256]{3,2,1,0:T(8,128)(2,1)S(1)}, u32[]{:S(2)}, u32[]{:S(2)}) collective-permute-start(bf16[2,4,64,256]{3,2,1,0:T(8,128)(2,1)S(1)} %pad_maximum_fusion.own_ref), channel_id=1, source_target_pairs={{0,256},{32,288},{256,0},{288,32},{1,257},{33,289},{257,1},{289,33... | collective-permute-start | bytes 786440 | tf_op jit(solution)/shard_map/ppermute | solution.py:215
  25.0 13.5 %collective-permute-start.1 = (bf16[2,4,64,256]{3,2,1,0:T(8,128)(2,1)S(1)}, bf16[2,4,64,256]{3,2,1,0:T(8,128)(2,1)S(1)}, u32[]{:S(2)}, u32[]{:S(2)}) collective-permute-start(bf16[2,4,64,256]{3,2,1,0:T(8,128)(2,1)S(1)} %pad_maximum_fusion.own_ref), channel_id=1, source_target_pairs={{0,32},{32,0},{256,288},{288,256},{1,33},{33,1},{257,289},{289,257... | collective-permute-start | bytes 786440 | tf_op jit(solution)/shard_map/ppermute | solution.py:215
  28.1 10.7 %collective-permute-start.2 = (bf16[2,4,64,256]{3,2,1,0:T(8,128)(2,1)S(1)}, bf16[2,4,64,256]{3,2,1,0:T(8,128)(2,1)S(1)}, u32[]{:S(2)}, u32[]{:S(2)}) collective-permute-start(bf16[2,4,64,256]{3,2,1,0:T(8,128)(2,1)S(1)} %pad_maximum_fusion.own_ref), channel_id=1, source_target_pairs={{0,288},{32,256},{256,32},{288,0},{1,289},{33,257},{257,33},{289,1... | collective-permute-start | bytes 786440 | tf_op jit(solution)/shard_map/ppermute | solution.py:215
  32.0 43.9 %collective-permute-start.3 = (bf16[2048,256]{1,0:T(8,128)(2,1)S(1)}, bf16[2048,256]{1,0:T(8,128)(2,1)}, u32[]{:S(2)}, u32[]{:S(2)}) collective-permute-start(bf16[2048,256]{1,0:T(8,128)(2,1)S(1)} %get-tuple-element.16), channel_id=1, source_target_pairs={{0,16},{16,256},{256,272},{272,0},{1,17},{17,257},{257,273},{273,1... | collective-permute-start | bytes 3145736 | tf_op jit(solution)/shard_map/ppermute | solution.py:221
  35.1 40.8 %collective-permute-start.4 = (bf16[2048,256]{1,0:T(8,128)(2,1)S(1)}, bf16[2048,256]{1,0:T(8,128)(2,1)}, u32[]{:S(2)}, u32[]{:S(2)}) collective-permute-start(bf16[2048,256]{1,0:T(8,128)(2,1)S(1)} %get-tuple-element.15), channel_id=1, source_target_pairs={{0,272},{16,0},{256,16},{272,256},{1,273},{17,1},{257,17},{273,257... | collective-permute-start | bytes 3145736 | tf_op jit(solution)/shard_map/ppermute | solution.py:224
  40.6 16.1 %all-to-all-start.1 = ((bf16[4,4,64,256]{3,2,1,0:T(8,128)(2,1)}), bf16[4,4,64,256]{3,2,1,0:T(8,128)(2,1)S(1)}, u32[]{:S(2)}, u32[]{:S(2)}) async-start(bf16[4,4,64,256]{3,2,1,0:T(8,128)(2,1)} %shard_map.73), calls=%async_computation.1 | async-start | bytes 1048576 | tf_op jit(solution)/shard_map/all_to_all | solution.py:230
  58.4 26.5 %all-to-all-start.2 = ((f32[32,8,128]{2,1,0:T(8,128)}), f32[32,8,128]{2,1,0:T(8,128)S(1)}, u32[]{:S(2)}, u32[]{:S(2)}) async-start(f32[32,8,128]{2,1,0:T(8,128)} %bitcast.5), calls=%async_computation.2 | async-start | bytes 262144 | tf_op jit(solution)/shard_map/all_to_all | solution.py:233
  81.0 18.7 %collective-permute-start.5 = (bf16[512,256]{1,0:T(8,128)(2,1)}, bf16[512,256]{1,0:T(8,128)(2,1)S(1)}, u32[]{:S(2)}, u32[]{:S(2)}) collective-permute-start(bf16[512,256]{1,0:T(8,128)(2,1)} %get-tuple-element.14), channel_id=1, source_target_pairs={{0,16},{16,0},{1,17},{17,1},{2,18},{18,2},{3,19},{19,3},{4,20},{20... | collective-permute-start | bytes 786440 | tf_op jit(solution)/shard_map/ppermute | solution.py:238
  99.7 1.0 copy-start.1
Sparse Core Ops, SparseCore 0:
  9.4 58.3 all-gather.1

commit v6 on v5

--- a/solution.py
+++ b/solution.py
@@ -16,6 +16,7 @@
 OWNED = 4
 ZS = 8
 PEERS = 4
+SUM_TYPE = jnp.float32
 HALF = 4096
 DEPTH = 1024
 
@@ -30,25 +31,20 @@
 
 def select_kernel(ids_ref, stored_ref, place_ref, own_ref, x_ref, z_ref, xz_ref, out_ref):
     held = (own_ref, x_ref, z_ref, xz_ref)
-
-    def step(i, carry):
-        zh, r = i // 2, i % 2
-        row = stored_ref[ids_ref[zh, 0, r]]
-        slot = row % OWNED
-        owner = row // OWNED
-        across_x = owner // ZS != place_ref[0]
-        across_z = owner % 2 != place_ref[1]
-        which = across_x.astype(jnp.int32) + 2 * across_z.astype(jnp.int32)
-        for j in range(4):
-
-            @pl.when(which == j)
-            def _():
-                for part in range(2):
-                    out_ref[zh, 2 * r + part] = held[j][part, slot]
-
-        return carry
-
-    lax.fori_loop(0, 2 * PEERS, step, 0)
+    for zh in range(PEERS):
+        for r in range(2):
+            row = stored_ref[ids_ref[zh, 0, r]]
+            slot = row % OWNED
+            owner = row // OWNED
+            across_x = owner // ZS != place_ref[0]
+            across_z = owner % 2 != place_ref[1]
+            which = across_x.astype(jnp.int32) + 2 * across_z.astype(jnp.int32)
+            for j in range(4):
+
+                @pl.when(which == j)
+                def _(zh=zh, r=r, slot=slot, j=j):
+                    for part in range(2):
+                        out_ref[zh, 2 * r + part] = held[j][part, slot]
 
 
 def select(ids, stored, place, own, x, z, xz):
@@ -72,8 +68,13 @@
     return copies
 
 
-def down_kernel(ids_ref, stored_ref, seg_ref, dp_ref, tokens_ref, got_ref, out_ref, mats, sems):
-    for copy in fetch(ids_ref, stored_ref, got_ref, mats, sems, 0):
+def down_kernel(
+    ids_ref, stored_ref, seg_ref, dp_ref, tokens_ref, got_ref, out_ref, ups_ref,
+    mats, ups, sems, up_sems,
+):
+    copies = fetch(ids_ref, stored_ref, got_ref, mats, sems, 0)
+    up_copies = fetch(ids_ref, stored_ref, got_ref, ups, up_sems, 1)
+    for copy in copies:
         copy.wait()
     for k in range(4):
         part = lax.dot_general(
@@ -83,18 +84,25 @@
             preferred_element_type=jnp.float32,
         )
         row, col = (k % 2) * SEG, (k // 2) * RANK
-        out_ref[row : row + SEG, col : col + RANK] = part
+        out_ref[row : row + SEG, col : col + RANK] = part.astype(out_ref.dtype)
+    for copy in up_copies:
+        copy.wait()
+    for k in range(4):
+        ups_ref[k] = ups[seg_ref[k] - 2 * dp_ref[0]]
 
 
 def down_product(ids, stored, seg, dp, tokens, got):
+    mats = pltpu.VMEM((2, RANK, WIDTH), jnp.bfloat16)
     return pl.pallas_call(
         down_kernel,
-        out_shape=jax.ShapeDtypeStruct((256, 128), jnp.float32),
+        out_shape=[
+            jax.ShapeDtypeStruct((256, 128), SUM_TYPE),
+            jax.ShapeDtypeStruct((4, RANK, WIDTH), jnp.bfloat16),
+        ],
         in_specs=[SMEM, SMEM, SMEM, SMEM, VMEM, ANY],
-        out_specs=VMEM,
+        out_specs=[VMEM, VMEM],
         scratch_shapes=[
-            pltpu.VMEM((2, RANK, WIDTH), jnp.bfloat16),
-            pltpu.SemaphoreType.DMA((2,)),
+            mats, mats, pltpu.SemaphoreType.DMA((2,)), pltpu.SemaphoreType.DMA((2,))
         ],
         compiler_params=vmem(4),
         cost_estimate=pl.CostEstimate(flops=1 << 24, bytes_accessed=1 << 20, transcendentals=0),
@@ -102,7 +110,7 @@
 
 
 def sum_kernel(parts_ref, out_ref):
-    total = jnp.sum(parts_ref[...], axis=0).astype(jnp.bfloat16)
+    total = jnp.sum(parts_ref[...].astype(jnp.float32), axis=0).astype(jnp.bfloat16)
     out_ref[...] = jnp.broadcast_to(total[None], out_ref.shape)
 
 
@@ -172,33 +180,39 @@
     )(half, gathered, wa, wb, weight)
 
 
-def last_kernel(
-    ids_ref, stored_ref, seg_ref, dp_ref, low_ref, got_ref, ours_ref, recv_ref, out_ref, mats, sems
-):
-    copies = fetch(ids_ref, stored_ref, got_ref, mats, sems, 1)
-    for copy in copies:
-        copy.wait()
+def add_kernel(ours_ref, recv_ref, out_ref):
+    out_ref[...] = ours_ref[...] + recv_ref[...].astype(jnp.float32)
+
+
+def add(ours, recv):
+    return pl.pallas_call(
+        add_kernel,
+        out_shape=jax.ShapeDtypeStruct((ROWS, WIDTH), jnp.float32),
+        in_specs=[VMEM, VMEM],
+        out_specs=VMEM,
+        compiler_params=vmem(8),
+        cost_estimate=pl.CostEstimate(flops=1 << 17, bytes_accessed=2 << 20, transcendentals=0),
+    )(ours, recv)
+
+
+def last_kernel(low_ref, ups_ref, base_ref, out_ref):
     for k in range(4):
         row, col = (k % 2) * SEG, (k // 2) * RANK
         low = low_ref[row : row + SEG, col : col + RANK]
-        up = jnp.dot(low, mats[seg_ref[k] - 2 * dp_ref[0]], preferred_element_type=jnp.float32)
+        up = jnp.dot(low, ups_ref[k], preferred_element_type=jnp.float32)
         rows = slice(k * SEG, (k + 1) * SEG)
-        out_ref[rows, :] = (ours_ref[rows, :] + recv_ref[rows, :].astype(jnp.float32) + 2.0 * up).astype(jnp.bfloat16)
-
-
-def last_product(ids, stored, seg, dp, low, got, ours, recv):
+        out_ref[rows, :] = (base_ref[rows, :] + 2.0 * up).astype(jnp.bfloat16)
+
+
+def last_product(low, ups, base):
     return pl.pallas_call(
         last_kernel,
         out_shape=jax.ShapeDtypeStruct((ROWS, WIDTH), jnp.bfloat16),
-        in_specs=[SMEM, SMEM, SMEM, SMEM, VMEM, ANY, VMEM, VMEM],
-        out_specs=VMEM,
-        scratch_shapes=[
-            pltpu.VMEM((2, RANK, WIDTH), jnp.bfloat16),
-            pltpu.SemaphoreType.DMA((2,)),
-        ],
+        in_specs=[VMEM, VMEM, VMEM],
+        out_specs=VMEM,
         compiler_params=vmem(8),
         cost_estimate=pl.CostEstimate(flops=1 << 24, bytes_accessed=2 << 20, transcendentals=0),
-    )(ids, stored, seg, dp, low, got, ours, recv)
+    )(low, ups, base)
 
 
 def body(tokens, weight, down, up, segment_request, request_ids, stored_row):
@@ -229,16 +243,14 @@
 
     got = lax.all_to_all(sent, "zh", 0, 0, tiled=True)
 
-    partial = down_product(request_ids, stored_row, segment_request, dp, tokens, got)
+    partial, ups = down_product(request_ids, stored_row, segment_request, dp, tokens, got)
     parts = lax.all_to_all(partial.reshape(32, 8, 128), TENSOR, 0, 0)
     low = lax.all_to_all(sum_parts(parts), TENSOR, 0, 0)
 
     weight, _ = lax.optimization_barrier((weight, partial))
     theirs, ours = base_products(xl[None], gathered, wa, wb, weight)
     recv = lax.ppermute(theirs, "xl", SWAP)
-    return last_product(
-        request_ids, stored_row, segment_request, dp, low.reshape(256, 128), got, ours, recv
-    )
+    return last_product(low.reshape(256, 128), ups, add(ours, recv))
 
 
 def solution(mesh):

time: 110 us -> 109 us (level)
  blocking collectives: 14.7 us -> 0 us
  starting transfers between devices: 54.4 us -> 61.3 us
  waiting for transfers between devices: 11.3 us -> 18.2 us
    all_to_all x1 -> x0, blocking collectives: 14.7 us -> none  [body(): low = lax.all_to_all(sum_parts(parts), TENSOR, 0, 0)]
    all_to_all x0 -> x1, waiting for transfers between devices: none -> 6.97 us  [body(): low = lax.all_to_all(sum_parts(parts), TENSOR, 0, 0)]
    all_to_all x0 -> x1, starting transfers between devices: none -> 6.87 us  [body(): low = lax.all_to_all(sum_parts(parts), TENSOR, 0, 0)]
  transfers between devices with their start and end apart: 10 -> 11, of which waited for: 3 -> 4; matrix products, arithmetic and copies ran while one was open for 4% -> 4% of each run, Pallas kernels for 8% -> 9%
where the time goes in v6:
time: 109 us; the launch traced here: 108 us
  starting transfers between devices  61.3 us (56%)
  waiting for transfers between devices  18.2 us (17%)
  between operations  13.6 us (12%)
  Pallas kernels  10.3 us (9%)
  local copies, waits for them, and re-layouts  3.97 us (4%)
    all_to_all x1, starting transfers between devices, body(): parts = lax.all_to_all(partial.reshape(32, 8, 128), TENSOR, 0, 0)  17.4 us
    all_to_all x1, starting transfers between devices, body(): every_id = lax.all_to_all(spread, 'zh', 0, 0, tiled=True)  10.8 us
    ppermute x3, starting transfers between devices, body(): lax.ppermute(own, pair, [(i, i ^ flip) for i in range(4)])  9.88 us
    all_to_all x1, waiting for transfers between devices, body(): got = lax.all_to_all(sent, 'zh', 0, 0, tiled=True)  9.69 us
    all_to_all x1, waiting for transfers between devices, body(): low = lax.all_to_all(sum_parts(parts), TENSOR, 0, 0)  6.97 us
    all_to_all x1, starting transfers between devices, body(): low = lax.all_to_all(sum_parts(parts), TENSOR, 0, 0)  6.87 us
    all_to_all x1, starting transfers between devices, body(): got = lax.all_to_all(sent, 'zh', 0, 0, tiled=True)  6.43 us
    pallas_call x1, Pallas kernels, base_products(): pl.pallas_call(base_kernel, out_shape=[jax.ShapeDtypeStruct((ROWS, WIDTH)...  5.07 us
  transfers between devices with their start and end apart: 11, of which 4 were waited for; matrix products, arithmetic and copies ran while one was open for 4% of the time, Pallas kernels for 9%

profile of v6, /device:TPU:1, one launch (start us, length us, event | category | flops | bytes accessed | tf_op | source)
XLA Modules:
  0.0 108.4 jit_solution(11508357780684972053)
XLA Ops:
  6.5 0.0 all-gather.2.cloned.1.call-start
  6.6 0.7 all-gather.2.cloned.1.call-update
  7.3 1.2 %broadcast_in_dim.13 = s32[4,1,2]{2,1,0:T(1,128)} broadcast(s32[2]{0:T(128)} %ids_ref.1), dimensions={2} | broadcast | bytes 40 | tf_op jit(solution)/shard_map/broadcast_in_dim | solution.py:225
  8.5 10.8 %all-to-all-start = ((s32[4,1,2]{2,1,0:T(1,128)}), s32[4,1,2]{2,1,0:T(1,128)S(1)}, u32[]{:S(2)}, u32[]{:S(2)}) async-start(s32[4,1,2]{2,1,0:T(1,128)} %broadcast_in_dim.13), calls=%async_computation | async-start | bytes 4096 | tf_op jit(solution)/shard_map/all_to_all | solution.py:226
  19.4 1.0 pad_maximum_fusion.own_ref
  20.4 4.7 %collective-permute-start = (bf16[2,4,64,256]{3,2,1,0:T(8,128)(2,1)S(1)}, bf16[2,4,64,256]{3,2,1,0:T(8,128)(2,1)S(1)}, u32[]{:S(2)}, u32[]{:S(2)}) collective-permute-start(bf16[2,4,64,256]{3,2,1,0:T(8,128)(2,1)S(1)} %pad_maximum_fusion.own_ref), channel_id=1, source_target_pairs={{0,256},{32,288},{256,0},{288,32},{1,257},{33,289},{257,1},{289,33... | collective-permute-start | bytes 786440 | tf_op jit(solution)/shard_map/ppermute | solution.py:229
  25.0 3.1 %collective-permute-start.1 = (bf16[2,4,64,256]{3,2,1,0:T(8,128)(2,1)S(1)}, bf16[2,4,64,256]{3,2,1,0:T(8,128)(2,1)S(1)}, u32[]{:S(2)}, u32[]{:S(2)}) collective-permute-start(bf16[2,4,64,256]{3,2,1,0:T(8,128)(2,1)S(1)} %pad_maximum_fusion.own_ref), channel_id=1, source_target_pairs={{0,32},{32,0},{256,288},{288,256},{1,33},{33,1},{257,289},{289,257... | collective-permute-start | bytes 786440 | tf_op jit(solution)/shard_map/ppermute | solution.py:229
  28.1 2.1 %collective-permute-start.2 = (bf16[2,4,64,256]{3,2,1,0:T(8,128)(2,1)S(1)}, bf16[2,4,64,256]{3,2,1,0:T(8,128)(2,1)S(1)}, u32[]{:S(2)}, u32[]{:S(2)}) collective-permute-start(bf16[2,4,64,256]{3,2,1,0:T(8,128)(2,1)S(1)} %pad_maximum_fusion.own_ref), channel_id=1, source_target_pairs={{0,288},{32,256},{256,32},{288,0},{1,289},{33,257},{257,33},{289,1... | collective-permute-start | bytes 786440 | tf_op jit(solution)/shard_map/ppermute | solution.py:229
  30.3 0.0 all-to-all-done.ids_ref
  30.3 1.7 %constant_dynamic-slice_fusion = (bf16[2048,256]{1,0:T(8,128)(2,1)S(1)}, bf16[2048,256]{1,0:T(8,128)(2,1)S(1)}) fusion(bf16[8192,256]{1,0:T(8,128)(2,1)} %w_ref, s32[]{:T(128)S(6)} %select_n.7, s32[]{:T(128)S(6)} %select_n.6), kind=kLoop, calls=%fused_computation.2 | loop fusion | bytes 4194312 | tf_op jit(solution)/shard_map/dynamic_slice | solution.py:239
  32.0 3.1 %collective-permute-start.3 = (bf16[2048,256]{1,0:T(8,128)(2,1)S(1)}, bf16[2048,256]{1,0:T(8,128)(2,1)}, u32[]{:S(2)}, u32[]{:S(2)}) collective-permute-start(bf16[2048,256]{1,0:T(8,128)(2,1)S(1)} %get-tuple-element.20), channel_id=1, source_target_pairs={{0,16},{16,256},{256,272},{272,0},{1,17},{17,257},{257,273},{273,1... | collective-permute-start | bytes 3145736 | tf_op jit(solution)/shard_map/ppermute | solution.py:235
  35.1 3.4 %collective-permute-start.4 = (bf16[2048,256]{1,0:T(8,128)(2,1)S(1)}, bf16[2048,256]{1,0:T(8,128)(2,1)}, u32[]{:S(2)}, u32[]{:S(2)}) collective-permute-start(bf16[2048,256]{1,0:T(8,128)(2,1)S(1)} %get-tuple-element.19), channel_id=1, source_target_pairs={{0,272},{16,0},{256,16},{272,256},{1,273},{17,1},{257,17},{273,257... | collective-permute-start | bytes 3145736 | tf_op jit(solution)/shard_map/ppermute | solution.py:238
  38.5 0.1 pad_add_fusion.place_ref
  38.5 0.0 collective-permute-done.x_ref
  38.6 0.0 collective-permute-done.1.z_ref
  38.6 0.2 collective-permute-done.2.xz_ref
  38.8 1.7 %shard_map.73 = bf16[4,4,64,256]{3,2,1,0:T(8,128)(2,1)} custom-call(s32[4,1,2]{2,1,0:T(1,128)S(1)} %all-to-all-done.ids_ref, s32[64]{0:T(128)S(1)} %copy-done.2, s32[2]{0:T(128)S(1)} %pad_add_fusion.place_ref, bf16[2,4,64,256]{3,2,1,0:T(8,128)(2,1)S(1)} %pad_maximum_fusion.own_ref, bf16[2,4,64,256]{3,2,1,0:T(8,128)(2,1)S(1)} %collective-permute-done.x_ref, ...), custom_call_target="tpu_custom_call" | custom-call | bytes 2097152 | tf_op jit(solution)/shard_map/pallas_call | solution.py:51
  40.5 6.4 %all-to-all-start.1 = ((bf16[4,4,64,256]{3,2,1,0:T(8,128)(2,1)}), bf16[4,4,64,256]{3,2,1,0:T(8,128)(2,1)S(1)}, u32[]{:S(2)}, u32[]{:S(2)}) async-start(bf16[4,4,64,256]{3,2,1,0:T(8,128)(2,1)} %shard_map.73), calls=%async_computation.1 | async-start | bytes 1048576 | tf_op jit(solution)/shard_map/all_to_all | solution.py:244
  47.0 9.7 %all-to-all-done.1.got_ref = bf16[4,4,64,256]{3,2,1,0:T(8,128)(2,1)S(1)} async-done(((bf16[4,4,64,256]{3,2,1,0:T(8,128)(2,1)}), bf16[4,4,64,256]{3,2,1,0:T(8,128)(2,1)S(1)}, u32[]{:S(2)}, u32[]{:S(2)}) %all-to-all-start.1) | async-done | bytes 524320 | tf_op jit(solution)/shard_map/all_to_all | solution.py:244
  56.7 1.8 %shard_map.74 = (f32[256,128]{1,0:T(8,128)}, bf16[4,64,256]{2,1,0:T(8,128)(2,1)S(1)}) custom-call(s32[2]{0:T(128)S(1)} %copy-done.3, s32[64]{0:T(128)S(1)} %copy-done.2, s32[4]{0:T(128)S(1)} %copy-done.4, s32[1]{0:T(128)} %bitcast.dp_ref, bf16[512,256]{1,0:T(8,128)(2,1)S(1)} %copy-done, bf16[4,4,64,256]{3,2,1,0:T(8,128)(2,1)S(1)} %all-to-all-done.1.got_ref), custom_call_target="tpu_custom_call" | custom-call | flops 16777216 | bytes 1048576 | tf_op jit(solution)/shard_map/pallas_call | solution.py:96
  58.5 17.4 %all-to-all-start.2 = ((f32[32,8,128]{2,1,0:T(8,128)}), f32[32,8,128]{2,1,0:T(8,128)S(1)}, u32[]{:S(2)}, u32[]{:S(2)}) async-start(f32[32,8,128]{2,1,0:T(8,128)} %bitcast.5), calls=%async_computation.2 | async-start | bytes 262144 | tf_op jit(solution)/shard_map/all_to_all | solution.py:247
  75.9 0.0 collective-permute-done.3.wa_ref
  75.9 0.0 collective-permute-done.4.wb_ref
  75.9 0.0 all-gather.2.cloned.1.call-done.t_ref
  76.0 5.1 %shard_map.76 = (bf16[512,256]{1,0:T(8,128)(2,1)}, f32[512,256]{1,0:T(8,128)}) custom-call(s32[1]{0:T(128)} %bitcast.7.half_ref, bf16[512,4096]{1,0:T(8,128)(2,1)} %all-gather.2.cloned.1.call-done.t_ref, bf16[2048,256]{1,0:T(8,128)(2,1)} %collective-permute-done.3.wa_ref, bf16[2048,256]{1,0:T(8,128)(2,1)} %collective-permute-done.4.wb_ref, bf16[8192,256]{1,0:T(8,128)(2,1)} %w_ref), custom_call_target="tpu_custom_call" | custom-call | flops 2147483648 | bytes 10485760 | tf_op jit(solution)/shard_map/pallas_call | solution.py:161
  81.0 3.3 %collective-permute-start.5 = (bf16[512,256]{1,0:T(8,128)(2,1)}, bf16[512,256]{1,0:T(8,128)(2,1)S(1)}, u32[]{:S(2)}, u32[]{:S(2)}) collective-permute-start(bf16[512,256]{1,0:T(8,128)(2,1)} %get-tuple-element.18), channel_id=1, source_target_pairs={{0,16},{16,0},{1,17},{17,1},{2,18},{18,2},{3,19},{19,3},{4,20},{20... | collective-permute-start | bytes 786440 | tf_op jit(solution)/shard_map/ppermute | solution.py:252
  84.3 0.6 all-to-all-done.2.parts_ref
  85.0 0.7 shard_map.75
  85.6 6.9 %all-to-all-start.3 = ((bf16[32,8,128]{2,1,0:T(8,128)(2,1)}), bf16[32,8,128]{2,1,0:T(8,128)(2,1)S(1)}, u32[]{:S(2)}, u32[]{:S(2)}) async-start(bf16[32,8,128]{2,1,0:T(8,128)(2,1)} %shard_map.75), calls=%async_computation.3 | async-start | bytes 131072 | tf_op jit(solution)/shard_map/all_to_all | solution.py:248
  92.5 1.0 copy-done.1
  93.6 7.0 %all-to-all-done.3 = bf16[32,8,128]{2,1,0:T(8,128)(2,1)S(1)} async-done(((bf16[32,8,128]{2,1,0:T(8,128)(2,1)}), bf16[32,8,128]{2,1,0:T(8,128)(2,1)S(1)}, u32[]{:S(2)}, u32[]{:S(2)}) %all-to-all-start.3) | async-done | bytes 65568 | tf_op jit(solution)/shard_map/all_to_all | solution.py:248
  100.6 0.9 shard_map.78
  (11 shorter events, 0.1 us)
Async XLA Ops:
  6.5 50.1 %copy-start = (bf16[512,256]{1,0:T(8,128)(2,1)S(1)}, bf16[512,256]{1,0:T(8,128)(2,1)}, u32[]{:S(2)}) copy-start(bf16[512,256]{1,0:T(8,128)(2,1)} %tokens_ref.1) | copy-start | bytes 786436
  6.5 50.1 %copy-start.3 = (s32[2]{0:T(128)S(1)}, s32[2]{0:T(128)}, u32[]{:S(2)}) copy-start(s32[2]{0:T(128)} %ids_ref.1) | copy-start | bytes 28
  6.5 32.3 %copy-start.2 = (s32[64]{0:T(128)S(1)}, s32[64]{0:T(128)}, u32[]{:S(2)}) copy-start(s32[64]{0:T(128)} %stored_ref.3) | copy-start | bytes 772
  6.5 50.1 %copy-start.4 = (s32[4]{0:T(128)S(1)}, s32[4]{0:T(128)}, u32[]{:S(2)}) copy-start(s32[4]{0:T(128)} %seg_ref.1) | copy-start | bytes 52
  6.5 69.4 %all-gather.2.cloned.1.call-start = ((), (), s32[]{:S(2)}) async-start(), calls=%async_computation.4 | async-start | bytes 4456448 | tf_op jit(solution)/shard_map/all_gather | solution.py:223
  8.5 21.8 %all-to-all-start = ((s32[4,1,2]{2,1,0:T(1,128)}), s32[4,1,2]{2,1,0:T(1,128)S(1)}, u32[]{:S(2)}, u32[]{:S(2)}) async-start(s32[4,1,2]{2,1,0:T(1,128)} %broadcast_in_dim.13), calls=%async_computation | async-start | bytes 4096 | tf_op jit(solution)/shard_map/all_to_all | solution.py:226
  20.4 18.2 %collective-permute-start = (bf16[2,4,64,256]{3,2,1,0:T(8,128)(2,1)S(1)}, bf16[2,4,64,256]{3,2,1,0:T(8,128)(2,1)S(1)}, u32[]{:S(2)}, u32[]{:S(2)}) collective-permute-start(bf16[2,4,64,256]{3,2,1,0:T(8,128)(2,1)S(1)} %pad_maximum_fusion.own_ref), channel_id=1, source_target_pairs={{0,256},{32,288},{256,0},{288,32},{1,257},{33,289},{257,1},{289,33... | collective-permute-start | bytes 786440 | tf_op jit(solution)/shard_map/ppermute | solution.py:229
  25.0 13.5 %collective-permute-start.1 = (bf16[2,4,64,256]{3,2,1,0:T(8,128)(2,1)S(1)}, bf16[2,4,64,256]{3,2,1,0:T(8,128)(2,1)S(1)}, u32[]{:S(2)}, u32[]{:S(2)}) collective-permute-start(bf16[2,4,64,256]{3,2,1,0:T(8,128)(2,1)S(1)} %pad_maximum_fusion.own_ref), channel_id=1, source_target_pairs={{0,32},{32,0},{256,288},{288,256},{1,33},{33,1},{257,289},{289,257... | collective-permute-start | bytes 786440 | tf_op jit(solution)/shard_map/ppermute | solution.py:229
  28.1 10.7 %collective-permute-start.2 = (bf16[2,4,64,256]{3,2,1,0:T(8,128)(2,1)S(1)}, bf16[2,4,64,256]{3,2,1,0:T(8,128)(2,1)S(1)}, u32[]{:S(2)}, u32[]{:S(2)}) collective-permute-start(bf16[2,4,64,256]{3,2,1,0:T(8,128)(2,1)S(1)} %pad_maximum_fusion.own_ref), channel_id=1, source_target_pairs={{0,288},{32,256},{256,32},{288,0},{1,289},{33,257},{257,33},{289,1... | collective-permute-start | bytes 786440 | tf_op jit(solution)/shard_map/ppermute | solution.py:229
  32.0 43.9 %collective-permute-start.3 = (bf16[2048,256]{1,0:T(8,128)(2,1)S(1)}, bf16[2048,256]{1,0:T(8,128)(2,1)}, u32[]{:S(2)}, u32[]{:S(2)}) collective-permute-start(bf16[2048,256]{1,0:T(8,128)(2,1)S(1)} %get-tuple-element.20), channel_id=1, source_target_pairs={{0,16},{16,256},{256,272},{272,0},{1,17},{17,257},{257,273},{273,1... | collective-permute-start | bytes 3145736 | tf_op jit(solution)/shard_map/ppermute | solution.py:235
  35.1 40.8 %collective-permute-start.4 = (bf16[2048,256]{1,0:T(8,128)(2,1)S(1)}, bf16[2048,256]{1,0:T(8,128)(2,1)}, u32[]{:S(2)}, u32[]{:S(2)}) collective-permute-start(bf16[2048,256]{1,0:T(8,128)(2,1)S(1)} %get-tuple-element.19), channel_id=1, source_target_pairs={{0,272},{16,0},{256,16},{272,256},{1,273},{17,1},{257,17},{273,257... | collective-permute-start | bytes 3145736 | tf_op jit(solution)/shard_map/ppermute | solution.py:238
  40.5 16.1 %all-to-all-start.1 = ((bf16[4,4,64,256]{3,2,1,0:T(8,128)(2,1)}), bf16[4,4,64,256]{3,2,1,0:T(8,128)(2,1)S(1)}, u32[]{:S(2)}, u32[]{:S(2)}) async-start(bf16[4,4,64,256]{3,2,1,0:T(8,128)(2,1)} %shard_map.73), calls=%async_computation.1 | async-start | bytes 1048576 | tf_op jit(solution)/shard_map/all_to_all | solution.py:244
  58.5 26.5 %all-to-all-start.2 = ((f32[32,8,128]{2,1,0:T(8,128)}), f32[32,8,128]{2,1,0:T(8,128)S(1)}, u32[]{:S(2)}, u32[]{:S(2)}) async-start(f32[32,8,128]{2,1,0:T(8,128)} %bitcast.5), calls=%async_computation.2 | async-start | bytes 262144 | tf_op jit(solution)/shard_map/all_to_all | solution.py:247
  81.0 11.5 %collective-permute-start.5 = (bf16[512,256]{1,0:T(8,128)(2,1)}, bf16[512,256]{1,0:T(8,128)(2,1)S(1)}, u32[]{:S(2)}, u32[]{:S(2)}) collective-permute-start(bf16[512,256]{1,0:T(8,128)(2,1)} %get-tuple-element.18), channel_id=1, source_target_pairs={{0,16},{16,0},{1,17},{17,1},{2,18},{18,2},{3,19},{19,3},{4,20},{20... | collective-permute-start | bytes 786440 | tf_op jit(solution)/shard_map/ppermute | solution.py:252
  85.6 14.9 %all-to-all-start.3 = ((bf16[32,8,128]{2,1,0:T(8,128)(2,1)}), bf16[32,8,128]{2,1,0:T(8,128)(2,1)S(1)}, u32[]{:S(2)}, u32[]{:S(2)}) async-start(bf16[32,8,128]{2,1,0:T(8,128)(2,1)} %shard_map.75), calls=%async_computation.3 | async-start | bytes 131072 | tf_op jit(solution)/shard_map/all_to_all | solution.py:248
  92.5 1.0 copy-start.1
Sparse Core Ops, SparseCore 0:
  9.4 58.3 all-gather.1

commit v7 on v6

--- a/solution.py
+++ b/solution.py
@@ -125,27 +125,26 @@
     )(parts)
 
 
-def base_kernel(half_ref, t_ref, wa_ref, wb_ref, w_ref, theirs_ref, ours_ref, t, wt, wo, acc, sems):
+def base_kernel(half_ref, t_ref, wa_ref, wb_ref, w_ref, theirs_ref, ours_ref, t, wo, acc, sems):
     count = HALF // DEPTH
     per_quarter = count // 2
     copies = []
     for i in range(count):
         cols = slice(i * DEPTH, (i + 1) * DEPTH)
-        source = wa_ref if i < per_quarter else wb_ref
-        rows = pl.ds((i % per_quarter) * DEPTH, DEPTH)
         start = pl.multiple_of(half_ref[0] * HALF + i * DEPTH, DEPTH)
-        trio = (
+        pair = (
             pltpu.make_async_copy(t_ref.at[:, cols], t.at[i], sems.at[i, 0]),
-            pltpu.make_async_copy(source.at[rows, :], wt.at[i], sems.at[i, 1]),
-            pltpu.make_async_copy(w_ref.at[pl.ds(start, DEPTH), :], wo.at[i], sems.at[i, 2]),
+            pltpu.make_async_copy(w_ref.at[pl.ds(start, DEPTH), :], wo.at[i], sems.at[i, 1]),
         )
-        for copy in trio:
+        for copy in pair:
             copy.start()
-        copies.append(trio)
+        copies.append(pair)
     for i in range(count):
         for copy in copies[i]:
             copy.wait()
-        theirs = jnp.dot(t[i], wt[i], preferred_element_type=jnp.float32)
+        source = wa_ref if i < per_quarter else wb_ref
+        rows = slice((i % per_quarter) * DEPTH, (i % per_quarter + 1) * DEPTH)
+        theirs = jnp.dot(t[i], source[rows, :], preferred_element_type=jnp.float32)
         ours = jnp.dot(t[i], wo[i], preferred_element_type=jnp.float32)
         if i == 0:
             acc[...] = theirs
@@ -164,16 +163,15 @@
             jax.ShapeDtypeStruct((ROWS, WIDTH), jnp.bfloat16),
             jax.ShapeDtypeStruct((ROWS, WIDTH), jnp.float32),
         ],
-        in_specs=[SMEM, ANY, ANY, ANY, ANY],
+        in_specs=[SMEM, ANY, VMEM, VMEM, ANY],
         out_specs=[VMEM, VMEM],
         scratch_shapes=[
             pltpu.VMEM((count, ROWS, DEPTH), jnp.bfloat16),
             pltpu.VMEM((count, DEPTH, WIDTH), jnp.bfloat16),
-            pltpu.VMEM((count, DEPTH, WIDTH), jnp.bfloat16),
             pltpu.VMEM((ROWS, WIDTH), jnp.float32),
-            pltpu.SemaphoreType.DMA((count, 3)),
-        ],
-        compiler_params=vmem(56),
+            pltpu.SemaphoreType.DMA((count, 2)),
+        ],
+        compiler_params=vmem(51),
         cost_estimate=pl.CostEstimate(
             flops=4 * ROWS * HALF * WIDTH, bytes_accessed=10 << 20, transcendentals=0
         ),
@@ -220,9 +218,9 @@
     dp = lax.axis_index(DP).astype(jnp.int32)[None]
     place = jnp.stack([lax.axis_index("xh"), lax.axis_index("zl")]).astype(jnp.int32)
 
-    gathered = lax.all_gather(tokens, ("y", "c"), axis=1, tiled=True)
-
     spread = jnp.broadcast_to(request_ids[None, None, :], (PEERS, 1, 2))
+    late_tokens, _ = lax.optimization_barrier((tokens, spread))
+    gathered = lax.all_gather(late_tokens, ("y", "c"), axis=1, tiled=True)
     every_id = lax.all_to_all(spread, "zh", 0, 0, tiled=True)
     own, _ = lax.optimization_barrier((jnp.stack([down, up]), spread))
     pair = ("xh", "zl")

time: 109 us -> 107 us (0.982)
  starting transfers between devices: 61.3 us -> 59.1 us
  waiting for transfers between devices: 18.2 us -> 19.4 us
  Pallas kernels: 10.3 us -> 9.14 us
    dynamic_slice x1, local copies, waits for them, and re-layouts: 1.68 us -> 3.03 us  [body(): lax.dynamic_slice_in_dim(late_weight, start + quarter, quarter, 0)]
    all_to_all x1, starting transfers between devices: 17.4 us -> 16.2 us  [body(): parts = lax.all_to_all(partial.reshape(32, 8, 128), TENSOR, 0, 0)]
    all_to_all x1, starting transfers between devices: 6.87 us -> 5.73 us  [body(): low = lax.all_to_all(sum_parts(parts), TENSOR, 0, 0)]
    all_to_all x1, waiting for transfers between devices: 0.62 us -> 1.75 us  [body(): parts = lax.all_to_all(partial.reshape(32, 8, 128), TENSOR, 0, 0)]
    pallas_call x1, Pallas kernels: 5.07 us -> 3.95 us  [base_products(): pl.pallas_call(base_kernel, out_shape=[jax.ShapeDtypeStruct((ROWS, WIDTH)...]
  transfers between devices with their start and end apart: 11 -> 11, of which waited for: 4 -> 3; matrix products, arithmetic and copies ran while one was open for 4% -> 4% of each run, Pallas kernels for 9% -> 8%
where the time goes in v7:
time: 107 us
  starting transfers between devices  59.1 us (55%)
  waiting for transfers between devices  19.4 us (18%)
  between operations  13.6 us (13%)
  Pallas kernels  9.14 us (9%)
  local copies, waits for them, and re-layouts  4.33 us (4%)
  other arithmetic  1.07 us (1%)
    all_to_all x1, starting transfers between devices, body(): parts = lax.all_to_all(partial.reshape(32, 8, 128), TENSOR, 0, 0)  16.2 us
    all_to_all x1, starting transfers between devices, body(): every_id = lax.all_to_all(spread, 'zh', 0, 0, tiled=True)  10.9 us
    ppermute x3, starting transfers between devices, body(): lax.ppermute(own, pair, [(i, i ^ flip) for i in range(4)])  9.88 us
    all_to_all x1, waiting for transfers between devices, body(): got = lax.all_to_all(sent, 'zh', 0, 0, tiled=True)  9.58 us
    all_to_all x1, waiting for transfers between devices, body(): low = lax.all_to_all(sum_parts(parts), TENSOR, 0, 0)  8 us
    all_to_all x1, starting transfers between devices, body(): got = lax.all_to_all(sent, 'zh', 0, 0, tiled=True)  6.68 us
    all_to_all x1, starting transfers between devices, body(): low = lax.all_to_all(sum_parts(parts), TENSOR, 0, 0)  5.73 us
    pallas_call x1, Pallas kernels, base_products(): pl.pallas_call(base_kernel, out_shape=[jax.ShapeDtypeStruct((ROWS, WIDTH)...  3.95 us
  transfers between devices with their start and end apart: 11, of which 3 were waited for; matrix products, arithmetic and copies ran while one was open for 4% of the time, Pallas kernels for 8%

profile of v7, /device:TPU:1, one launch (start us, length us, event | category | flops | bytes accessed | tf_op | source)
XLA Modules:
  0.0 106.6 jit_solution(10310093642141465412)
XLA Ops:
  6.5 0.0 all-gather.2.cloned.1.call-start
  6.6 1.3 %broadcast_in_dim.13 = s32[4,1,2]{2,1,0:T(1,128)} broadcast(s32[2]{0:T(128)} %ids_ref.1), dimensions={2} | broadcast | bytes 40 | tf_op jit(solution)/shard_map/broadcast_in_dim | solution.py:221
  7.9 0.0 all-gather.2.cloned.1.call-update
  7.9 10.9 %all-to-all-start = ((s32[4,1,2]{2,1,0:T(1,128)}), s32[4,1,2]{2,1,0:T(1,128)S(1)}, u32[]{:S(2)}, u32[]{:S(2)}) async-start(s32[4,1,2]{2,1,0:T(1,128)} %broadcast_in_dim.13), calls=%async_computation | async-start | bytes 4096 | tf_op jit(solution)/shard_map/all_to_all | solution.py:224
  18.8 1.0 pad_maximum_fusion.own_ref
  19.8 4.7 %collective-permute-start = (bf16[2,4,64,256]{3,2,1,0:T(8,128)(2,1)S(1)}, bf16[2,4,64,256]{3,2,1,0:T(8,128)(2,1)S(1)}, u32[]{:S(2)}, u32[]{:S(2)}) collective-permute-start(bf16[2,4,64,256]{3,2,1,0:T(8,128)(2,1)S(1)} %pad_maximum_fusion.own_ref), channel_id=1, source_target_pairs={{0,256},{32,288},{256,0},{288,32},{1,257},{33,289},{257,1},{289,33... | collective-permute-start | bytes 786440 | tf_op jit(solution)/shard_map/ppermute | solution.py:227
  24.4 3.1 %collective-permute-start.1 = (bf16[2,4,64,256]{3,2,1,0:T(8,128)(2,1)S(1)}, bf16[2,4,64,256]{3,2,1,0:T(8,128)(2,1)S(1)}, u32[]{:S(2)}, u32[]{:S(2)}) collective-permute-start(bf16[2,4,64,256]{3,2,1,0:T(8,128)(2,1)S(1)} %pad_maximum_fusion.own_ref), channel_id=1, source_target_pairs={{0,32},{32,0},{256,288},{288,256},{1,33},{33,1},{257,289},{289,257... | collective-permute-start | bytes 786440 | tf_op jit(solution)/shard_map/ppermute | solution.py:227
  27.5 2.1 %collective-permute-start.2 = (bf16[2,4,64,256]{3,2,1,0:T(8,128)(2,1)S(1)}, bf16[2,4,64,256]{3,2,1,0:T(8,128)(2,1)S(1)}, u32[]{:S(2)}, u32[]{:S(2)}) collective-permute-start(bf16[2,4,64,256]{3,2,1,0:T(8,128)(2,1)S(1)} %pad_maximum_fusion.own_ref), channel_id=1, source_target_pairs={{0,288},{32,256},{256,32},{288,0},{1,289},{33,257},{257,33},{289,1... | collective-permute-start | bytes 786440 | tf_op jit(solution)/shard_map/ppermute | solution.py:227
  29.7 0.0 all-to-all-done.ids_ref
  29.7 3.0 %constant_dynamic-slice_fusion = (bf16[2048,256]{1,0:T(8,128)(2,1)}, bf16[2048,256]{1,0:T(8,128)(2,1)}) fusion(bf16[8192,256]{1,0:T(8,128)(2,1)} %w_ref, s32[]{:T(128)S(6)} %select_n.7, s32[]{:T(128)S(6)} %select_n.6), kind=kLoop, calls=%fused_computation.2 | loop fusion | bytes 4194312 | tf_op jit(solution)/shard_map/dynamic_slice | solution.py:237
  32.7 3.1 %collective-permute-start.3 = (bf16[2048,256]{1,0:T(8,128)(2,1)}, bf16[2048,256]{1,0:T(8,128)(2,1)S(1)}, u32[]{:S(2)}, u32[]{:S(2)}) collective-permute-start(bf16[2048,256]{1,0:T(8,128)(2,1)} %get-tuple-element.22), channel_id=1, source_target_pairs={{0,16},{16,256},{256,272},{272,0},{1,17},{17,257},{257,273},{273,1... | collective-permute-start | bytes 3145736 | tf_op jit(solution)/shard_map/ppermute | solution.py:233
  35.8 3.4 %collective-permute-start.4 = (bf16[2048,256]{1,0:T(8,128)(2,1)}, bf16[2048,256]{1,0:T(8,128)(2,1)S(1)}, u32[]{:S(2)}, u32[]{:S(2)}) collective-permute-start(bf16[2048,256]{1,0:T(8,128)(2,1)} %get-tuple-element.21), channel_id=1, source_target_pairs={{0,272},{16,0},{256,16},{272,256},{1,273},{17,1},{257,17},{273,257... | collective-permute-start | bytes 3145736 | tf_op jit(solution)/shard_map/ppermute | solution.py:236
  39.2 0.1 pad_add_fusion.place_ref
  39.3 0.0 collective-permute-done.x_ref
  39.3 0.0 collective-permute-done.1.z_ref
  39.3 0.0 collective-permute-done.2.xz_ref
  39.3 1.7 %shard_map.73 = bf16[4,4,64,256]{3,2,1,0:T(8,128)(2,1)} custom-call(s32[4,1,2]{2,1,0:T(1,128)S(1)} %all-to-all-done.ids_ref, s32[64]{0:T(128)S(1)} %copy-done.1, s32[2]{0:T(128)S(1)} %pad_add_fusion.place_ref, bf16[2,4,64,256]{3,2,1,0:T(8,128)(2,1)S(1)} %pad_maximum_fusion.own_ref, bf16[2,4,64,256]{3,2,1,0:T(8,128)(2,1)S(1)} %collective-permute-done.x_ref, ...), custom_call_target="tpu_custom_call" | custom-call | bytes 2097152 | tf_op jit(solution)/shard_map/pallas_call | solution.py:51
  41.0 6.7 %all-to-all-start.1 = ((bf16[4,4,64,256]{3,2,1,0:T(8,128)(2,1)}), bf16[4,4,64,256]{3,2,1,0:T(8,128)(2,1)S(1)}, u32[]{:S(2)}, u32[]{:S(2)}) async-start(bf16[4,4,64,256]{3,2,1,0:T(8,128)(2,1)} %shard_map.73), calls=%async_computation.1 | async-start | bytes 1048576 | tf_op jit(solution)/shard_map/all_to_all | solution.py:242
  47.7 9.6 %all-to-all-done.1.got_ref = bf16[4,4,64,256]{3,2,1,0:T(8,128)(2,1)S(1)} async-done(((bf16[4,4,64,256]{3,2,1,0:T(8,128)(2,1)}), bf16[4,4,64,256]{3,2,1,0:T(8,128)(2,1)S(1)}, u32[]{:S(2)}, u32[]{:S(2)}) %all-to-all-start.1) | async-done | bytes 524320 | tf_op jit(solution)/shard_map/all_to_all | solution.py:242
  57.3 1.8 %shard_map.74 = (f32[256,128]{1,0:T(8,128)}, bf16[4,64,256]{2,1,0:T(8,128)(2,1)S(1)}) custom-call(s32[2]{0:T(128)S(1)} %copy-done.2, s32[64]{0:T(128)S(1)} %copy-done.1, s32[4]{0:T(128)S(1)} %copy-done.3, s32[1]{0:T(128)} %bitcast.dp_ref, bf16[512,256]{1,0:T(8,128)(2,1)S(1)} %copy-done, bf16[4,4,64,256]{3,2,1,0:T(8,128)(2,1)S(1)} %all-to-all-done.1.got_ref), custom_call_target="tpu_custom_call" | custom-call | flops 16777216 | bytes 1048576 | tf_op jit(solution)/shard_map/pallas_call | solution.py:96
  59.1 16.2 %all-to-all-start.2 = ((f32[32,8,128]{2,1,0:T(8,128)}), f32[32,8,128]{2,1,0:T(8,128)S(1)}, u32[]{:S(2)}, u32[]{:S(2)}) async-start(f32[32,8,128]{2,1,0:T(8,128)} %bitcast.5), calls=%async_computation.2 | async-start | bytes 262144 | tf_op jit(solution)/shard_map/all_to_all | solution.py:245
  75.3 0.0 collective-permute-done.3.wa_ref
  75.3 0.0 collective-permute-done.4.wb_ref
  75.3 0.0 all-gather.2.cloned.1.call-done.t_ref
  75.3 4.0 %shard_map.76 = (bf16[512,256]{1,0:T(8,128)(2,1)S(1)}, f32[512,256]{1,0:T(8,128)S(1)}) custom-call(s32[1]{0:T(128)} %bitcast.7.half_ref, bf16[512,4096]{1,0:T(8,128)(2,1)} %all-gather.2.cloned.1.call-done.t_ref, bf16[2048,256]{1,0:T(8,128)(2,1)S(1)} %collective-permute-done.3.wa_ref, bf16[2048,256]{1,0:T(8,128)(2,1)S(1)} %collective-permute-done.4.wb_ref, ...), custom_call_target="tpu_custom_call" | custom-call | flops 2147483648 | bytes 10485760 | tf_op jit(solution)/shard_map/pallas_call | solution.py:160
  79.3 3.3 %collective-permute-start.5 = (bf16[512,256]{1,0:T(8,128)(2,1)S(1)}, bf16[512,256]{1,0:T(8,128)(2,1)S(1)}, u32[]{:S(2)}, u32[]{:S(2)}) collective-permute-start(bf16[512,256]{1,0:T(8,128)(2,1)S(1)} %get-tuple-element.20), channel_id=1, source_target_pairs={{0,16},{16,0},{1,17},{17,1},{2,18},{18,2},{3,19},{19,3},{4,20},{20... | collective-permute-start | bytes 786440 | tf_op jit(solution)/shard_map/ppermute | solution.py:250
  82.6 1.8 %all-to-all-done.2.parts_ref = f32[32,8,128]{2,1,0:T(8,128)S(1)} async-done(((f32[32,8,128]{2,1,0:T(8,128)}), f32[32,8,128]{2,1,0:T(8,128)S(1)}, u32[]{:S(2)}, u32[]{:S(2)}) %all-to-all-start.2) | async-done | bytes 131104 | tf_op jit(solution)/shard_map/all_to_all | solution.py:245
  84.4 0.7 shard_map.75
  85.0 5.7 %all-to-all-start.3 = ((bf16[32,8,128]{2,1,0:T(8,128)(2,1)}), bf16[32,8,128]{2,1,0:T(8,128)(2,1)S(1)}, u32[]{:S(2)}, u32[]{:S(2)}) async-start(bf16[32,8,128]{2,1,0:T(8,128)(2,1)} %shard_map.75), calls=%async_computation.3 | async-start | bytes 131072 | tf_op jit(solution)/shard_map/all_to_all | solution.py:246
  90.8 0.1 shard_map.77.base_ref
  90.8 8.0 %all-to-all-done.3 = bf16[32,8,128]{2,1,0:T(8,128)(2,1)S(1)} async-done(((bf16[32,8,128]{2,1,0:T(8,128)(2,1)}), bf16[32,8,128]{2,1,0:T(8,128)(2,1)S(1)}, u32[]{:S(2)}, u32[]{:S(2)}) %all-to-all-start.3) | async-done | bytes 65568 | tf_op jit(solution)/shard_map/all_to_all | solution.py:246
  98.8 0.9 shard_map.78
  (9 shorter events, 0.0 us)
Async XLA Ops:
  6.5 50.8 %copy-start.2 = (s32[2]{0:T(128)S(1)}, s32[2]{0:T(128)}, u32[]{:S(2)}) copy-start(s32[2]{0:T(128)} %ids_ref.1) | copy-start | bytes 28
  6.5 50.8 %copy-start = (bf16[512,256]{1,0:T(8,128)(2,1)S(1)}, bf16[512,256]{1,0:T(8,128)(2,1)}, u32[]{:S(2)}) copy-start(bf16[512,256]{1,0:T(8,128)(2,1)} %tokens_ref.1) | copy-start | bytes 786436
  6.5 32.8 %copy-start.1 = (s32[64]{0:T(128)S(1)}, s32[64]{0:T(128)}, u32[]{:S(2)}) copy-start(s32[64]{0:T(128)} %stored_ref.3) | copy-start | bytes 772
  6.5 50.8 %copy-start.3 = (s32[4]{0:T(128)S(1)}, s32[4]{0:T(128)}, u32[]{:S(2)}) copy-start(s32[4]{0:T(128)} %seg_ref.1) | copy-start | bytes 52
  6.5 68.8 %all-gather.2.cloned.1.call-start = ((), (), s32[]{:S(2)}) async-start(), calls=%async_computation.4 | async-start | bytes 4456448 | tf_op jit(solution)/shard_map/all_gather | solution.py:223
  7.9 21.8 %all-to-all-start = ((s32[4,1,2]{2,1,0:T(1,128)}), s32[4,1,2]{2,1,0:T(1,128)S(1)}, u32[]{:S(2)}, u32[]{:S(2)}) async-start(s32[4,1,2]{2,1,0:T(1,128)} %broadcast_in_dim.13), calls=%async_computation | async-start | bytes 4096 | tf_op jit(solution)/shard_map/all_to_all | solution.py:224
  19.8 19.5 %collective-permute-start = (bf16[2,4,64,256]{3,2,1,0:T(8,128)(2,1)S(1)}, bf16[2,4,64,256]{3,2,1,0:T(8,128)(2,1)S(1)}, u32[]{:S(2)}, u32[]{:S(2)}) collective-permute-start(bf16[2,4,64,256]{3,2,1,0:T(8,128)(2,1)S(1)} %pad_maximum_fusion.own_ref), channel_id=1, source_target_pairs={{0,256},{32,288},{256,0},{288,32},{1,257},{33,289},{257,1},{289,33... | collective-permute-start | bytes 786440 | tf_op jit(solution)/shard_map/ppermute | solution.py:227
  24.4 14.9 %collective-permute-start.1 = (bf16[2,4,64,256]{3,2,1,0:T(8,128)(2,1)S(1)}, bf16[2,4,64,256]{3,2,1,0:T(8,128)(2,1)S(1)}, u32[]{:S(2)}, u32[]{:S(2)}) collective-permute-start(bf16[2,4,64,256]{3,2,1,0:T(8,128)(2,1)S(1)} %pad_maximum_fusion.own_ref), channel_id=1, source_target_pairs={{0,32},{32,0},{256,288},{288,256},{1,33},{33,1},{257,289},{289,257... | collective-permute-start | bytes 786440 | tf_op jit(solution)/shard_map/ppermute | solution.py:227
  27.5 11.8 %collective-permute-start.2 = (bf16[2,4,64,256]{3,2,1,0:T(8,128)(2,1)S(1)}, bf16[2,4,64,256]{3,2,1,0:T(8,128)(2,1)S(1)}, u32[]{:S(2)}, u32[]{:S(2)}) collective-permute-start(bf16[2,4,64,256]{3,2,1,0:T(8,128)(2,1)S(1)} %pad_maximum_fusion.own_ref), channel_id=1, source_target_pairs={{0,288},{32,256},{256,32},{288,0},{1,289},{33,257},{257,33},{289,1... | collective-permute-start | bytes 786440 | tf_op jit(solution)/shard_map/ppermute | solution.py:227
  32.7 42.6 %collective-permute-start.3 = (bf16[2048,256]{1,0:T(8,128)(2,1)}, bf16[2048,256]{1,0:T(8,128)(2,1)S(1)}, u32[]{:S(2)}, u32[]{:S(2)}) collective-permute-start(bf16[2048,256]{1,0:T(8,128)(2,1)} %get-tuple-element.22), channel_id=1, source_target_pairs={{0,16},{16,256},{256,272},{272,0},{1,17},{17,257},{257,273},{273,1... | collective-permute-start | bytes 3145736 | tf_op jit(solution)/shard_map/ppermute | solution.py:233
  35.8 39.5 %collective-permute-start.4 = (bf16[2048,256]{1,0:T(8,128)(2,1)}, bf16[2048,256]{1,0:T(8,128)(2,1)S(1)}, u32[]{:S(2)}, u32[]{:S(2)}) collective-permute-start(bf16[2048,256]{1,0:T(8,128)(2,1)} %get-tuple-element.21), channel_id=1, source_target_pairs={{0,272},{16,0},{256,16},{272,256},{1,273},{17,1},{257,17},{273,257... | collective-permute-start | bytes 3145736 | tf_op jit(solution)/shard_map/ppermute | solution.py:236
  41.0 16.3 %all-to-all-start.1 = ((bf16[4,4,64,256]{3,2,1,0:T(8,128)(2,1)}), bf16[4,4,64,256]{3,2,1,0:T(8,128)(2,1)S(1)}, u32[]{:S(2)}, u32[]{:S(2)}) async-start(bf16[4,4,64,256]{3,2,1,0:T(8,128)(2,1)} %shard_map.73), calls=%async_computation.1 | async-start | bytes 1048576 | tf_op jit(solution)/shard_map/all_to_all | solution.py:242
  59.1 25.2 %all-to-all-start.2 = ((f32[32,8,128]{2,1,0:T(8,128)}), f32[32,8,128]{2,1,0:T(8,128)S(1)}, u32[]{:S(2)}, u32[]{:S(2)}) async-start(f32[32,8,128]{2,1,0:T(8,128)} %bitcast.5), calls=%async_computation.2 | async-start | bytes 262144 | tf_op jit(solution)/shard_map/all_to_all | solution.py:245
  79.3 11.5 %collective-permute-start.5 = (bf16[512,256]{1,0:T(8,128)(2,1)S(1)}, bf16[512,256]{1,0:T(8,128)(2,1)S(1)}, u32[]{:S(2)}, u32[]{:S(2)}) collective-permute-start(bf16[512,256]{1,0:T(8,128)(2,1)S(1)} %get-tuple-element.20), channel_id=1, source_target_pairs={{0,16},{16,0},{1,17},{17,1},{2,18},{18,2},{3,19},{19,3},{4,20},{20... | collective-permute-start | bytes 786440 | tf_op jit(solution)/shard_map/ppermute | solution.py:250
  85.0 13.8 %all-to-all-start.3 = ((bf16[32,8,128]{2,1,0:T(8,128)(2,1)}), bf16[32,8,128]{2,1,0:T(8,128)(2,1)S(1)}, u32[]{:S(2)}, u32[]{:S(2)}) async-start(bf16[32,8,128]{2,1,0:T(8,128)(2,1)} %shard_map.75), calls=%async_computation.3 | async-start | bytes 131072 | tf_op jit(solution)/shard_map/all_to_all | solution.py:246
Sparse Core Ops, SparseCore 0:
  9.4 58.3 all-gather.1

commit v8 on v7

--- a/solution.py
+++ b/solution.py
@@ -16,7 +16,6 @@
 OWNED = 4
 ZS = 8
 PEERS = 4
-SUM_TYPE = jnp.float32
 HALF = 4096
 DEPTH = 1024
 
@@ -68,13 +67,8 @@
     return copies
 
 
-def down_kernel(
-    ids_ref, stored_ref, seg_ref, dp_ref, tokens_ref, got_ref, out_ref, ups_ref,
-    mats, ups, sems, up_sems,
-):
-    copies = fetch(ids_ref, stored_ref, got_ref, mats, sems, 0)
-    up_copies = fetch(ids_ref, stored_ref, got_ref, ups, up_sems, 1)
-    for copy in copies:
+def down_kernel(ids_ref, stored_ref, seg_ref, dp_ref, tokens_ref, got_ref, out_ref, mats, sems):
+    for copy in fetch(ids_ref, stored_ref, got_ref, mats, sems, 0):
         copy.wait()
     for k in range(4):
         part = lax.dot_general(
@@ -84,29 +78,44 @@
             preferred_element_type=jnp.float32,
         )
         row, col = (k % 2) * SEG, (k // 2) * RANK
-        out_ref[row : row + SEG, col : col + RANK] = part.astype(out_ref.dtype)
-    for copy in up_copies:
-        copy.wait()
-    for k in range(4):
-        ups_ref[k] = ups[seg_ref[k] - 2 * dp_ref[0]]
+        out_ref[row : row + SEG, col : col + RANK] = part
 
 
 def down_product(ids, stored, seg, dp, tokens, got):
-    mats = pltpu.VMEM((2, RANK, WIDTH), jnp.bfloat16)
     return pl.pallas_call(
         down_kernel,
-        out_shape=[
-            jax.ShapeDtypeStruct((256, 128), SUM_TYPE),
-            jax.ShapeDtypeStruct((4, RANK, WIDTH), jnp.bfloat16),
-        ],
+        out_shape=jax.ShapeDtypeStruct((256, 128), jnp.float32),
         in_specs=[SMEM, SMEM, SMEM, SMEM, VMEM, ANY],
-        out_specs=[VMEM, VMEM],
+        out_specs=VMEM,
         scratch_shapes=[
-            mats, mats, pltpu.SemaphoreType.DMA((2,)), pltpu.SemaphoreType.DMA((2,))
+            pltpu.VMEM((2, RANK, WIDTH), jnp.bfloat16),
+            pltpu.SemaphoreType.DMA((2,)),
         ],
         compiler_params=vmem(4),
         cost_estimate=pl.CostEstimate(flops=1 << 24, bytes_accessed=1 << 20, transcendentals=0),
     )(ids, stored, seg, dp, tokens, got)
+
+
+def pick_kernel(ids_ref, stored_ref, seg_ref, dp_ref, got_ref, out_ref, mats, sems):
+    for copy in fetch(ids_ref, stored_ref, got_ref, mats, sems, 1):
+        copy.wait()
+    for k in range(4):
+        out_ref[k] = mats[seg_ref[k] - 2 * dp_ref[0]]
+
+
+def pick(ids, stored, seg, dp, got):
+    return pl.pallas_call(
+        pick_kernel,
+        out_shape=jax.ShapeDtypeStruct((4, RANK, WIDTH), jnp.bfloat16),
+        in_specs=[SMEM, SMEM, SMEM, SMEM, ANY],
+        out_specs=VMEM,
+        scratch_shapes=[
+            pltpu.VMEM((2, RANK, WIDTH), jnp.bfloat16),
+            pltpu.SemaphoreType.DMA((2,)),
+        ],
+        compiler_params=vmem(4),
+        cost_estimate=pl.CostEstimate(flops=0, bytes_accessed=1 << 18, transcendentals=0),
+    )(ids, stored, seg, dp, got)
 
 
 def sum_kernel(parts_ref, out_ref):
@@ -241,13 +250,14 @@
 
     got = lax.all_to_all(sent, "zh", 0, 0, tiled=True)
 
-    partial, ups = down_product(request_ids, stored_row, segment_request, dp, tokens, got)
+    partial = down_product(request_ids, stored_row, segment_request, dp, tokens, got)
     parts = lax.all_to_all(partial.reshape(32, 8, 128), TENSOR, 0, 0)
     low = lax.all_to_all(sum_parts(parts), TENSOR, 0, 0)
 
     weight, _ = lax.optimization_barrier((weight, partial))
     theirs, ours = base_products(xl[None], gathered, wa, wb, weight)
     recv = lax.ppermute(theirs, "xl", SWAP)
+    ups = pick(request_ids, stored_row, segment_request, dp, got)
     return last_product(low.reshape(256, 128), ups, add(ours, recv))
 
 

time: 107 us -> 106 us (level)
  the two profiles are of different devices: /device:TPU:1 before, /device:TPU:68 now
where the time goes in v8:
time: 106 us; the launch traced here: 105 us
  starting transfers between devices  51.3 us (48%)
  waiting for transfers between devices  24.7 us (23%)
  between operations  13.6 us (13%)
  Pallas kernels  10.4 us (10%)
  local copies, waits for them, and re-layouts  4.32 us (4%)
  other arithmetic  1.07 us (1%)
    all_to_all x1, waiting for transfers between devices, body(): got = lax.all_to_all(sent, 'zh', 0, 0, tiled=True)  14.3 us
    ppermute x3, starting transfers between devices, body(): lax.ppermute(own, pair, [(i, i ^ flip) for i in range(4)])  10.7 us
    all_to_all x1, starting transfers between devices, body(): every_id = lax.all_to_all(spread, 'zh', 0, 0, tiled=True)  9.41 us
    all_to_all x1, starting transfers between devices, body(): parts = lax.all_to_all(partial.reshape(32, 8, 128), TENSOR, 0, 0)  9.35 us
    all_to_all x1, waiting for transfers between devices, body(): low = lax.all_to_all(sum_parts(parts), TENSOR, 0, 0)  8.28 us
    all_to_all x1, starting transfers between devices, body(): got = lax.all_to_all(sent, 'zh', 0, 0, tiled=True)  7.2 us
    all_to_all x1, starting transfers between devices, body(): low = lax.all_to_all(sum_parts(parts), TENSOR, 0, 0)  5.02 us
    pallas_call x1, Pallas kernels, base_products(): pl.pallas_call(base_kernel, out_shape=[jax.ShapeDtypeStruct((ROWS, WIDTH)...  4.63 us
  transfers between devices with their start and end apart: 11, of which 3 were waited for; matrix products, arithmetic and copies ran while one was open for 4% of the time, Pallas kernels for 9%

profile of v8, /device:TPU:68, one launch (start us, length us, event | category | flops | bytes accessed | tf_op | source)
XLA Modules:
  0.0 105.3 jit_solution(15697411353408523844)
XLA Ops:
  6.5 0.0 all-gather.2.cloned.1.call-start
  6.6 1.3 %broadcast_in_dim.13 = s32[4,1,2]{2,1,0:T(1,128)} broadcast(s32[2]{0:T(128)} %ids_ref.3), dimensions={2} | broadcast | bytes 40 | tf_op jit(solution)/shard_map/broadcast_in_dim | solution.py:230
  7.9 0.0 all-gather.2.cloned.1.call-update
  7.9 9.4 %all-to-all-start = ((s32[4,1,2]{2,1,0:T(1,128)}), s32[4,1,2]{2,1,0:T(1,128)S(1)}, u32[]{:S(2)}, u32[]{:S(2)}) async-start(s32[4,1,2]{2,1,0:T(1,128)} %broadcast_in_dim.13), calls=%async_computation | async-start | bytes 4096 | tf_op jit(solution)/shard_map/all_to_all | solution.py:233
  17.3 1.0 pad_maximum_fusion.own_ref
  18.3 2.4 %collective-permute-start.2 = (bf16[2,4,64,256]{3,2,1,0:T(8,128)(2,1)S(1)}, bf16[2,4,64,256]{3,2,1,0:T(8,128)(2,1)S(1)}, u32[]{:S(2)}, u32[]{:S(2)}) collective-permute-start(bf16[2,4,64,256]{3,2,1,0:T(8,128)(2,1)S(1)} %pad_maximum_fusion.own_ref), channel_id=1, source_target_pairs={{0,288},{32,256},{256,32},{288,0},{1,289},{33,257},{257,33},{289,1... | collective-permute-start | bytes 786440 | tf_op jit(solution)/shard_map/ppermute | solution.py:236
  20.7 3.4 %collective-permute-start.1 = (bf16[2,4,64,256]{3,2,1,0:T(8,128)(2,1)S(1)}, bf16[2,4,64,256]{3,2,1,0:T(8,128)(2,1)S(1)}, u32[]{:S(2)}, u32[]{:S(2)}) collective-permute-start(bf16[2,4,64,256]{3,2,1,0:T(8,128)(2,1)S(1)} %pad_maximum_fusion.own_ref), channel_id=1, source_target_pairs={{0,32},{32,0},{256,288},{288,256},{1,33},{33,1},{257,289},{289,257... | collective-permute-start | bytes 786440 | tf_op jit(solution)/shard_map/ppermute | solution.py:236
  24.1 4.9 %collective-permute-start = (bf16[2,4,64,256]{3,2,1,0:T(8,128)(2,1)S(1)}, bf16[2,4,64,256]{3,2,1,0:T(8,128)(2,1)S(1)}, u32[]{:S(2)}, u32[]{:S(2)}) collective-permute-start(bf16[2,4,64,256]{3,2,1,0:T(8,128)(2,1)S(1)} %pad_maximum_fusion.own_ref), channel_id=1, source_target_pairs={{0,256},{32,288},{256,0},{288,32},{1,257},{33,289},{257,1},{289,33... | collective-permute-start | bytes 786440 | tf_op jit(solution)/shard_map/ppermute | solution.py:236
  29.0 0.0 all-to-all-done.ids_ref
  29.1 3.0 %constant_dynamic-slice_fusion = (bf16[2048,256]{1,0:T(8,128)(2,1)}, bf16[2048,256]{1,0:T(8,128)(2,1)}) fusion(bf16[8192,256]{1,0:T(8,128)(2,1)} %w_ref, s32[]{:T(128)S(6)} %select_n.7, s32[]{:T(128)S(6)} %select_n.6), kind=kLoop, calls=%fused_computation.2 | loop fusion | bytes 4194312 | tf_op jit(solution)/shard_map/dynamic_slice | solution.py:246
  32.1 2.4 %collective-permute-start.4 = (bf16[2048,256]{1,0:T(8,128)(2,1)}, bf16[2048,256]{1,0:T(8,128)(2,1)S(1)}, u32[]{:S(2)}, u32[]{:S(2)}) collective-permute-start(bf16[2048,256]{1,0:T(8,128)(2,1)} %get-tuple-element.17), channel_id=1, source_target_pairs={{0,272},{16,0},{256,16},{272,256},{1,273},{17,1},{257,17},{273,257... | collective-permute-start | bytes 3145736 | tf_op jit(solution)/shard_map/ppermute | solution.py:245
  34.5 3.4 %collective-permute-start.3 = (bf16[2048,256]{1,0:T(8,128)(2,1)}, bf16[2048,256]{1,0:T(8,128)(2,1)S(1)}, u32[]{:S(2)}, u32[]{:S(2)}) collective-permute-start(bf16[2048,256]{1,0:T(8,128)(2,1)} %get-tuple-element.18), channel_id=1, source_target_pairs={{0,16},{16,256},{256,272},{272,0},{1,17},{17,257},{257,273},{273,1... | collective-permute-start | bytes 3145736 | tf_op jit(solution)/shard_map/ppermute | solution.py:242
  37.9 0.1 pad_add_fusion.place_ref
  38.0 0.0 collective-permute-done.2.xz_ref
  38.0 0.0 collective-permute-done.1.z_ref
  38.0 0.0 collective-permute-done.x_ref
  38.0 1.7 %shard_map.73 = bf16[4,4,64,256]{3,2,1,0:T(8,128)(2,1)} custom-call(s32[4,1,2]{2,1,0:T(1,128)S(1)} %all-to-all-done.ids_ref, s32[64]{0:T(128)S(1)} %copy-done.1, s32[2]{0:T(128)S(1)} %pad_add_fusion.place_ref, bf16[2,4,64,256]{3,2,1,0:T(8,128)(2,1)S(1)} %pad_maximum_fusion.own_ref, bf16[2,4,64,256]{3,2,1,0:T(8,128)(2,1)S(1)} %collective-permute-done.x_ref, ...), custom_call_target="tpu_custom_call" | custom-call | bytes 2097152 | tf_op jit(solution)/shard_map/pallas_call | solution.py:50
  39.8 7.2 %all-to-all-start.1 = ((bf16[4,4,64,256]{3,2,1,0:T(8,128)(2,1)}), bf16[4,4,64,256]{3,2,1,0:T(8,128)(2,1)S(1)}, u32[]{:S(2)}, u32[]{:S(2)}) async-start(bf16[4,4,64,256]{3,2,1,0:T(8,128)(2,1)} %shard_map.73), calls=%async_computation.1 | async-start | bytes 1048576 | tf_op jit(solution)/shard_map/all_to_all | solution.py:251
  47.0 14.3 %all-to-all-done.1.got_ref = bf16[4,4,64,256]{3,2,1,0:T(8,128)(2,1)S(1)} async-done(((bf16[4,4,64,256]{3,2,1,0:T(8,128)(2,1)}), bf16[4,4,64,256]{3,2,1,0:T(8,128)(2,1)S(1)}, u32[]{:S(2)}, u32[]{:S(2)}) %all-to-all-start.1) | async-done | bytes 524320 | tf_op jit(solution)/shard_map/all_to_all | solution.py:251
  61.2 1.6 %shard_map.74 = f32[256,128]{1,0:T(8,128)} custom-call(s32[2]{0:T(128)S(1)} %copy-done.2, s32[64]{0:T(128)S(1)} %copy-done.1, s32[4]{0:T(128)S(1)} %copy-done.3, s32[1]{0:T(128)} %bitcast.dp_ref, bf16[512,256]{1,0:T(8,128)(2,1)S(1)} %copy-done, bf16[4,4,64,256]{3,2,1,0:T(8,128)(2,1)S(1)} %all-to-all-done.1.got_ref), custom_call_target="tpu_custom_call" | custom-call | flops 16777216 | bytes 1048576 | tf_op jit(solution)/shard_map/pallas_call | solution.py:85
  62.9 9.4 %all-to-all-start.2 = ((f32[32,8,128]{2,1,0:T(8,128)}), f32[32,8,128]{2,1,0:T(8,128)S(1)}, u32[]{:S(2)}, u32[]{:S(2)}) async-start(f32[32,8,128]{2,1,0:T(8,128)} %bitcast.5), calls=%async_computation.2 | async-start | bytes 262144 | tf_op jit(solution)/shard_map/all_to_all | solution.py:254
  72.3 0.0 collective-permute-done.3.wa_ref
  72.3 0.0 all-gather.2.cloned.1.call-done.t_ref
  72.3 4.6 %shard_map.77 = (bf16[512,256]{1,0:T(8,128)(2,1)}, f32[512,256]{1,0:T(8,128)S(1)}) custom-call(s32[1]{0:T(128)} %bitcast.7.half_ref, bf16[512,4096]{1,0:T(8,128)(2,1)} %all-gather.2.cloned.1.call-done.t_ref, bf16[2048,256]{1,0:T(8,128)(2,1)S(1)} %collective-permute-done.3.wa_ref, bf16[2048,256]{1,0:T(8,128)(2,1)S(1)} %collective-permute-done.4.wb_ref, ...), custom_call_target="tpu_custom_call" | custom-call | flops 2147483648 | bytes 10485760 | tf_op jit(solution)/shard_map/pallas_call | solution.py:169
  76.9 3.7 %collective-permute-start.5 = (bf16[512,256]{1,0:T(8,128)(2,1)}, bf16[512,256]{1,0:T(8,128)(2,1)S(1)}, u32[]{:S(2)}, u32[]{:S(2)}) collective-permute-start(bf16[512,256]{1,0:T(8,128)(2,1)} %get-tuple-element.16), channel_id=1, source_target_pairs={{0,16},{16,0},{1,17},{17,1},{2,18},{18,2},{3,19},{19,3},{4,20},{20... | collective-permute-start | bytes 786440 | tf_op jit(solution)/shard_map/ppermute | solution.py:259
  80.7 2.1 %all-to-all-done.2.parts_ref = f32[32,8,128]{2,1,0:T(8,128)S(1)} async-done(((f32[32,8,128]{2,1,0:T(8,128)}), f32[32,8,128]{2,1,0:T(8,128)S(1)}, u32[]{:S(2)}, u32[]{:S(2)}) %all-to-all-start.2) | async-done | bytes 131104 | tf_op jit(solution)/shard_map/all_to_all | solution.py:254
  82.7 0.7 shard_map.75
  83.4 5.0 %all-to-all-start.3 = ((bf16[32,8,128]{2,1,0:T(8,128)(2,1)}), bf16[32,8,128]{2,1,0:T(8,128)(2,1)S(1)}, u32[]{:S(2)}, u32[]{:S(2)}) async-start(bf16[32,8,128]{2,1,0:T(8,128)(2,1)} %shard_map.75), calls=%async_computation.3 | async-start | bytes 131072 | tf_op jit(solution)/shard_map/all_to_all | solution.py:255
  88.4 0.7 shard_map.76.ups_ref
  89.2 0.1 shard_map.78.base_ref
  89.2 8.3 %all-to-all-done.3 = bf16[32,8,128]{2,1,0:T(8,128)(2,1)S(1)} async-done(((bf16[32,8,128]{2,1,0:T(8,128)(2,1)}), bf16[32,8,128]{2,1,0:T(8,128)(2,1)S(1)}, u32[]{:S(2)}, u32[]{:S(2)}) %all-to-all-start.3) | async-done | bytes 65568 | tf_op jit(solution)/shard_map/all_to_all | solution.py:255
  97.5 0.9 shard_map.79
  (10 shorter events, 0.0 us)
Async XLA Ops:
  6.5 54.7 %copy-start = (bf16[512,256]{1,0:T(8,128)(2,1)S(1)}, bf16[512,256]{1,0:T(8,128)(2,1)}, u32[]{:S(2)}) copy-start(bf16[512,256]{1,0:T(8,128)(2,1)} %tokens_ref.1) | copy-start | bytes 786436
  6.5 54.7 %copy-start.2 = (s32[2]{0:T(128)S(1)}, s32[2]{0:T(128)}, u32[]{:S(2)}) copy-start(s32[2]{0:T(128)} %ids_ref.3) | copy-start | bytes 28
  6.5 31.5 %copy-start.1 = (s32[64]{0:T(128)S(1)}, s32[64]{0:T(128)}, u32[]{:S(2)}) copy-start(s32[64]{0:T(128)} %stored_ref.5) | copy-start | bytes 772
  6.5 54.7 %copy-start.3 = (s32[4]{0:T(128)S(1)}, s32[4]{0:T(128)}, u32[]{:S(2)}) copy-start(s32[4]{0:T(128)} %seg_ref.3) | copy-start | bytes 52
  6.5 65.8 %all-gather.2.cloned.1.call-start = ((), (), s32[]{:S(2)}) async-start(), calls=%async_computation.4 | async-start | bytes 4456448 | tf_op jit(solution)/shard_map/all_gather | solution.py:232
  7.9 21.2 %all-to-all-start = ((s32[4,1,2]{2,1,0:T(1,128)}), s32[4,1,2]{2,1,0:T(1,128)S(1)}, u32[]{:S(2)}, u32[]{:S(2)}) async-start(s32[4,1,2]{2,1,0:T(1,128)} %broadcast_in_dim.13), calls=%async_computation | async-start | bytes 4096 | tf_op jit(solution)/shard_map/all_to_all | solution.py:233
  18.3 19.7 %collective-permute-start.2 = (bf16[2,4,64,256]{3,2,1,0:T(8,128)(2,1)S(1)}, bf16[2,4,64,256]{3,2,1,0:T(8,128)(2,1)S(1)}, u32[]{:S(2)}, u32[]{:S(2)}) collective-permute-start(bf16[2,4,64,256]{3,2,1,0:T(8,128)(2,1)S(1)} %pad_maximum_fusion.own_ref), channel_id=1, source_target_pairs={{0,288},{32,256},{256,32},{288,0},{1,289},{33,257},{257,33},{289,1... | collective-permute-start | bytes 786440 | tf_op jit(solution)/shard_map/ppermute | solution.py:236
  20.7 17.3 %collective-permute-start.1 = (bf16[2,4,64,256]{3,2,1,0:T(8,128)(2,1)S(1)}, bf16[2,4,64,256]{3,2,1,0:T(8,128)(2,1)S(1)}, u32[]{:S(2)}, u32[]{:S(2)}) collective-permute-start(bf16[2,4,64,256]{3,2,1,0:T(8,128)(2,1)S(1)} %pad_maximum_fusion.own_ref), channel_id=1, source_target_pairs={{0,32},{32,0},{256,288},{288,256},{1,33},{33,1},{257,289},{289,257... | collective-permute-start | bytes 786440 | tf_op jit(solution)/shard_map/ppermute | solution.py:236
  24.1 13.9 %collective-permute-start = (bf16[2,4,64,256]{3,2,1,0:T(8,128)(2,1)S(1)}, bf16[2,4,64,256]{3,2,1,0:T(8,128)(2,1)S(1)}, u32[]{:S(2)}, u32[]{:S(2)}) collective-permute-start(bf16[2,4,64,256]{3,2,1,0:T(8,128)(2,1)S(1)} %pad_maximum_fusion.own_ref), channel_id=1, source_target_pairs={{0,256},{32,288},{256,0},{288,32},{1,257},{33,289},{257,1},{289,33... | collective-permute-start | bytes 786440 | tf_op jit(solution)/shard_map/ppermute | solution.py:236
  32.1 40.2 %collective-permute-start.4 = (bf16[2048,256]{1,0:T(8,128)(2,1)}, bf16[2048,256]{1,0:T(8,128)(2,1)S(1)}, u32[]{:S(2)}, u32[]{:S(2)}) collective-permute-start(bf16[2048,256]{1,0:T(8,128)(2,1)} %get-tuple-element.17), channel_id=1, source_target_pairs={{0,272},{16,0},{256,16},{272,256},{1,273},{17,1},{257,17},{273,257... | collective-permute-start | bytes 3145736 | tf_op jit(solution)/shard_map/ppermute | solution.py:245
  34.5 37.8 %collective-permute-start.3 = (bf16[2048,256]{1,0:T(8,128)(2,1)}, bf16[2048,256]{1,0:T(8,128)(2,1)S(1)}, u32[]{:S(2)}, u32[]{:S(2)}) collective-permute-start(bf16[2048,256]{1,0:T(8,128)(2,1)} %get-tuple-element.18), channel_id=1, source_target_pairs={{0,16},{16,256},{256,272},{272,0},{1,17},{17,257},{257,273},{273,1... | collective-permute-start | bytes 3145736 | tf_op jit(solution)/shard_map/ppermute | solution.py:242
  39.8 21.5 %all-to-all-start.1 = ((bf16[4,4,64,256]{3,2,1,0:T(8,128)(2,1)}), bf16[4,4,64,256]{3,2,1,0:T(8,128)(2,1)S(1)}, u32[]{:S(2)}, u32[]{:S(2)}) async-start(bf16[4,4,64,256]{3,2,1,0:T(8,128)(2,1)} %shard_map.73), calls=%async_computation.1 | async-start | bytes 1048576 | tf_op jit(solution)/shard_map/all_to_all | solution.py:251
  62.9 19.8 %all-to-all-start.2 = ((f32[32,8,128]{2,1,0:T(8,128)}), f32[32,8,128]{2,1,0:T(8,128)S(1)}, u32[]{:S(2)}, u32[]{:S(2)}) async-start(f32[32,8,128]{2,1,0:T(8,128)} %bitcast.5), calls=%async_computation.2 | async-start | bytes 262144 | tf_op jit(solution)/shard_map/all_to_all | solution.py:254
  76.9 12.2 %collective-permute-start.5 = (bf16[512,256]{1,0:T(8,128)(2,1)}, bf16[512,256]{1,0:T(8,128)(2,1)S(1)}, u32[]{:S(2)}, u32[]{:S(2)}) collective-permute-start(bf16[512,256]{1,0:T(8,128)(2,1)} %get-tuple-element.16), channel_id=1, source_target_pairs={{0,16},{16,0},{1,17},{17,1},{2,18},{18,2},{3,19},{19,3},{4,20},{20... | collective-permute-start | bytes 786440 | tf_op jit(solution)/shard_map/ppermute | solution.py:259
  83.4 14.1 %all-to-all-start.3 = ((bf16[32,8,128]{2,1,0:T(8,128)(2,1)}), bf16[32,8,128]{2,1,0:T(8,128)(2,1)S(1)}, u32[]{:S(2)}, u32[]{:S(2)}) async-start(bf16[32,8,128]{2,1,0:T(8,128)(2,1)} %shard_map.75), calls=%async_computation.3 | async-start | bytes 131072 | tf_op jit(solution)/shard_map/all_to_all | solution.py:255
Sparse Core Ops, SparseCore 0:
  9.4 54.9 all-gather.1

commit v9 on v8

--- a/solution.py
+++ b/solution.py
@@ -17,7 +17,7 @@
 ZS = 8
 PEERS = 4
 HALF = 4096
-DEPTH = 1024
+DEPTH = 512
 
 ANY = pl.BlockSpec(memory_space=pl.ANY)
 SMEM = pl.BlockSpec(memory_space=pltpu.SMEM)
@@ -134,26 +134,27 @@
     )(parts)
 
 
-def base_kernel(half_ref, t_ref, wa_ref, wb_ref, w_ref, theirs_ref, ours_ref, t, wo, acc, sems):
+def base_kernel(half_ref, t_ref, wa_ref, wb_ref, w_ref, theirs_ref, ours_ref, t, wt, wo, acc, sems):
     count = HALF // DEPTH
     per_quarter = count // 2
     copies = []
     for i in range(count):
         cols = slice(i * DEPTH, (i + 1) * DEPTH)
+        source = wa_ref if i < per_quarter else wb_ref
+        rows = pl.ds((i % per_quarter) * DEPTH, DEPTH)
         start = pl.multiple_of(half_ref[0] * HALF + i * DEPTH, DEPTH)
-        pair = (
+        trio = (
             pltpu.make_async_copy(t_ref.at[:, cols], t.at[i], sems.at[i, 0]),
-            pltpu.make_async_copy(w_ref.at[pl.ds(start, DEPTH), :], wo.at[i], sems.at[i, 1]),
+            pltpu.make_async_copy(source.at[rows, :], wt.at[i], sems.at[i, 1]),
+            pltpu.make_async_copy(w_ref.at[pl.ds(start, DEPTH), :], wo.at[i], sems.at[i, 2]),
         )
-        for copy in pair:
+        for copy in trio:
             copy.start()
-        copies.append(pair)
+        copies.append(trio)
     for i in range(count):
         for copy in copies[i]:
             copy.wait()
-        source = wa_ref if i < per_quarter else wb_ref
-        rows = slice((i % per_quarter) * DEPTH, (i % per_quarter + 1) * DEPTH)
-        theirs = jnp.dot(t[i], source[rows, :], preferred_element_type=jnp.float32)
+        theirs = jnp.dot(t[i], wt[i], preferred_element_type=jnp.float32)
         ours = jnp.dot(t[i], wo[i], preferred_element_type=jnp.float32)
         if i == 0:
             acc[...] = theirs
@@ -172,15 +173,16 @@
             jax.ShapeDtypeStruct((ROWS, WIDTH), jnp.bfloat16),
             jax.ShapeDtypeStruct((ROWS, WIDTH), jnp.float32),
         ],
-        in_specs=[SMEM, ANY, VMEM, VMEM, ANY],
+        in_specs=[SMEM, ANY, ANY, ANY, ANY],
         out_specs=[VMEM, VMEM],
         scratch_shapes=[
             pltpu.VMEM((count, ROWS, DEPTH), jnp.bfloat16),
             pltpu.VMEM((count, DEPTH, WIDTH), jnp.bfloat16),
+            pltpu.VMEM((count, DEPTH, WIDTH), jnp.bfloat16),
             pltpu.VMEM((ROWS, WIDTH), jnp.float32),
-            pltpu.SemaphoreType.DMA((count, 2)),
-        ],
-        compiler_params=vmem(51),
+            pltpu.SemaphoreType.DMA((count, 3)),
+        ],
+        compiler_params=vmem(53),
         cost_estimate=pl.CostEstimate(
             flops=4 * ROWS * HALF * WIDTH, bytes_accessed=10 << 20, transcendentals=0
         ),

time: 106 us -> 105 us (level)
  no operation moved by 1% of the time
where the time goes in v9:
time: 105 us; the launch traced here: 104 us
  starting transfers between devices  50.8 us (48%)
  waiting for transfers between devices  25.2 us (24%)
  between operations  13.6 us (13%)
  Pallas kernels  9.87 us (9%)
  local copies, waits for them, and re-layouts  3.95 us (4%)
  other arithmetic  1.07 us (1%)
    all_to_all x1, waiting for transfers between devices, body(): got = lax.all_to_all(sent, 'zh', 0, 0, tiled=True)  14.3 us
    ppermute x3, starting transfers between devices, body(): lax.ppermute(own, pair, [(i, i ^ flip) for i in range(4)])  10.7 us
    all_to_all x1, starting transfers between devices, body(): every_id = lax.all_to_all(spread, 'zh', 0, 0, tiled=True)  9.41 us
    all_to_all x1, starting transfers between devices, body(): parts = lax.all_to_all(partial.reshape(32, 8, 128), TENSOR, 0, 0)  9.35 us
    all_to_all x1, waiting for transfers between devices, body(): low = lax.all_to_all(sum_parts(parts), TENSOR, 0, 0)  8.29 us
    all_to_all x1, starting transfers between devices, body(): got = lax.all_to_all(sent, 'zh', 0, 0, tiled=True)  7.2 us
    all_to_all x1, starting transfers between devices, body(): low = lax.all_to_all(sum_parts(parts), TENSOR, 0, 0)  4.52 us
    pallas_call x1, Pallas kernels, base_products(): pl.pallas_call(base_kernel, out_shape=[jax.ShapeDtypeStruct((ROWS, WIDTH)...  4.13 us
  transfers between devices with their start and end apart: 11, of which 3 were waited for; matrix products, arithmetic and copies ran while one was open for 4% of the time, Pallas kernels for 9%

profile of v9, /device:TPU:68, one launch (start us, length us, event | category | flops | bytes accessed | tf_op | source)
XLA Modules:
  0.0 104.4 jit_solution(2499112591005481970)
XLA Ops:
  6.5 0.0 all-gather.2.cloned.1.call-start
  6.6 1.3 %broadcast_in_dim.13 = s32[4,1,2]{2,1,0:T(1,128)} broadcast(s32[2]{0:T(128)} %ids_ref.3), dimensions={2} | broadcast | bytes 40 | tf_op jit(solution)/shard_map/broadcast_in_dim | solution.py:232
  7.9 0.0 all-gather.2.cloned.1.call-update
  7.9 9.4 %all-to-all-start = ((s32[4,1,2]{2,1,0:T(1,128)}), s32[4,1,2]{2,1,0:T(1,128)S(1)}, u32[]{:S(2)}, u32[]{:S(2)}) async-start(s32[4,1,2]{2,1,0:T(1,128)} %broadcast_in_dim.13), calls=%async_computation | async-start | bytes 4096 | tf_op jit(solution)/shard_map/all_to_all | solution.py:235
  17.3 1.0 pad_maximum_fusion.own_ref
  18.3 2.4 %collective-permute-start.2 = (bf16[2,4,64,256]{3,2,1,0:T(8,128)(2,1)S(1)}, bf16[2,4,64,256]{3,2,1,0:T(8,128)(2,1)S(1)}, u32[]{:S(2)}, u32[]{:S(2)}) collective-permute-start(bf16[2,4,64,256]{3,2,1,0:T(8,128)(2,1)S(1)} %pad_maximum_fusion.own_ref), channel_id=1, source_target_pairs={{0,288},{32,256},{256,32},{288,0},{1,289},{33,257},{257,33},{289,1... | collective-permute-start | bytes 786440 | tf_op jit(solution)/shard_map/ppermute | solution.py:238
  20.7 3.4 %collective-permute-start.1 = (bf16[2,4,64,256]{3,2,1,0:T(8,128)(2,1)S(1)}, bf16[2,4,64,256]{3,2,1,0:T(8,128)(2,1)S(1)}, u32[]{:S(2)}, u32[]{:S(2)}) collective-permute-start(bf16[2,4,64,256]{3,2,1,0:T(8,128)(2,1)S(1)} %pad_maximum_fusion.own_ref), channel_id=1, source_target_pairs={{0,32},{32,0},{256,288},{288,256},{1,33},{33,1},{257,289},{289,257... | collective-permute-start | bytes 786440 | tf_op jit(solution)/shard_map/ppermute | solution.py:238
  24.1 4.9 %collective-permute-start = (bf16[2,4,64,256]{3,2,1,0:T(8,128)(2,1)S(1)}, bf16[2,4,64,256]{3,2,1,0:T(8,128)(2,1)S(1)}, u32[]{:S(2)}, u32[]{:S(2)}) collective-permute-start(bf16[2,4,64,256]{3,2,1,0:T(8,128)(2,1)S(1)} %pad_maximum_fusion.own_ref), channel_id=1, source_target_pairs={{0,256},{32,288},{256,0},{288,32},{1,257},{33,289},{257,1},{289,33... | collective-permute-start | bytes 786440 | tf_op jit(solution)/shard_map/ppermute | solution.py:238
  29.0 0.0 all-to-all-done.ids_ref
  29.1 2.7 %constant_dynamic-slice_fusion = (bf16[2048,256]{1,0:T(8,128)(2,1)}, bf16[2048,256]{1,0:T(8,128)(2,1)S(1)}) fusion(bf16[8192,256]{1,0:T(8,128)(2,1)} %w_ref, s32[]{:T(128)S(6)} %select_n.7, s32[]{:T(128)S(6)} %select_n.6), kind=kLoop, calls=%fused_computation.2 | loop fusion | bytes 4194312 | tf_op jit(solution)/shard_map/dynamic_slice | solution.py:248
  31.7 2.4 %collective-permute-start.4 = (bf16[2048,256]{1,0:T(8,128)(2,1)}, bf16[2048,256]{1,0:T(8,128)(2,1)}, u32[]{:S(2)}, u32[]{:S(2)}) collective-permute-start(bf16[2048,256]{1,0:T(8,128)(2,1)} %get-tuple-element.17), channel_id=1, source_target_pairs={{0,272},{16,0},{256,16},{272,256},{1,273},{17,1},{257,17},{273,257... | collective-permute-start | bytes 3145736 | tf_op jit(solution)/shard_map/ppermute | solution.py:247
  34.1 3.4 %collective-permute-start.3 = (bf16[2048,256]{1,0:T(8,128)(2,1)S(1)}, bf16[2048,256]{1,0:T(8,128)(2,1)}, u32[]{:S(2)}, u32[]{:S(2)}) collective-permute-start(bf16[2048,256]{1,0:T(8,128)(2,1)S(1)} %get-tuple-element.18), channel_id=1, source_target_pairs={{0,16},{16,256},{256,272},{272,0},{1,17},{17,257},{257,273},{273,1... | collective-permute-start | bytes 3145736 | tf_op jit(solution)/shard_map/ppermute | solution.py:244
  37.6 0.1 pad_add_fusion.place_ref
  37.6 0.0 collective-permute-done.2.xz_ref
  37.6 0.0 collective-permute-done.1.z_ref
  37.6 0.0 collective-permute-done.x_ref
  37.7 1.7 %shard_map.73 = bf16[4,4,64,256]{3,2,1,0:T(8,128)(2,1)} custom-call(s32[4,1,2]{2,1,0:T(1,128)S(1)} %all-to-all-done.ids_ref, s32[64]{0:T(128)S(1)} %copy-done.1, s32[2]{0:T(128)S(1)} %pad_add_fusion.place_ref, bf16[2,4,64,256]{3,2,1,0:T(8,128)(2,1)S(1)} %pad_maximum_fusion.own_ref, bf16[2,4,64,256]{3,2,1,0:T(8,128)(2,1)S(1)} %collective-permute-done.x_ref, ...), custom_call_target="tpu_custom_call" | custom-call | bytes 2097152 | tf_op jit(solution)/shard_map/pallas_call | solution.py:50
  39.4 7.2 %all-to-all-start.1 = ((bf16[4,4,64,256]{3,2,1,0:T(8,128)(2,1)}), bf16[4,4,64,256]{3,2,1,0:T(8,128)(2,1)S(1)}, u32[]{:S(2)}, u32[]{:S(2)}) async-start(bf16[4,4,64,256]{3,2,1,0:T(8,128)(2,1)} %shard_map.73), calls=%async_computation.1 | async-start | bytes 1048576 | tf_op jit(solution)/shard_map/all_to_all | solution.py:253
  46.6 14.3 %all-to-all-done.1.got_ref = bf16[4,4,64,256]{3,2,1,0:T(8,128)(2,1)S(1)} async-done(((bf16[4,4,64,256]{3,2,1,0:T(8,128)(2,1)}), bf16[4,4,64,256]{3,2,1,0:T(8,128)(2,1)S(1)}, u32[]{:S(2)}, u32[]{:S(2)}) %all-to-all-start.1) | async-done | bytes 524320 | tf_op jit(solution)/shard_map/all_to_all | solution.py:253
  60.9 1.6 %shard_map.74 = f32[256,128]{1,0:T(8,128)} custom-call(s32[2]{0:T(128)S(1)} %copy-done.2, s32[64]{0:T(128)S(1)} %copy-done.1, s32[4]{0:T(128)S(1)} %copy-done.3, s32[1]{0:T(128)} %bitcast.dp_ref, bf16[512,256]{1,0:T(8,128)(2,1)S(1)} %copy-done, bf16[4,4,64,256]{3,2,1,0:T(8,128)(2,1)S(1)} %all-to-all-done.1.got_ref), custom_call_target="tpu_custom_call" | custom-call | flops 16777216 | bytes 1048576 | tf_op jit(solution)/shard_map/pallas_call | solution.py:85
  62.5 9.3 %all-to-all-start.2 = ((f32[32,8,128]{2,1,0:T(8,128)}), f32[32,8,128]{2,1,0:T(8,128)S(1)}, u32[]{:S(2)}, u32[]{:S(2)}) async-start(f32[32,8,128]{2,1,0:T(8,128)} %bitcast.5), calls=%async_computation.2 | async-start | bytes 262144 | tf_op jit(solution)/shard_map/all_to_all | solution.py:256
  71.9 0.0 collective-permute-done.3.wa_ref
  71.9 0.0 all-gather.2.cloned.1.call-done.t_ref
  71.9 4.1 %shard_map.77 = (bf16[512,256]{1,0:T(8,128)(2,1)S(1)}, f32[512,256]{1,0:T(8,128)S(1)}) custom-call(s32[1]{0:T(128)} %bitcast.7.half_ref, bf16[512,4096]{1,0:T(8,128)(2,1)} %all-gather.2.cloned.1.call-done.t_ref, bf16[2048,256]{1,0:T(8,128)(2,1)} %collective-permute-done.3.wa_ref, bf16[2048,256]{1,0:T(8,128)(2,1)} %collective-permute-done.4.wb_ref, ...), custom_call_target="tpu_custom_call" | custom-call | flops 2147483648 | bytes 10485760 | tf_op jit(solution)/shard_map/pallas_call | solution.py:170
  76.1 3.7 %collective-permute-start.5 = (bf16[512,256]{1,0:T(8,128)(2,1)S(1)}, bf16[512,256]{1,0:T(8,128)(2,1)S(1)}, u32[]{:S(2)}, u32[]{:S(2)}) collective-permute-start(bf16[512,256]{1,0:T(8,128)(2,1)S(1)} %get-tuple-element.16), channel_id=1, source_target_pairs={{0,16},{16,0},{1,17},{17,1},{2,18},{18,2},{3,19},{19,3},{4,20},{20... | collective-permute-start | bytes 786440 | tf_op jit(solution)/shard_map/ppermute | solution.py:261
  79.8 2.6 %all-to-all-done.2.parts_ref = f32[32,8,128]{2,1,0:T(8,128)S(1)} async-done(((f32[32,8,128]{2,1,0:T(8,128)}), f32[32,8,128]{2,1,0:T(8,128)S(1)}, u32[]{:S(2)}, u32[]{:S(2)}) %all-to-all-start.2) | async-done | bytes 131104 | tf_op jit(solution)/shard_map/all_to_all | solution.py:256
  82.3 0.7 shard_map.75
  83.0 4.5 %all-to-all-start.3 = ((bf16[32,8,128]{2,1,0:T(8,128)(2,1)}), bf16[32,8,128]{2,1,0:T(8,128)(2,1)S(1)}, u32[]{:S(2)}, u32[]{:S(2)}) async-start(bf16[32,8,128]{2,1,0:T(8,128)(2,1)} %shard_map.75), calls=%async_computation.3 | async-start | bytes 131072 | tf_op jit(solution)/shard_map/all_to_all | solution.py:257
  87.5 0.7 shard_map.76.ups_ref
  88.3 0.0 collective-permute-done.5.recv_ref
  88.3 8.3 %all-to-all-done.3 = bf16[32,8,128]{2,1,0:T(8,128)(2,1)S(1)} async-done(((bf16[32,8,128]{2,1,0:T(8,128)(2,1)}), bf16[32,8,128]{2,1,0:T(8,128)(2,1)S(1)}, u32[]{:S(2)}, u32[]{:S(2)}) %all-to-all-start.3) | async-done | bytes 65568 | tf_op jit(solution)/shard_map/all_to_all | solution.py:257
  96.6 0.9 shard_map.79
  (10 shorter events, 0.1 us)
Async XLA Ops:
  6.5 54.3 %copy-start = (bf16[512,256]{1,0:T(8,128)(2,1)S(1)}, bf16[512,256]{1,0:T(8,128)(2,1)}, u32[]{:S(2)}) copy-start(bf16[512,256]{1,0:T(8,128)(2,1)} %tokens_ref.1) | copy-start | bytes 786436
  6.5 54.3 %copy-start.2 = (s32[2]{0:T(128)S(1)}, s32[2]{0:T(128)}, u32[]{:S(2)}) copy-start(s32[2]{0:T(128)} %ids_ref.3) | copy-start | bytes 28
  6.5 31.1 %copy-start.1 = (s32[64]{0:T(128)S(1)}, s32[64]{0:T(128)}, u32[]{:S(2)}) copy-start(s32[64]{0:T(128)} %stored_ref.5) | copy-start | bytes 772
  6.5 54.3 %copy-start.3 = (s32[4]{0:T(128)S(1)}, s32[4]{0:T(128)}, u32[]{:S(2)}) copy-start(s32[4]{0:T(128)} %seg_ref.3) | copy-start | bytes 52
  6.5 65.4 %all-gather.2.cloned.1.call-start = ((), (), s32[]{:S(2)}) async-start(), calls=%async_computation.4 | async-start | bytes 4456448 | tf_op jit(solution)/shard_map/all_gather | solution.py:234
  7.9 21.2 %all-to-all-start = ((s32[4,1,2]{2,1,0:T(1,128)}), s32[4,1,2]{2,1,0:T(1,128)S(1)}, u32[]{:S(2)}, u32[]{:S(2)}) async-start(s32[4,1,2]{2,1,0:T(1,128)} %broadcast_in_dim.13), calls=%async_computation | async-start | bytes 4096 | tf_op jit(solution)/shard_map/all_to_all | solution.py:235
  18.3 19.3 %collective-permute-start.2 = (bf16[2,4,64,256]{3,2,1,0:T(8,128)(2,1)S(1)}, bf16[2,4,64,256]{3,2,1,0:T(8,128)(2,1)S(1)}, u32[]{:S(2)}, u32[]{:S(2)}) collective-permute-start(bf16[2,4,64,256]{3,2,1,0:T(8,128)(2,1)S(1)} %pad_maximum_fusion.own_ref), channel_id=1, source_target_pairs={{0,288},{32,256},{256,32},{288,0},{1,289},{33,257},{257,33},{289,1... | collective-permute-start | bytes 786440 | tf_op jit(solution)/shard_map/ppermute | solution.py:238
  20.7 16.9 %collective-permute-start.1 = (bf16[2,4,64,256]{3,2,1,0:T(8,128)(2,1)S(1)}, bf16[2,4,64,256]{3,2,1,0:T(8,128)(2,1)S(1)}, u32[]{:S(2)}, u32[]{:S(2)}) collective-permute-start(bf16[2,4,64,256]{3,2,1,0:T(8,128)(2,1)S(1)} %pad_maximum_fusion.own_ref), channel_id=1, source_target_pairs={{0,32},{32,0},{256,288},{288,256},{1,33},{33,1},{257,289},{289,257... | collective-permute-start | bytes 786440 | tf_op jit(solution)/shard_map/ppermute | solution.py:238
  24.1 13.6 %collective-permute-start = (bf16[2,4,64,256]{3,2,1,0:T(8,128)(2,1)S(1)}, bf16[2,4,64,256]{3,2,1,0:T(8,128)(2,1)S(1)}, u32[]{:S(2)}, u32[]{:S(2)}) collective-permute-start(bf16[2,4,64,256]{3,2,1,0:T(8,128)(2,1)S(1)} %pad_maximum_fusion.own_ref), channel_id=1, source_target_pairs={{0,256},{32,288},{256,0},{288,32},{1,257},{33,289},{257,1},{289,33... | collective-permute-start | bytes 786440 | tf_op jit(solution)/shard_map/ppermute | solution.py:238
  31.7 40.2 %collective-permute-start.4 = (bf16[2048,256]{1,0:T(8,128)(2,1)}, bf16[2048,256]{1,0:T(8,128)(2,1)}, u32[]{:S(2)}, u32[]{:S(2)}) collective-permute-start(bf16[2048,256]{1,0:T(8,128)(2,1)} %get-tuple-element.17), channel_id=1, source_target_pairs={{0,272},{16,0},{256,16},{272,256},{1,273},{17,1},{257,17},{273,257... | collective-permute-start | bytes 3145736 | tf_op jit(solution)/shard_map/ppermute | solution.py:247
  34.1 37.7 %collective-permute-start.3 = (bf16[2048,256]{1,0:T(8,128)(2,1)S(1)}, bf16[2048,256]{1,0:T(8,128)(2,1)}, u32[]{:S(2)}, u32[]{:S(2)}) collective-permute-start(bf16[2048,256]{1,0:T(8,128)(2,1)S(1)} %get-tuple-element.18), channel_id=1, source_target_pairs={{0,16},{16,256},{256,272},{272,0},{1,17},{17,257},{257,273},{273,1... | collective-permute-start | bytes 3145736 | tf_op jit(solution)/shard_map/ppermute | solution.py:244
  39.4 21.5 %all-to-all-start.1 = ((bf16[4,4,64,256]{3,2,1,0:T(8,128)(2,1)}), bf16[4,4,64,256]{3,2,1,0:T(8,128)(2,1)S(1)}, u32[]{:S(2)}, u32[]{:S(2)}) async-start(bf16[4,4,64,256]{3,2,1,0:T(8,128)(2,1)} %shard_map.73), calls=%async_computation.1 | async-start | bytes 1048576 | tf_op jit(solution)/shard_map/all_to_all | solution.py:253
  62.5 19.8 %all-to-all-start.2 = ((f32[32,8,128]{2,1,0:T(8,128)}), f32[32,8,128]{2,1,0:T(8,128)S(1)}, u32[]{:S(2)}, u32[]{:S(2)}) async-start(f32[32,8,128]{2,1,0:T(8,128)} %bitcast.5), calls=%async_computation.2 | async-start | bytes 262144 | tf_op jit(solution)/shard_map/all_to_all | solution.py:256
  76.1 12.2 %collective-permute-start.5 = (bf16[512,256]{1,0:T(8,128)(2,1)S(1)}, bf16[512,256]{1,0:T(8,128)(2,1)S(1)}, u32[]{:S(2)}, u32[]{:S(2)}) collective-permute-start(bf16[512,256]{1,0:T(8,128)(2,1)S(1)} %get-tuple-element.16), channel_id=1, source_target_pairs={{0,16},{16,0},{1,17},{17,1},{2,18},{18,2},{3,19},{19,3},{4,20},{20... | collective-permute-start | bytes 786440 | tf_op jit(solution)/shard_map/ppermute | solution.py:261
  83.0 13.6 %all-to-all-start.3 = ((bf16[32,8,128]{2,1,0:T(8,128)(2,1)}), bf16[32,8,128]{2,1,0:T(8,128)(2,1)S(1)}, u32[]{:S(2)}, u32[]{:S(2)}) async-start(bf16[32,8,128]{2,1,0:T(8,128)(2,1)} %shard_map.75), calls=%async_computation.3 | async-start | bytes 131072 | tf_op jit(solution)/shard_map/all_to_all | solution.py:257
Sparse Core Ops, SparseCore 0:
  9.4 54.7 all-gather.1

commit v10 on v9

--- a/solution.py
+++ b/solution.py
@@ -9,6 +9,7 @@
 DP = ("xh", "zh", "zl")
 X = ("xh", "xl")
 TENSOR = ("xl", "y", "c")
+PEER_ORDER = ("c", "y", "xl")
 ROWS = 512
 SEG = 128
 RANK = 64
@@ -28,7 +29,7 @@
     return pltpu.CompilerParams(vmem_limit_bytes=mib << 20)
 
 
-def select_kernel(ids_ref, stored_ref, place_ref, own_ref, x_ref, z_ref, xz_ref, out_ref):
+def select_kernel(ids_ref, stored_ref, place_ref, own_ref, x_ref, z_ref, xz_ref, out_ref, hold, sems):
     held = (own_ref, x_ref, z_ref, xz_ref)
     for zh in range(PEERS):
         for r in range(2):
@@ -43,7 +44,10 @@
                 @pl.when(which == j)
                 def _(zh=zh, r=r, slot=slot, j=j):
                     for part in range(2):
-                        out_ref[zh, 2 * r + part] = held[j][part, slot]
+                        hold[zh, 2 * r + part] = held[j][part, slot]
+        pltpu.make_async_copy(hold.at[zh], out_ref.at[zh], sems.at[zh]).start()
+    for zh in range(PEERS):
+        pltpu.make_async_copy(hold.at[zh], out_ref.at[zh], sems.at[zh]).wait()
 
 
 def select(ids, stored, place, own, x, z, xz):
@@ -51,7 +55,11 @@
         select_kernel,
         out_shape=jax.ShapeDtypeStruct((PEERS, 4, RANK, WIDTH), own.dtype),
         in_specs=[SMEM, SMEM, SMEM, VMEM, VMEM, VMEM, VMEM],
-        out_specs=VMEM,
+        out_specs=ANY,
+        scratch_shapes=[
+            pltpu.VMEM((PEERS, 4, RANK, WIDTH), own.dtype),
+            pltpu.SemaphoreType.DMA((PEERS,)),
+        ],
         compiler_params=vmem(8),
         cost_estimate=pl.CostEstimate(flops=0, bytes_accessed=2 << 20, transcendentals=0),
     )(ids, stored, place, own, x, z, xz)
@@ -253,8 +261,8 @@
     got = lax.all_to_all(sent, "zh", 0, 0, tiled=True)
 
     partial = down_product(request_ids, stored_row, segment_request, dp, tokens, got)
-    parts = lax.all_to_all(partial.reshape(32, 8, 128), TENSOR, 0, 0)
-    low = lax.all_to_all(sum_parts(parts), TENSOR, 0, 0)
+    parts = lax.all_to_all(partial.reshape(32, 8, 128), PEER_ORDER, 0, 0)
+    low = lax.all_to_all(sum_parts(parts), PEER_ORDER, 0, 0)
 
     weight, _ = lax.optimization_barrier((weight, partial))
     theirs, ours = base_products(xl[None], gathered, wa, wb, weight)

time: 105 us -> 105 us (level)
  transfers between devices with their start and end apart: 11 -> 11, of which waited for: 3 -> 3; matrix products, arithmetic and copies ran while one was open for 4% -> 4% of each run, Pallas kernels for 9% -> 8%
where the time goes in v10:
time: 105 us; the launch traced here: 104 us
  starting transfers between devices  51.3 us (49%)
  waiting for transfers between devices  24.3 us (23%)
  between operations  13.6 us (13%)
  Pallas kernels  9.77 us (9%)
  local copies, waits for them, and re-layouts  3.95 us (4%)
  other arithmetic  1.07 us (1%)
    all_to_all x1, waiting for transfers between devices, body(): got = lax.all_to_all(sent, 'zh', 0, 0, tiled=True)  14.3 us
    ppermute x3, starting transfers between devices, body(): lax.ppermute(own, pair, [(i, i ^ flip) for i in range(4)])  10.7 us
    all_to_all x1, starting transfers between devices, body(): every_id = lax.all_to_all(spread, 'zh', 0, 0, tiled=True)  9.41 us
    all_to_all x1, starting transfers between devices, body(): parts = lax.all_to_all(partial.reshape(32, 8, 128), PEER_ORDER, 0, 0)  9.35 us
    all_to_all x1, waiting for transfers between devices, body(): low = lax.all_to_all(sum_parts(parts), PEER_ORDER, 0, 0)  8.03 us
    all_to_all x1, starting transfers between devices, body(): got = lax.all_to_all(sent, 'zh', 0, 0, tiled=True)  7.21 us
    all_to_all x1, starting transfers between devices, body(): low = lax.all_to_all(sum_parts(parts), PEER_ORDER, 0, 0)  5.08 us
    pallas_call x1, Pallas kernels, base_products(): pl.pallas_call(base_kernel, out_shape=[jax.ShapeDtypeStruct((ROWS, WIDTH)...  4.14 us
  transfers between devices with their start and end apart: 11, of which 3 were waited for; matrix products, arithmetic and copies ran while one was open for 4% of the time, Pallas kernels for 8%

profile of v10, /device:TPU:68, one launch (start us, length us, event | category | flops | bytes accessed | tf_op | source)
XLA Modules:
  0.0 104.0 jit_solution(17899386077325595292)
XLA Ops:
  6.5 0.0 all-gather.2.cloned.1.call-start
  6.6 1.3 %broadcast_in_dim.13 = s32[4,1,2]{2,1,0:T(1,128)} broadcast(s32[2]{0:T(128)} %ids_ref.3), dimensions={2} | broadcast | bytes 40 | tf_op jit(solution)/shard_map/broadcast_in_dim | solution.py:240
  7.9 0.0 all-gather.2.cloned.1.call-update
  7.9 9.4 %all-to-all-start = ((s32[4,1,2]{2,1,0:T(1,128)}), s32[4,1,2]{2,1,0:T(1,128)S(1)}, u32[]{:S(2)}, u32[]{:S(2)}) async-start(s32[4,1,2]{2,1,0:T(1,128)} %broadcast_in_dim.13), calls=%async_computation | async-start | bytes 4096 | tf_op jit(solution)/shard_map/all_to_all | solution.py:243
  17.3 1.0 pad_maximum_fusion.own_ref
  18.3 2.4 %collective-permute-start.2 = (bf16[2,4,64,256]{3,2,1,0:T(8,128)(2,1)S(1)}, bf16[2,4,64,256]{3,2,1,0:T(8,128)(2,1)S(1)}, u32[]{:S(2)}, u32[]{:S(2)}) collective-permute-start(bf16[2,4,64,256]{3,2,1,0:T(8,128)(2,1)S(1)} %pad_maximum_fusion.own_ref), channel_id=1, source_target_pairs={{0,288},{32,256},{256,32},{288,0},{1,289},{33,257},{257,33},{289,1... | collective-permute-start | bytes 786440 | tf_op jit(solution)/shard_map/ppermute | solution.py:246
  20.7 3.4 %collective-permute-start.1 = (bf16[2,4,64,256]{3,2,1,0:T(8,128)(2,1)S(1)}, bf16[2,4,64,256]{3,2,1,0:T(8,128)(2,1)S(1)}, u32[]{:S(2)}, u32[]{:S(2)}) collective-permute-start(bf16[2,4,64,256]{3,2,1,0:T(8,128)(2,1)S(1)} %pad_maximum_fusion.own_ref), channel_id=1, source_target_pairs={{0,32},{32,0},{256,288},{288,256},{1,33},{33,1},{257,289},{289,257... | collective-permute-start | bytes 786440 | tf_op jit(solution)/shard_map/ppermute | solution.py:246
  24.1 4.9 %collective-permute-start = (bf16[2,4,64,256]{3,2,1,0:T(8,128)(2,1)S(1)}, bf16[2,4,64,256]{3,2,1,0:T(8,128)(2,1)S(1)}, u32[]{:S(2)}, u32[]{:S(2)}) collective-permute-start(bf16[2,4,64,256]{3,2,1,0:T(8,128)(2,1)S(1)} %pad_maximum_fusion.own_ref), channel_id=1, source_target_pairs={{0,256},{32,288},{256,0},{288,32},{1,257},{33,289},{257,1},{289,33... | collective-permute-start | bytes 786440 | tf_op jit(solution)/shard_map/ppermute | solution.py:246
  29.0 0.0 all-to-all-done.ids_ref
  29.1 2.7 %constant_dynamic-slice_fusion = (bf16[2048,256]{1,0:T(8,128)(2,1)}, bf16[2048,256]{1,0:T(8,128)(2,1)S(1)}) fusion(bf16[8192,256]{1,0:T(8,128)(2,1)} %w_ref, s32[]{:T(128)S(6)} %select_n.7, s32[]{:T(128)S(6)} %select_n.6), kind=kLoop, calls=%fused_computation.2 | loop fusion | bytes 4194312 | tf_op jit(solution)/shard_map/dynamic_slice | solution.py:256
  31.7 2.4 %collective-permute-start.4 = (bf16[2048,256]{1,0:T(8,128)(2,1)}, bf16[2048,256]{1,0:T(8,128)(2,1)}, u32[]{:S(2)}, u32[]{:S(2)}) collective-permute-start(bf16[2048,256]{1,0:T(8,128)(2,1)} %get-tuple-element.17), channel_id=1, source_target_pairs={{0,272},{16,0},{256,16},{272,256},{1,273},{17,1},{257,17},{273,257... | collective-permute-start | bytes 3145736 | tf_op jit(solution)/shard_map/ppermute | solution.py:255
  34.1 3.4 %collective-permute-start.3 = (bf16[2048,256]{1,0:T(8,128)(2,1)S(1)}, bf16[2048,256]{1,0:T(8,128)(2,1)}, u32[]{:S(2)}, u32[]{:S(2)}) collective-permute-start(bf16[2048,256]{1,0:T(8,128)(2,1)S(1)} %get-tuple-element.18), channel_id=1, source_target_pairs={{0,16},{16,256},{256,272},{272,0},{1,17},{17,257},{257,273},{273,1... | collective-permute-start | bytes 3145736 | tf_op jit(solution)/shard_map/ppermute | solution.py:252
  37.6 0.1 pad_add_fusion.place_ref
  37.6 0.0 collective-permute-done.2.xz_ref
  37.6 0.0 collective-permute-done.1.z_ref
  37.6 0.0 collective-permute-done.x_ref
  37.7 1.6 %shard_map.73 = bf16[4,4,64,256]{3,2,1,0:T(8,128)(2,1)} custom-call(s32[4,1,2]{2,1,0:T(1,128)S(1)} %all-to-all-done.ids_ref, s32[64]{0:T(128)S(1)} %copy-done.1, s32[2]{0:T(128)S(1)} %pad_add_fusion.place_ref, bf16[2,4,64,256]{3,2,1,0:T(8,128)(2,1)S(1)} %pad_maximum_fusion.own_ref, bf16[2,4,64,256]{3,2,1,0:T(8,128)(2,1)S(1)} %collective-permute-done.x_ref, ...), custom_call_target="tpu_custom_call" | custom-call | bytes 2097152 | tf_op jit(solution)/shard_map/pallas_call | solution.py:54
  39.3 7.2 %all-to-all-start.1 = ((bf16[4,4,64,256]{3,2,1,0:T(8,128)(2,1)}), bf16[4,4,64,256]{3,2,1,0:T(8,128)(2,1)S(1)}, u32[]{:S(2)}, u32[]{:S(2)}) async-start(bf16[4,4,64,256]{3,2,1,0:T(8,128)(2,1)} %shard_map.73), calls=%async_computation.1 | async-start | bytes 1048576 | tf_op jit(solution)/shard_map/all_to_all | solution.py:261
  46.5 14.3 %all-to-all-done.1.got_ref = bf16[4,4,64,256]{3,2,1,0:T(8,128)(2,1)S(1)} async-done(((bf16[4,4,64,256]{3,2,1,0:T(8,128)(2,1)}), bf16[4,4,64,256]{3,2,1,0:T(8,128)(2,1)S(1)}, u32[]{:S(2)}, u32[]{:S(2)}) %all-to-all-start.1) | async-done | bytes 524320 | tf_op jit(solution)/shard_map/all_to_all | solution.py:261
  60.8 1.6 %shard_map.74 = f32[256,128]{1,0:T(8,128)} custom-call(s32[2]{0:T(128)S(1)} %copy-done.2, s32[64]{0:T(128)S(1)} %copy-done.1, s32[4]{0:T(128)S(1)} %copy-done.3, s32[1]{0:T(128)} %bitcast.dp_ref, bf16[512,256]{1,0:T(8,128)(2,1)S(1)} %copy-done, bf16[4,4,64,256]{3,2,1,0:T(8,128)(2,1)S(1)} %all-to-all-done.1.got_ref), custom_call_target="tpu_custom_call" | custom-call | flops 16777216 | bytes 1048576 | tf_op jit(solution)/shard_map/pallas_call | solution.py:93
  62.4 9.3 %all-to-all-start.2 = ((f32[32,8,128]{2,1,0:T(8,128)}), f32[32,8,128]{2,1,0:T(8,128)S(1)}, u32[]{:S(2)}, u32[]{:S(2)}) async-start(f32[32,8,128]{2,1,0:T(8,128)} %bitcast.5), calls=%async_computation.2 | async-start | bytes 262144 | tf_op jit(solution)/shard_map/all_to_all | solution.py:264
  71.8 0.0 collective-permute-done.4.wb_ref
  71.8 0.0 collective-permute-done.3.wa_ref
  71.8 0.0 all-gather.2.cloned.1.call-done.t_ref
  71.8 4.1 %shard_map.77 = (bf16[512,256]{1,0:T(8,128)(2,1)S(1)}, f32[512,256]{1,0:T(8,128)S(1)}) custom-call(s32[1]{0:T(128)} %bitcast.7.half_ref, bf16[512,4096]{1,0:T(8,128)(2,1)} %all-gather.2.cloned.1.call-done.t_ref, bf16[2048,256]{1,0:T(8,128)(2,1)} %collective-permute-done.3.wa_ref, bf16[2048,256]{1,0:T(8,128)(2,1)} %collective-permute-done.4.wb_ref, ...), custom_call_target="tpu_custom_call" | custom-call | flops 2147483648 | bytes 10485760 | tf_op jit(solution)/shard_map/pallas_call | solution.py:178
  76.0 3.7 %collective-permute-start.5 = (bf16[512,256]{1,0:T(8,128)(2,1)S(1)}, bf16[512,256]{1,0:T(8,128)(2,1)S(1)}, u32[]{:S(2)}, u32[]{:S(2)}) collective-permute-start(bf16[512,256]{1,0:T(8,128)(2,1)S(1)} %get-tuple-element.16), channel_id=1, source_target_pairs={{0,16},{16,0},{1,17},{17,1},{2,18},{18,2},{3,19},{19,3},{4,20},{20... | collective-permute-start | bytes 786440 | tf_op jit(solution)/shard_map/ppermute | solution.py:269
  79.7 2.0 %all-to-all-done.2.parts_ref = f32[32,8,128]{2,1,0:T(8,128)S(1)} async-done(((f32[32,8,128]{2,1,0:T(8,128)}), f32[32,8,128]{2,1,0:T(8,128)S(1)}, u32[]{:S(2)}, u32[]{:S(2)}) %all-to-all-start.2) | async-done | bytes 131104 | tf_op jit(solution)/shard_map/all_to_all | solution.py:264
  81.7 0.7 shard_map.75
  82.3 5.1 %all-to-all-start.3 = ((bf16[32,8,128]{2,1,0:T(8,128)(2,1)}), bf16[32,8,128]{2,1,0:T(8,128)(2,1)S(1)}, u32[]{:S(2)}, u32[]{:S(2)}) async-start(bf16[32,8,128]{2,1,0:T(8,128)(2,1)} %shard_map.75), calls=%async_computation.3 | async-start | bytes 131072 | tf_op jit(solution)/shard_map/all_to_all | solution.py:265
  87.4 0.7 shard_map.76.ups_ref
  88.2 8.0 %all-to-all-done.3 = bf16[32,8,128]{2,1,0:T(8,128)(2,1)S(1)} async-done(((bf16[32,8,128]{2,1,0:T(8,128)(2,1)}), bf16[32,8,128]{2,1,0:T(8,128)(2,1)S(1)}, u32[]{:S(2)}, u32[]{:S(2)}) %all-to-all-start.3) | async-done | bytes 65568 | tf_op jit(solution)/shard_map/all_to_all | solution.py:265
  96.2 0.9 shard_map.79
  (10 shorter events, 0.1 us)
Async XLA Ops:
  6.5 54.2 %copy-start = (bf16[512,256]{1,0:T(8,128)(2,1)S(1)}, bf16[512,256]{1,0:T(8,128)(2,1)}, u32[]{:S(2)}) copy-start(bf16[512,256]{1,0:T(8,128)(2,1)} %tokens_ref.1) | copy-start | bytes 786436
  6.5 54.2 %copy-start.2 = (s32[2]{0:T(128)S(1)}, s32[2]{0:T(128)}, u32[]{:S(2)}) copy-start(s32[2]{0:T(128)} %ids_ref.3) | copy-start | bytes 28
  6.5 31.1 %copy-start.1 = (s32[64]{0:T(128)S(1)}, s32[64]{0:T(128)}, u32[]{:S(2)}) copy-start(s32[64]{0:T(128)} %stored_ref.5) | copy-start | bytes 772
  6.5 54.2 %copy-start.3 = (s32[4]{0:T(128)S(1)}, s32[4]{0:T(128)}, u32[]{:S(2)}) copy-start(s32[4]{0:T(128)} %seg_ref.3) | copy-start | bytes 52
  6.5 65.3 %all-gather.2.cloned.1.call-start = ((), (), s32[]{:S(2)}) async-start(), calls=%async_computation.4 | async-start | bytes 4456448 | tf_op jit(solution)/shard_map/all_gather | solution.py:242
  7.9 21.2 %all-to-all-start = ((s32[4,1,2]{2,1,0:T(1,128)}), s32[4,1,2]{2,1,0:T(1,128)S(1)}, u32[]{:S(2)}, u32[]{:S(2)}) async-start(s32[4,1,2]{2,1,0:T(1,128)} %broadcast_in_dim.13), calls=%async_computation | async-start | bytes 4096 | tf_op jit(solution)/shard_map/all_to_all | solution.py:243
  18.3 19.3 %collective-permute-start.2 = (bf16[2,4,64,256]{3,2,1,0:T(8,128)(2,1)S(1)}, bf16[2,4,64,256]{3,2,1,0:T(8,128)(2,1)S(1)}, u32[]{:S(2)}, u32[]{:S(2)}) collective-permute-start(bf16[2,4,64,256]{3,2,1,0:T(8,128)(2,1)S(1)} %pad_maximum_fusion.own_ref), channel_id=1, source_target_pairs={{0,288},{32,256},{256,32},{288,0},{1,289},{33,257},{257,33},{289,1... | collective-permute-start | bytes 786440 | tf_op jit(solution)/shard_map/ppermute | solution.py:246
  20.7 16.9 %collective-permute-start.1 = (bf16[2,4,64,256]{3,2,1,0:T(8,128)(2,1)S(1)}, bf16[2,4,64,256]{3,2,1,0:T(8,128)(2,1)S(1)}, u32[]{:S(2)}, u32[]{:S(2)}) collective-permute-start(bf16[2,4,64,256]{3,2,1,0:T(8,128)(2,1)S(1)} %pad_maximum_fusion.own_ref), channel_id=1, source_target_pairs={{0,32},{32,0},{256,288},{288,256},{1,33},{33,1},{257,289},{289,257... | collective-permute-start | bytes 786440 | tf_op jit(solution)/shard_map/ppermute | solution.py:246
  24.1 13.6 %collective-permute-start = (bf16[2,4,64,256]{3,2,1,0:T(8,128)(2,1)S(1)}, bf16[2,4,64,256]{3,2,1,0:T(8,128)(2,1)S(1)}, u32[]{:S(2)}, u32[]{:S(2)}) collective-permute-start(bf16[2,4,64,256]{3,2,1,0:T(8,128)(2,1)S(1)} %pad_maximum_fusion.own_ref), channel_id=1, source_target_pairs={{0,256},{32,288},{256,0},{288,32},{1,257},{33,289},{257,1},{289,33... | collective-permute-start | bytes 786440 | tf_op jit(solution)/shard_map/ppermute | solution.py:246
  31.7 40.1 %collective-permute-start.4 = (bf16[2048,256]{1,0:T(8,128)(2,1)}, bf16[2048,256]{1,0:T(8,128)(2,1)}, u32[]{:S(2)}, u32[]{:S(2)}) collective-permute-start(bf16[2048,256]{1,0:T(8,128)(2,1)} %get-tuple-element.17), channel_id=1, source_target_pairs={{0,272},{16,0},{256,16},{272,256},{1,273},{17,1},{257,17},{273,257... | collective-permute-start | bytes 3145736 | tf_op jit(solution)/shard_map/ppermute | solution.py:255
  34.1 37.7 %collective-permute-start.3 = (bf16[2048,256]{1,0:T(8,128)(2,1)S(1)}, bf16[2048,256]{1,0:T(8,128)(2,1)}, u32[]{:S(2)}, u32[]{:S(2)}) collective-permute-start(bf16[2048,256]{1,0:T(8,128)(2,1)S(1)} %get-tuple-element.18), channel_id=1, source_target_pairs={{0,16},{16,256},{256,272},{272,0},{1,17},{17,257},{257,273},{273,1... | collective-permute-start | bytes 3145736 | tf_op jit(solution)/shard_map/ppermute | solution.py:252
  39.3 21.5 %all-to-all-start.1 = ((bf16[4,4,64,256]{3,2,1,0:T(8,128)(2,1)}), bf16[4,4,64,256]{3,2,1,0:T(8,128)(2,1)S(1)}, u32[]{:S(2)}, u32[]{:S(2)}) async-start(bf16[4,4,64,256]{3,2,1,0:T(8,128)(2,1)} %shard_map.73), calls=%async_computation.1 | async-start | bytes 1048576 | tf_op jit(solution)/shard_map/all_to_all | solution.py:261
  62.4 19.2 %all-to-all-start.2 = ((f32[32,8,128]{2,1,0:T(8,128)}), f32[32,8,128]{2,1,0:T(8,128)S(1)}, u32[]{:S(2)}, u32[]{:S(2)}) async-start(f32[32,8,128]{2,1,0:T(8,128)} %bitcast.5), calls=%async_computation.2 | async-start | bytes 262144 | tf_op jit(solution)/shard_map/all_to_all | solution.py:264
  76.0 12.2 %collective-permute-start.5 = (bf16[512,256]{1,0:T(8,128)(2,1)S(1)}, bf16[512,256]{1,0:T(8,128)(2,1)S(1)}, u32[]{:S(2)}, u32[]{:S(2)}) collective-permute-start(bf16[512,256]{1,0:T(8,128)(2,1)S(1)} %get-tuple-element.16), channel_id=1, source_target_pairs={{0,16},{16,0},{1,17},{17,1},{2,18},{18,2},{3,19},{19,3},{4,20},{20... | collective-permute-start | bytes 786440 | tf_op jit(solution)/shard_map/ppermute | solution.py:269
  82.3 13.9 %all-to-all-start.3 = ((bf16[32,8,128]{2,1,0:T(8,128)(2,1)}), bf16[32,8,128]{2,1,0:T(8,128)(2,1)S(1)}, u32[]{:S(2)}, u32[]{:S(2)}) async-start(bf16[32,8,128]{2,1,0:T(8,128)(2,1)} %shard_map.75), calls=%async_computation.3 | async-start | bytes 131072 | tf_op jit(solution)/shard_map/all_to_all | solution.py:265
Sparse Core Ops, SparseCore 0:
  9.4 54.7 all-gather.1

commit v11 on v10

--- a/solution.py
+++ b/solution.py
@@ -190,7 +190,7 @@
             pltpu.VMEM((ROWS, WIDTH), jnp.float32),
             pltpu.SemaphoreType.DMA((count, 3)),
         ],
-        compiler_params=vmem(53),
+        compiler_params=vmem(54),
         cost_estimate=pl.CostEstimate(
             flops=4 * ROWS * HALF * WIDTH, bytes_accessed=10 << 20, transcendentals=0
         ),

time: 105 us -> 106 us (level)
  the two profiles are of different devices: /device:TPU:68 before, /device:TPU:1 now
where the time goes in v11:
time: 106 us; the launch traced here: 105 us
  starting transfers between devices  58.9 us (56%)
  waiting for transfers between devices  17 us (16%)
  between operations  13.6 us (13%)
  Pallas kernels  10.6 us (10%)
  local copies, waits for them, and re-layouts  4.01 us (4%)
  other arithmetic  1.07 us (1%)
    all_to_all x1, starting transfers between devices, body(): parts = lax.all_to_all(partial.reshape(32, 8, 128), PEER_ORDER, 0, 0)  15.3 us
    all_to_all x1, starting transfers between devices, body(): every_id = lax.all_to_all(spread, 'zh', 0, 0, tiled=True)  10.9 us
    ppermute x3, starting transfers between devices, body(): lax.ppermute(own, pair, [(i, i ^ flip) for i in range(4)])  9.88 us
    all_to_all x1, waiting for transfers between devices, body(): got = lax.all_to_all(sent, 'zh', 0, 0, tiled=True)  9.54 us
    all_to_all x1, starting transfers between devices, body(): got = lax.all_to_all(sent, 'zh', 0, 0, tiled=True)  6.68 us
    all_to_all x1, starting transfers between devices, body(): low = lax.all_to_all(sum_parts(parts), PEER_ORDER, 0, 0)  6.47 us
    all_to_all x1, waiting for transfers between devices, body(): low = lax.all_to_all(sum_parts(parts), PEER_ORDER, 0, 0)  6.4 us
    pallas_call x1, Pallas kernels, base_products(): pl.pallas_call(base_kernel, out_shape=[jax.ShapeDtypeStruct((ROWS, WIDTH)...  5.01 us
  transfers between devices with their start and end apart: 11, of which 3 were waited for; matrix products, arithmetic and copies ran while one was open for 3% of the time, Pallas kernels for 9%

profile of v11, /device:TPU:1, one launch (start us, length us, event | category | flops | bytes accessed | tf_op | source)
XLA Modules:
  0.0 105.1 jit_solution(123018486550935752)
XLA Ops:
  6.5 0.0 all-gather.2.cloned.1.call-start
  6.6 1.3 %broadcast_in_dim.13 = s32[4,1,2]{2,1,0:T(1,128)} broadcast(s32[2]{0:T(128)} %ids_ref.3), dimensions={2} | broadcast | bytes 40 | tf_op jit(solution)/shard_map/broadcast_in_dim | solution.py:240
  7.9 0.0 all-gather.2.cloned.1.call-update
  7.9 10.9 %all-to-all-start = ((s32[4,1,2]{2,1,0:T(1,128)}), s32[4,1,2]{2,1,0:T(1,128)S(1)}, u32[]{:S(2)}, u32[]{:S(2)}) async-start(s32[4,1,2]{2,1,0:T(1,128)} %broadcast_in_dim.13), calls=%async_computation | async-start | bytes 4096 | tf_op jit(solution)/shard_map/all_to_all | solution.py:243
  18.7 1.0 pad_maximum_fusion.own_ref
  19.7 5.6 %collective-permute-start.2 = (bf16[2,4,64,256]{3,2,1,0:T(8,128)(2,1)S(1)}, bf16[2,4,64,256]{3,2,1,0:T(8,128)(2,1)S(1)}, u32[]{:S(2)}, u32[]{:S(2)}) collective-permute-start(bf16[2,4,64,256]{3,2,1,0:T(8,128)(2,1)S(1)} %pad_maximum_fusion.own_ref), channel_id=1, source_target_pairs={{0,288},{32,256},{256,32},{288,0},{1,289},{33,257},{257,33},{289,1... | collective-permute-start | bytes 786440 | tf_op jit(solution)/shard_map/ppermute | solution.py:246
  25.3 2.2 %collective-permute-start.1 = (bf16[2,4,64,256]{3,2,1,0:T(8,128)(2,1)S(1)}, bf16[2,4,64,256]{3,2,1,0:T(8,128)(2,1)S(1)}, u32[]{:S(2)}, u32[]{:S(2)}) collective-permute-start(bf16[2,4,64,256]{3,2,1,0:T(8,128)(2,1)S(1)} %pad_maximum_fusion.own_ref), channel_id=1, source_target_pairs={{0,32},{32,0},{256,288},{288,256},{1,33},{33,1},{257,289},{289,257... | collective-permute-start | bytes 786440 | tf_op jit(solution)/shard_map/ppermute | solution.py:246
  27.5 2.1 %collective-permute-start = (bf16[2,4,64,256]{3,2,1,0:T(8,128)(2,1)S(1)}, bf16[2,4,64,256]{3,2,1,0:T(8,128)(2,1)S(1)}, u32[]{:S(2)}, u32[]{:S(2)}) collective-permute-start(bf16[2,4,64,256]{3,2,1,0:T(8,128)(2,1)S(1)} %pad_maximum_fusion.own_ref), channel_id=1, source_target_pairs={{0,256},{32,288},{256,0},{288,32},{1,257},{33,289},{257,1},{289,33... | collective-permute-start | bytes 786440 | tf_op jit(solution)/shard_map/ppermute | solution.py:246
  29.6 0.0 all-to-all-done.ids_ref
  29.7 1.7 %constant_dynamic-slice_fusion = (bf16[2048,256]{1,0:T(8,128)(2,1)S(1)}, bf16[2048,256]{1,0:T(8,128)(2,1)S(1)}) fusion(bf16[8192,256]{1,0:T(8,128)(2,1)} %w_ref, s32[]{:T(128)S(6)} %select_n.7, s32[]{:T(128)S(6)} %select_n.6), kind=kLoop, calls=%fused_computation.2 | loop fusion | bytes 4194312 | tf_op jit(solution)/shard_map/dynamic_slice | solution.py:256
  31.4 4.4 %collective-permute-start.4 = (bf16[2048,256]{1,0:T(8,128)(2,1)S(1)}, bf16[2048,256]{1,0:T(8,128)(2,1)}, u32[]{:S(2)}, u32[]{:S(2)}) collective-permute-start(bf16[2048,256]{1,0:T(8,128)(2,1)S(1)} %get-tuple-element.17), channel_id=1, source_target_pairs={{0,272},{16,0},{256,16},{272,256},{1,273},{17,1},{257,17},{273,257... | collective-permute-start | bytes 3145736 | tf_op jit(solution)/shard_map/ppermute | solution.py:255
  35.8 1.9 %collective-permute-start.3 = (bf16[2048,256]{1,0:T(8,128)(2,1)S(1)}, bf16[2048,256]{1,0:T(8,128)(2,1)}, u32[]{:S(2)}, u32[]{:S(2)}) collective-permute-start(bf16[2048,256]{1,0:T(8,128)(2,1)S(1)} %get-tuple-element.18), channel_id=1, source_target_pairs={{0,16},{16,256},{256,272},{272,0},{1,17},{17,257},{257,273},{273,1... | collective-permute-start | bytes 3145736 | tf_op jit(solution)/shard_map/ppermute | solution.py:252
  37.7 0.1 pad_add_fusion.place_ref
  37.8 0.0 collective-permute-done.2.xz_ref
  37.8 0.0 collective-permute-done.1.z_ref
  37.8 0.0 collective-permute-done.x_ref
  37.8 1.6 %shard_map.73 = bf16[4,4,64,256]{3,2,1,0:T(8,128)(2,1)} custom-call(s32[4,1,2]{2,1,0:T(1,128)S(1)} %all-to-all-done.ids_ref, s32[64]{0:T(128)S(1)} %copy-done.2, s32[2]{0:T(128)S(1)} %pad_add_fusion.place_ref, bf16[2,4,64,256]{3,2,1,0:T(8,128)(2,1)S(1)} %pad_maximum_fusion.own_ref, bf16[2,4,64,256]{3,2,1,0:T(8,128)(2,1)S(1)} %collective-permute-done.x_ref, ...), custom_call_target="tpu_custom_call" | custom-call | bytes 2097152 | tf_op jit(solution)/shard_map/pallas_call | solution.py:54
  39.4 6.7 %all-to-all-start.1 = ((bf16[4,4,64,256]{3,2,1,0:T(8,128)(2,1)}), bf16[4,4,64,256]{3,2,1,0:T(8,128)(2,1)S(1)}, u32[]{:S(2)}, u32[]{:S(2)}) async-start(bf16[4,4,64,256]{3,2,1,0:T(8,128)(2,1)} %shard_map.73), calls=%async_computation.1 | async-start | bytes 1048576 | tf_op jit(solution)/shard_map/all_to_all | solution.py:261
  46.1 9.5 %all-to-all-done.1.got_ref = bf16[4,4,64,256]{3,2,1,0:T(8,128)(2,1)S(1)} async-done(((bf16[4,4,64,256]{3,2,1,0:T(8,128)(2,1)}), bf16[4,4,64,256]{3,2,1,0:T(8,128)(2,1)S(1)}, u32[]{:S(2)}, u32[]{:S(2)}) %all-to-all-start.1) | async-done | bytes 524320 | tf_op jit(solution)/shard_map/all_to_all | solution.py:261
  55.6 1.7 %shard_map.74 = f32[256,128]{1,0:T(8,128)} custom-call(s32[2]{0:T(128)S(1)} %copy-done.3, s32[64]{0:T(128)S(1)} %copy-done.2, s32[4]{0:T(128)S(1)} %copy-done.4, s32[1]{0:T(128)} %bitcast.dp_ref, bf16[512,256]{1,0:T(8,128)(2,1)S(1)} %copy-done, bf16[4,4,64,256]{3,2,1,0:T(8,128)(2,1)S(1)} %all-to-all-done.1.got_ref), custom_call_target="tpu_custom_call" | custom-call | flops 16777216 | bytes 1048576 | tf_op jit(solution)/shard_map/pallas_call | solution.py:93
  57.3 15.3 %all-to-all-start.2 = ((f32[32,8,128]{2,1,0:T(8,128)}), f32[32,8,128]{2,1,0:T(8,128)S(1)}, u32[]{:S(2)}, u32[]{:S(2)}) async-start(f32[32,8,128]{2,1,0:T(8,128)} %bitcast.5), calls=%async_computation.2 | async-start | bytes 262144 | tf_op jit(solution)/shard_map/all_to_all | solution.py:264
  72.6 0.0 collective-permute-done.4.wb_ref
  72.7 0.0 all-gather.2.cloned.1.call-done.t_ref
  72.7 5.0 %shard_map.77 = (bf16[512,256]{1,0:T(8,128)(2,1)}, f32[512,256]{1,0:T(8,128)}) custom-call(s32[1]{0:T(128)} %bitcast.7.half_ref, bf16[512,4096]{1,0:T(8,128)(2,1)} %all-gather.2.cloned.1.call-done.t_ref, bf16[2048,256]{1,0:T(8,128)(2,1)} %collective-permute-done.3.wa_ref, bf16[2048,256]{1,0:T(8,128)(2,1)} %collective-permute-done.4.wb_ref, bf16[8192,256]{1,0:T(8,128)(2,1)} %w_ref), custom_call_target="tpu_custom_call" | custom-call | flops 2147483648 | bytes 10485760 | tf_op jit(solution)/shard_map/pallas_call | solution.py:178
  77.7 3.3 %collective-permute-start.5 = (bf16[512,256]{1,0:T(8,128)(2,1)}, bf16[512,256]{1,0:T(8,128)(2,1)S(1)}, u32[]{:S(2)}, u32[]{:S(2)}) collective-permute-start(bf16[512,256]{1,0:T(8,128)(2,1)} %get-tuple-element.16), channel_id=1, source_target_pairs={{0,16},{16,0},{1,17},{17,1},{2,18},{18,2},{3,19},{19,3},{4,20},{20... | collective-permute-start | bytes 786440 | tf_op jit(solution)/shard_map/ppermute | solution.py:269
  81.0 1.0 all-to-all-done.2.parts_ref
  82.0 0.7 shard_map.75
  82.7 6.5 %all-to-all-start.3 = ((bf16[32,8,128]{2,1,0:T(8,128)(2,1)}), bf16[32,8,128]{2,1,0:T(8,128)(2,1)S(1)}, u32[]{:S(2)}, u32[]{:S(2)}) async-start(bf16[32,8,128]{2,1,0:T(8,128)(2,1)} %shard_map.75), calls=%async_computation.3 | async-start | bytes 131072 | tf_op jit(solution)/shard_map/all_to_all | solution.py:265
  89.1 0.7 shard_map.76.ups_ref
  89.9 1.0 copy-done.1
  91.0 6.4 %all-to-all-done.3 = bf16[32,8,128]{2,1,0:T(8,128)(2,1)S(1)} async-done(((bf16[32,8,128]{2,1,0:T(8,128)(2,1)}), bf16[32,8,128]{2,1,0:T(8,128)(2,1)S(1)}, u32[]{:S(2)}, u32[]{:S(2)}) %all-to-all-start.3) | async-done | bytes 65568 | tf_op jit(solution)/shard_map/all_to_all | solution.py:265
  97.4 0.9 shard_map.79
  (12 shorter events, 0.1 us)
Async XLA Ops:
  6.5 49.1 %copy-start = (bf16[512,256]{1,0:T(8,128)(2,1)S(1)}, bf16[512,256]{1,0:T(8,128)(2,1)}, u32[]{:S(2)}) copy-start(bf16[512,256]{1,0:T(8,128)(2,1)} %tokens_ref.1) | copy-start | bytes 786436
  6.5 49.1 %copy-start.3 = (s32[2]{0:T(128)S(1)}, s32[2]{0:T(128)}, u32[]{:S(2)}) copy-start(s32[2]{0:T(128)} %ids_ref.3) | copy-start | bytes 28
  6.5 31.2 %copy-start.2 = (s32[64]{0:T(128)S(1)}, s32[64]{0:T(128)}, u32[]{:S(2)}) copy-start(s32[64]{0:T(128)} %stored_ref.5) | copy-start | bytes 772
  6.5 49.1 %copy-start.4 = (s32[4]{0:T(128)S(1)}, s32[4]{0:T(128)}, u32[]{:S(2)}) copy-start(s32[4]{0:T(128)} %seg_ref.3) | copy-start | bytes 52
  6.5 66.1 %all-gather.2.cloned.1.call-start = ((), (), s32[]{:S(2)}) async-start(), calls=%async_computation.4 | async-start | bytes 4456448 | tf_op jit(solution)/shard_map/all_gather | solution.py:242
  7.9 21.8 %all-to-all-start = ((s32[4,1,2]{2,1,0:T(1,128)}), s32[4,1,2]{2,1,0:T(1,128)S(1)}, u32[]{:S(2)}, u32[]{:S(2)}) async-start(s32[4,1,2]{2,1,0:T(1,128)} %broadcast_in_dim.13), calls=%async_computation | async-start | bytes 4096 | tf_op jit(solution)/shard_map/all_to_all | solution.py:243
  19.7 18.0 %collective-permute-start.2 = (bf16[2,4,64,256]{3,2,1,0:T(8,128)(2,1)S(1)}, bf16[2,4,64,256]{3,2,1,0:T(8,128)(2,1)S(1)}, u32[]{:S(2)}, u32[]{:S(2)}) collective-permute-start(bf16[2,4,64,256]{3,2,1,0:T(8,128)(2,1)S(1)} %pad_maximum_fusion.own_ref), channel_id=1, source_target_pairs={{0,288},{32,256},{256,32},{288,0},{1,289},{33,257},{257,33},{289,1... | collective-permute-start | bytes 786440 | tf_op jit(solution)/shard_map/ppermute | solution.py:246
  25.3 12.5 %collective-permute-start.1 = (bf16[2,4,64,256]{3,2,1,0:T(8,128)(2,1)S(1)}, bf16[2,4,64,256]{3,2,1,0:T(8,128)(2,1)S(1)}, u32[]{:S(2)}, u32[]{:S(2)}) collective-permute-start(bf16[2,4,64,256]{3,2,1,0:T(8,128)(2,1)S(1)} %pad_maximum_fusion.own_ref), channel_id=1, source_target_pairs={{0,32},{32,0},{256,288},{288,256},{1,33},{33,1},{257,289},{289,257... | collective-permute-start | bytes 786440 | tf_op jit(solution)/shard_map/ppermute | solution.py:246
  27.5 10.3 %collective-permute-start = (bf16[2,4,64,256]{3,2,1,0:T(8,128)(2,1)S(1)}, bf16[2,4,64,256]{3,2,1,0:T(8,128)(2,1)S(1)}, u32[]{:S(2)}, u32[]{:S(2)}) collective-permute-start(bf16[2,4,64,256]{3,2,1,0:T(8,128)(2,1)S(1)} %pad_maximum_fusion.own_ref), channel_id=1, source_target_pairs={{0,256},{32,288},{256,0},{288,32},{1,257},{33,289},{257,1},{289,33... | collective-permute-start | bytes 786440 | tf_op jit(solution)/shard_map/ppermute | solution.py:246
  31.4 41.3 %collective-permute-start.4 = (bf16[2048,256]{1,0:T(8,128)(2,1)S(1)}, bf16[2048,256]{1,0:T(8,128)(2,1)}, u32[]{:S(2)}, u32[]{:S(2)}) collective-permute-start(bf16[2048,256]{1,0:T(8,128)(2,1)S(1)} %get-tuple-element.17), channel_id=1, source_target_pairs={{0,272},{16,0},{256,16},{272,256},{1,273},{17,1},{257,17},{273,257... | collective-permute-start | bytes 3145736 | tf_op jit(solution)/shard_map/ppermute | solution.py:255
  35.8 36.9 %collective-permute-start.3 = (bf16[2048,256]{1,0:T(8,128)(2,1)S(1)}, bf16[2048,256]{1,0:T(8,128)(2,1)}, u32[]{:S(2)}, u32[]{:S(2)}) collective-permute-start(bf16[2048,256]{1,0:T(8,128)(2,1)S(1)} %get-tuple-element.18), channel_id=1, source_target_pairs={{0,16},{16,256},{256,272},{272,0},{1,17},{17,257},{257,273},{273,1... | collective-permute-start | bytes 3145736 | tf_op jit(solution)/shard_map/ppermute | solution.py:252
  39.4 16.2 %all-to-all-start.1 = ((bf16[4,4,64,256]{3,2,1,0:T(8,128)(2,1)}), bf16[4,4,64,256]{3,2,1,0:T(8,128)(2,1)S(1)}, u32[]{:S(2)}, u32[]{:S(2)}) async-start(bf16[4,4,64,256]{3,2,1,0:T(8,128)(2,1)} %shard_map.73), calls=%async_computation.1 | async-start | bytes 1048576 | tf_op jit(solution)/shard_map/all_to_all | solution.py:261
  57.3 24.7 %all-to-all-start.2 = ((f32[32,8,128]{2,1,0:T(8,128)}), f32[32,8,128]{2,1,0:T(8,128)S(1)}, u32[]{:S(2)}, u32[]{:S(2)}) async-start(f32[32,8,128]{2,1,0:T(8,128)} %bitcast.5), calls=%async_computation.2 | async-start | bytes 262144 | tf_op jit(solution)/shard_map/all_to_all | solution.py:264
  77.7 12.2 %collective-permute-start.5 = (bf16[512,256]{1,0:T(8,128)(2,1)}, bf16[512,256]{1,0:T(8,128)(2,1)S(1)}, u32[]{:S(2)}, u32[]{:S(2)}) collective-permute-start(bf16[512,256]{1,0:T(8,128)(2,1)} %get-tuple-element.16), channel_id=1, source_target_pairs={{0,16},{16,0},{1,17},{17,1},{2,18},{18,2},{3,19},{19,3},{4,20},{20... | collective-permute-start | bytes 786440 | tf_op jit(solution)/shard_map/ppermute | solution.py:269
  82.7 14.7 %all-to-all-start.3 = ((bf16[32,8,128]{2,1,0:T(8,128)(2,1)}), bf16[32,8,128]{2,1,0:T(8,128)(2,1)S(1)}, u32[]{:S(2)}, u32[]{:S(2)}) async-start(bf16[32,8,128]{2,1,0:T(8,128)(2,1)} %shard_map.75), calls=%async_computation.3 | async-start | bytes 131072 | tf_op jit(solution)/shard_map/all_to_all | solution.py:265
  89.9 1.0 copy-start.1
Sparse Core Ops, SparseCore 0:
  9.4 58.3 all-gather.1
